TPU v7x, 512 devices: a whole 4x8x8 slice. The times are simulated.
512 devices in a mesh: expert: 64 (over x, z, core), group: 8 (over y).
Axes of the slice: x: 4, y: 8, z: 8, core: 2. Of those that a mesh axis runs over, the one named last changes fastest.
Arguments:
- tokens: bfloat16 [32768, 2048], P(('expert', 'group')), may hold values from -6 to 6
- expert_ids: int32 [32768, 2], P(('expert', 'group')), may hold values from 0 to 63, all different within a row; in each aligned block of 64 rows (0 to 63, 64 to 127, ...) at most 2 rows name the same one
- gates: float32 [32768, 2], P(('expert', 'group')), may hold values from 0.2 to 1
- ln_gain: float32 [2048], replicated, may hold values from 0.25 to 2.5
- w_in: bfloat16 [64, 2048, 4096], P('expert', None, 'group'), may hold values from -0.125 to 0.125
- b_in: float32 [64, 4096], P('expert', 'group'), may hold values from -3 to 3
- w_out: bfloat16 [64, 4096, 2048], P('expert', 'group'), may hold values from -0.125 to 0.125
- b_out: float32 [64, 2048], P('expert'), may hold values from -3 to 3
- final_gain: float32 [2048], replicated, may hold values from 0.1 to 1.9
- w_cross: bfloat16 [2048, 2048], P('expert', 'group'), may hold values from -0.125 to 0.125
- lengths: int32 [512, 4], replicated, may hold values from 1 to 32, 64 in all within a row
- page_table: int32 [512, 4], replicated, may hold values from 0 to 63, as said below
- queries: bfloat16 [2048, 1024], P('expert', 'group'), may hold values from -25 to 25
Outputs:
- encoded: bfloat16 [32768, 2048], P(('expert', 'group'))
- context: bfloat16 [2048, 1024], P('expert', 'group')
Inputs may be any that keep to these rules, and one draw needn't show every extreme that they name: `expert_ids`: in the 64 rows of one device every expert is named exactly 2 times; a row names two different experts. `lengths`: every row sums to 64. For each group index g and sentence number k there is a shift s with page_table[c * 8 + g, k] = (c + s) mod 64 for every c; the shifts of the 32 pairs (g, k) are distinct.
All inputs are finite; a program needn't handle non-finite values.
Results may differ from a plain program's by a relative error of at most 0.04.
Values may be sent and summed in bfloat16 or wider, within the bound.
No kernel may reach another device: no remote copies, remote signals or barrier semaphores. Data moves between devices by JAX's collectives and lax.ppermute only.
A program may use at most 64 MiB of HBM per device.

v0:
```python
import math

import jax
import jax.numpy as jnp
from jax import lax
from jax.sharding import PartitionSpec as P

EPSILON = 1e-05


def layer_norm(values, gain_row):
    average = jnp.mean(values, axis=-1, keepdims=True)
    centred = values - average
    variance = jnp.mean(centred * centred, axis=-1, keepdims=True)
    return centred * lax.rsqrt(variance + EPSILON) * gain_row


def slot_numbers(id_rows):
    flat_ids = id_rows.reshape(-1)
    count = flat_ids.shape[0]
    same_expert = (flat_ids[:, None] == flat_ids[None, :]).astype(jnp.int32)
    position = jnp.arange(count, dtype=jnp.int32)
    earlier = (position[None, :] < position[:, None]).astype(jnp.int32)
    return jnp.sum(same_expert * earlier, axis=1)


def build_dispatch(block_rows, id_rows, experts, capacity):
    slot_rank = slot_numbers(id_rows)
    target = id_rows.reshape(-1) * capacity + slot_rank
    places = jnp.arange(experts * capacity, dtype=jnp.int32)
    selector = (places[:, None] == target[None, :]).astype(jnp.bfloat16)
    repeated = jnp.repeat(block_rows, 2, axis=0)
    outgoing = jnp.dot(selector, repeated, preferred_element_type=jnp.float32).astype(jnp.bfloat16)
    return outgoing.reshape(experts, capacity, block_rows.shape[1])


def attend(query_rows, sentence_rows, sentence_lengths):
    head_size = query_rows.shape[1]
    key_part = sentence_rows[:, :, :head_size]
    value_part = sentence_rows[:, :, head_size:]
    scores = jnp.einsum(
        "js,jrs->jr", query_rows, key_part, preferred_element_type=jnp.float32
    ) / math.sqrt(head_size)
    offsets = jnp.arange(sentence_rows.shape[1], dtype=jnp.int32)
    visible = offsets[None, :] < sentence_lengths[:, None]
    scores = jnp.where(visible, scores, -jnp.inf)
    highest = jnp.max(scores, axis=-1, keepdims=True)
    exponent = jnp.exp(scores - highest)
    attention = (exponent / jnp.sum(exponent, axis=-1, keepdims=True)).astype(jnp.bfloat16)
    return jnp.einsum(
        "jr,jrs->js", attention, value_part, preferred_element_type=jnp.float32
    ).astype(jnp.bfloat16)


def on_device(
    tokens,
    expert_ids,
    gates,
    ln_gain,
    w_in,
    b_in,
    w_out,
    b_out,
    final_gain,
    w_cross,
    lengths,
    page_table,
    queries,
):
    rows_dev = tokens.shape[0]
    model_width = tokens.shape[1]
    experts = lax.axis_size("expert")
    groups = lax.axis_size("group")
    capacity = max(2, 2 * rows_dev // experts)
    first = w_in[0]
    first_bias = b_in[0]
    second = w_out[0]
    normed = layer_norm(tokens.astype(jnp.float32), ln_gain).astype(jnp.bfloat16)
    column_normed, column_ids = (
        lax.all_gather(normed, "group", axis=0, tiled=True),
        lax.all_gather(expert_ids, "group", axis=0, tiled=True),
    )
    outgoing = jax.vmap(
        lambda block_rows, id_rows: build_dispatch(block_rows, id_rows, experts, capacity)
    )(column_normed.reshape(groups, rows_dev, model_width), column_ids.reshape(groups, rows_dev, 2))
    arrived = lax.all_to_all(outgoing, "expert", split_axis=1, concat_axis=1, tiled=True)
    shard_rows = arrived.reshape(groups * experts, capacity, model_width)
    flat_rows = shard_rows.reshape(-1, model_width)
    hidden = jax.nn.relu(jnp.dot(flat_rows, first, preferred_element_type=jnp.float32) + first_bias)
    hidden_all = hidden.astype(jnp.bfloat16).reshape(shard_rows.shape[0], shard_rows.shape[1], -1)
    flat_hidden = hidden_all.reshape(-1, hidden_all.shape[-1])
    block_rows = flat_hidden
    summed = lax.psum_scatter(
        jnp.dot(block_rows, second, preferred_element_type=jnp.float32).astype(jnp.bfloat16),
        "group",
        scatter_dimension=0,
        tiled=True,
    ).astype(jnp.float32)
    expert_out = (summed + b_out[0]).astype(jnp.bfloat16).reshape(experts, capacity, model_width)
    returned = lax.all_to_all(expert_out, "expert", split_axis=0, concat_axis=0, tiled=True)
    slot_rank = slot_numbers(expert_ids)
    target = expert_ids.reshape(-1) * capacity + slot_rank
    picked = returned.reshape(experts * capacity, model_width)[target].reshape(
        rows_dev, 2, model_width
    )
    moe = jnp.sum(gates[:, :, None] * picked.astype(jnp.float32), axis=1)
    encoded = layer_norm(tokens.astype(jnp.float32) + moe, final_gain).astype(jnp.bfloat16)
    column = lax.all_gather(encoded, "group", axis=0, tiled=True)
    keyvals = jnp.dot(
        column,
        lax.all_gather(w_cross, "expert", axis=0, tiled=True),
        preferred_element_type=jnp.float32,
    ).astype(jnp.bfloat16)
    sentences = lengths.shape[1]
    max_len = rows_dev // 2
    my_column = lax.axis_index("expert")
    column_lengths = lax.dynamic_slice_in_dim(lengths, my_column * groups, groups, 0)
    column_owners = lax.dynamic_slice_in_dim(page_table, my_column * groups, groups, 0).reshape(-1)
    group_base = jnp.arange(groups, dtype=jnp.int32)[:, None] * rows_dev
    starts = (group_base + jnp.cumsum(column_lengths, axis=1) - column_lengths).reshape(-1)
    offsets = jnp.arange(max_len, dtype=jnp.int32)
    row_index = jnp.minimum(starts[:, None] + offsets[None, :], column.shape[0] - 1)
    sentence_rows = keyvals[row_index]
    table_grid = page_table.reshape(experts, groups, sentences)
    owned = (table_grid == my_column).astype(jnp.int32)
    column_ids = jnp.arange(experts, dtype=jnp.int32)
    source_column = jnp.sum(owned * column_ids[:, None, None], axis=0).reshape(-1)
    owned_lengths = jnp.sum(owned * lengths.reshape(experts, groups, sentences), axis=0).reshape(-1)
    to_owner = (column_owners[None, :] == column_ids[:, None]).astype(jnp.bfloat16)
    outgoing_pages = jnp.einsum(
        "pj,jrc->prc", to_owner, sentence_rows, preferred_element_type=jnp.float32
    ).astype(jnp.bfloat16)
    arrived_pages = lax.all_to_all(
        outgoing_pages, "expert", split_axis=0, concat_axis=0, tiled=True
    )
    context = attend(queries, arrived_pages[source_column], owned_lengths)
    return (encoded, context)


def solution(mesh):
    return jax.shard_map(
        on_device,
        mesh=mesh,
        in_specs=(
            P(("expert", "group"), None),
            P(("expert", "group"), None),
            P(("expert", "group"), None),
            P(),
            P("expert", None, "group"),
            P("expert", "group"),
            P("expert", "group", None),
            P("expert", None),
            P(),
            P("expert", "group"),
            P(),
            P(),
            P("expert", "group"),
        ),
        out_specs=(P(("expert", "group"), None), P("expert", "group")),
        check_vma=False,
    )
```

profile of v0, /device:TPU:1, one launch (start us, length us, event | category | flops | bytes accessed | tf_op | source)
XLA Modules:
  0.0 479.7 jit_solution(17000100980690876003)
XLA Ops:
  8.1 1.2 convert_reduce_fusion
  9.3 1.2 fusion.9
  10.5 1.8 fusion.11
  12.4 14.1 %all-gather = s32[8,64,2]{1,2,0:T(2,128)S(1)} all-gather(s32[1,64,2]{1,2,0:T(2,128)} %bitcast.51), channel_id=1, replica_groups=mesh['expert'=64,'group'=8] {'group'}, dimensions={0}, use_global_device_ids=true | all-gather | bytes 4608 | tf_op jit(solution)/shard_map/all_gather | solution.py:81
  26.5 0.1 copy.62
  26.7 0.4 select_reduce_fusion
  27.1 30.8 %all-gather.5.cloned.1.call-done = bf16[512,2048]{1,0:T(8,128)(2,1)} async-done(((bf16[64,2048]{1,0:T(8,128)(2,1)}), bf16[512,2048]{1,0:T(8,128)(2,1)}) %all-gather.5.cloned.1.call-update) | async-done | bytes 2097168 | tf_op jit(solution)/shard_map/all_gather | solution.py:80
  57.9 5.4 %broadcast_in_dim.5 = bf16[8,64,2,2048]{3,2,1,0:T(2,128)(2,1)} broadcast(bf16[8,64,2048]{2,1,0:T(8,128)(2,1)} %bitcast.44), dimensions={0,1,3} | broadcast | bytes 6291456 | tf_op jit(solution)/shard_map/vmap()/broadcast_in_dim | solution.py:32
  63.3 7.2 %reshape.196 = bf16[8,128,2048]{2,1,0:T(8,128)(2,1)} reshape(bf16[8,64,2,2048]{3,2,1,0:T(2,128)(2,1)} %broadcast_in_dim.5) | data formatting | bytes 8388608 | tf_op jit(solution)/shard_map/vmap()/reshape | solution.py:32
  70.5 5.4 %convolution_convert_fusion.1 = bf16[8,128,2048]{2,1,0:T(8,128)(2,1)} fusion(bf16[8,128,2048]{2,1,0:T(8,128)(2,1)} %reshape.196, s32[8,128]{1,0:T(8,128)S(1)} %multiply_add_fusion), kind=kOutput, calls=%fused_computation.4 | convolution fusion | flops 539099136 | bytes 8392704 | tf_op jit(solution)/shard_map/vmap()/dot_general | solution.py:33
  75.9 7.6 %reshape.197 = bf16[8,64,2,2048]{3,2,1,0:T(2,128)(2,1)} reshape(bf16[8,128,2048]{2,1,0:T(8,128)(2,1)} %convolution_convert_fusion.1) | data formatting | bytes 8388608 | tf_op jit(solution)/shard_map/vmap()/reshape | solution.py:34
  83.5 7.1 %copy.66 = bf16[8,64,2,2048]{3,2,0,1:T(2,128)(2,1)S(1)} copy(bf16[8,64,2,2048]{3,2,1,0:T(2,128)(2,1)} %reshape.197) | data formatting | bytes 8388608 | tf_op jit(solution)/shard_map/vmap()/reshape | solution.py:34
  90.6 110.7 %all_to_all.15 = bf16[8,64,2,2048]{3,2,0,1:T(2,128)(2,1)} all-to-all(bf16[8,64,2,2048]{3,2,0,1:T(2,128)(2,1)S(1)} %copy.66), channel_id=1, replica_groups=mesh['expert'=64,'group'=8] {'expert'}, dimensions={1} | all-to-all | bytes 8388608 | tf_op jit(solution)/shard_map/all_to_all | solution.py:86
  201.4 7.6 %copy.67 = bf16[8,64,2,2048]{3,2,1,0:T(2,128)(2,1)} copy(bf16[8,64,2,2048]{3,2,0,1:T(2,128)(2,1)} %all_to_all.15) | data formatting | bytes 8388608 | tf_op jit(solution)/shard_map/all_to_all | solution.py:86
  209.0 7.2 %reshape_reshape.9 = bf16[1024,2048]{1,0:T(8,128)(2,1)} reshape(bf16[8,64,2,2048]{3,2,1,0:T(2,128)(2,1)} %copy.67) | data formatting | bytes 8388608 | tf_op jit(solution)/shard_map/reshape;reshape | solution.py:88
  216.2 9.3 %convolution_convert_fusion = bf16[1024,2048]{1,0:T(8,128)(2,1)} fusion(bf16[1,512,2048]{2,1,0:T(8,128)(2,1)S(1)} %copy-done, bf16[1024,2048]{1,0:T(8,128)(2,1)} %reshape_reshape.9, bf16[1,2048,512]{2,1,0:T(8,128)(2,1)} %param.17, f32[512]{0:T(512)S(1)} %bitcast.54), kind=kOutput, calls=%fused_computation.3 | convolution fusion | flops 4298637312 | bytes 12584960 | tf_op jit(solution)/shard_map/dot_general | solution.py:94
  225.5 51.8 %reduce-scatter.2.cloned.1.call-done = bf16[128,2048]{1,0:T(8,128)(2,1)} async-done(((bf16[1024,2048]{1,0:T(8,128)(2,1)}), bf16[128,2048]{1,0:T(8,128)(2,1)}) %reduce-scatter.2.cloned.1.call-update) | async-done | bytes 524304 | tf_op jit(solution)/shard_map/reduce_scatter | solution.py:93
  277.3 1.1 add_convert_fusion
  278.5 1.1 reshape.198
  279.6 11.0 %all-to-all-start.1 = ((bf16[64,2,2048]{2,1,0:T(2,128)(2,1)}), bf16[64,2,2048]{2,1,0:T(2,128)(2,1)S(1)}, u32[]{:S(2)}, u32[]{:S(2)}) async-start(bf16[64,2,2048]{2,1,0:T(2,128)(2,1)} %reshape.198), calls=%async_computation.2 | async-start | bytes 1048576 | tf_op jit(solution)/shard_map/all_to_all | solution.py:100
  290.6 0.5 all-gather.9.cloned.1.call-update
  291.1 0.3 all-gather.7.cloned.1.call-start
  291.4 0.1 copy.69
  291.5 0.1 copy.68
  291.6 0.1 mul.118
  291.8 0.1 eq.71
  291.9 0.1 copy.61
  292.0 0.2 select_reduce_fusion.3
  292.2 15.7 %all-to-all-done.1 = bf16[64,2,2048]{2,1,0:T(2,128)(2,1)S(1)} async-done(((bf16[64,2,2048]{2,1,0:T(2,128)(2,1)}), bf16[64,2,2048]{2,1,0:T(2,128)(2,1)S(1)}, u32[]{:S(2)}, u32[]{:S(2)}) %all-to-all-start.1) | async-done | bytes 524320 | tf_op jit(solution)/shard_map/all_to_all | solution.py:100
  307.9 0.2 reshape.199
  308.1 0.9 gather_fusion
  309.1 1.6 reshape.202
  310.7 2.8 multiply_reduce_fusion
  313.5 0.2 fusion.18
  313.7 0.2 multiply_reduce_fusion.1
  314.0 0.9 multiply_convert_fusion
  314.9 0.1 constant_dynamic-slice_fusion
  315.0 0.1 copy.72
  315.1 0.1 add.145
  315.2 0.1 compare_select_fusion
  315.2 0.1 reshape.213
  315.3 0.1 copy.71
  315.4 0.1 eq.78
  315.5 60.4 %all-gather.9.cloned.1.call-done = bf16[2048,256]{1,0:T(8,128)(2,1)} async-done(((bf16[32,256]{1,0:T(8,128)(2,1)}), bf16[2048,256]{1,0:T(8,128)(2,1)}) %all-gather.9.cloned.1.call-update) | async-done | bytes 1048592 | tf_op jit(solution)/shard_map/all_gather | solution.py:111
  375.9 39.0 %all-gather.7.cloned.1.call-done = bf16[512,2048]{1,0:T(8,128)(2,1)} async-done(((bf16[64,2048]{1,0:T(8,128)(2,1)}), bf16[512,2048]{1,0:T(8,128)(2,1)}) %all-gather.7.cloned.1.call-update) | async-done | bytes 2097168 | tf_op jit(solution)/shard_map/all_gather | solution.py:108
  414.9 2.6 convolution_convert_fusion.3
  417.5 3.9 gather_fusion.1
  421.5 0.6 convolution_convert_fusion.2
  422.0 1.6 copy.74
  423.6 15.3 %all-to-all-start.2 = ((bf16[64,32,256]{2,1,0:T(8,128)(2,1)}), bf16[64,32,256]{2,1,0:T(8,128)(2,1)S(1)}, u32[]{:S(2)}, u32[]{:S(2)}) async-start(bf16[64,32,256]{2,1,0:T(8,128)(2,1)} %copy.74), calls=%async_computation.3 | async-start | bytes 2097152 | tf_op jit(solution)/shard_map/all_to_all | solution.py:133
  438.9 0.1 reshape.200
  439.0 0.1 eq.77
  439.2 0.1 copy.75
  439.3 0.1 reshape.201
  439.4 0.1 copy.70
  439.4 0.1 lt.96
  439.6 27.9 %all-to-all-done.2 = bf16[64,32,256]{2,1,0:T(8,128)(2,1)S(1)} async-done(((bf16[64,32,256]{2,1,0:T(8,128)(2,1)}), bf16[64,32,256]{2,1,0:T(8,128)(2,1)S(1)}, u32[]{:S(2)}, u32[]{:S(2)}) %all-to-all-start.2) | async-done | bytes 1048608 | tf_op jit(solution)/shard_map/all_to_all | solution.py:133
  467.4 1.4 gather_fusion.2
  468.8 1.2 fusion.15
  470.0 0.2 fusion.25
  470.2 0.2 fusion.24
  470.4 0.1 fusion.27
  470.5 1.1 fusion.13
  471.6 0.6 convert_element_type.73
  (44 shorter events, 0.5 us)
Async XLA Ops:
  8.0 208.2 %copy-start = (bf16[1,512,2048]{2,1,0:T(8,128)(2,1)S(1)}, bf16[1,512,2048]{2,1,0:T(8,128)(2,1)}, u32[]{:S(2)}) copy-start(bf16[1,512,2048]{2,1,0:T(8,128)(2,1)} %param.19) | copy-start | bytes 6291460
  8.0 49.9 %all-gather.5.cloned.1.call-start = ((), (), s32[]{:S(2)}) async-start(), calls=%async_computation.4 | async-start | bytes 2359296 | tf_op jit(solution)/shard_map/all_gather | solution.py:80
  12.3 265.0 %reduce-scatter.2.cloned.1.call-start = ((), (), s32[]{:S(2)}) async-start(), calls=%async_computation.5 | async-start | bytes 4718592 | tf_op jit(solution)/shard_map/reduce_scatter | solution.py:93
  209.0 7.2 %copy-start.9 = (f32[1,512]{1,0:T(1,128)S(1)}, f32[1,512]{1,0:T(1,128)}, u32[]{:S(2)}) copy-start(f32[1,512]{1,0:T(1,128)} %param.18) | copy-start | bytes 6148
  225.5 51.9 %copy-start.5 = (f32[1,2048]{1,0:T(1,128)S(1)}, f32[1,2048]{1,0:T(1,128)}, u32[]{:S(2)}) copy-start(f32[1,2048]{1,0:T(1,128)} %param.20) | copy-start | bytes 24580
  225.5 66.0 %copy-start.4 = (s32[64,2]{0,1:T(2,128)S(1)}, s32[64,2]{0,1:T(2,128)}, u32[]{:S(2)}) copy-start(s32[64,2]{0,1:T(2,128)} %param.14) | copy-start | bytes 1540
  225.5 66.4 %copy-start.7 = (f32[64,2]{0,1:T(2,128)S(1)}, f32[64,2]{0,1:T(2,128)}, u32[]{:S(2)}) copy-start(f32[64,2]{0,1:T(2,128)} %param.15) | copy-start | bytes 1540
  279.6 28.3 %all-to-all-start.1 = ((bf16[64,2,2048]{2,1,0:T(2,128)(2,1)}), bf16[64,2,2048]{2,1,0:T(2,128)(2,1)S(1)}, u32[]{:S(2)}, u32[]{:S(2)}) async-start(bf16[64,2,2048]{2,1,0:T(2,128)(2,1)} %reshape.198), calls=%async_computation.2 | async-start | bytes 1048576 | tf_op jit(solution)/shard_map/all_to_all | solution.py:100
  290.6 85.3 %all-gather.9.cloned.1.call-start = ((), (), s32[]{:S(2)}) async-start(), calls=%async_computation.7 | async-start | bytes 1064960 | tf_op jit(solution)/shard_map/all_gather | solution.py:111
  291.1 123.8 %all-gather.7.cloned.1.call-start = ((), (), s32[]{:S(2)}) async-start(), calls=%async_computation.6 | async-start | bytes 2359296 | tf_op jit(solution)/shard_map/all_gather | solution.py:108
  308.1 5.4 %copy-start.1 = (bf16[64,2048]{1,0:T(8,128)(2,1)S(1)}, bf16[64,2048]{1,0:T(8,128)(2,1)}, u32[]{:S(2)}) copy-start(bf16[64,2048]{1,0:T(8,128)(2,1)} %param.13) | copy-start | bytes 786436
  308.1 5.8 %copy-start.6 = (f32[2048]{0:T(1024)S(1)}, f32[2048]{0:T(1024)}, u32[]{:S(2)}) copy-start(f32[2048]{0:T(1024)} %param.21) | copy-start | bytes 24580
  309.1 5.8 %copy-start.2 = (s32[512,4]{0,1:T(4,128)S(1)}, s32[512,4]{0,1:T(4,128)}, u32[]{:S(2)}) copy-start(s32[512,4]{0,1:T(4,128)} %param.23) | copy-start | bytes 24580
  309.1 5.8 %copy-start.3 = (s32[512,4]{0,1:T(4,128)S(1)}, s32[512,4]{0,1:T(4,128)}, u32[]{:S(2)}) copy-start(s32[512,4]{0,1:T(4,128)} %param.24) | copy-start | bytes 24580
  421.4 47.4 %copy-start.8 = (bf16[32,128]{1,0:T(8,128)(2,1)S(1)}, bf16[32,128]{1,0:T(8,128)(2,1)}, u32[]{:S(2)}) copy-start(bf16[32,128]{1,0:T(8,128)(2,1)} %param.25) | copy-start | bytes 24580
  423.6 43.8 %all-to-all-start.2 = ((bf16[64,32,256]{2,1,0:T(8,128)(2,1)}), bf16[64,32,256]{2,1,0:T(8,128)(2,1)S(1)}, u32[]{:S(2)}, u32[]{:S(2)}) async-start(bf16[64,32,256]{2,1,0:T(8,128)(2,1)} %copy.74), calls=%async_computation.3 | async-start | bytes 2097152 | tf_op jit(solution)/shard_map/all_to_all | solution.py:133
Sparse Core Ops, SparseCore 0:
  12.5 45.3 all-gather.4
  225.6 51.6 reduce-scatter.1
Sparse Core Ops, SparseCore 1:
  294.4 81.4 all-gather.8
  378.4 36.5 all-gather.6
where the time goes:
time: 481 us; the launch traced here: 480 us
  waiting for transfers between devices  226 us (47%)
  blocking collectives  125 us (26%)
  local copies, waits for them, and re-layouts  54.8 us (11%)
  starting transfers between devices  26.6 us (6%)
  matrix products  20.1 us (4%)
  between operations  15.8 us (3%)
  other arithmetic  11.3 us (2%)
    all_to_all x1, blocking collectives, on_device(): lax.all_to_all(outgoing, 'expert', split_axis=1, concat_axis=1, tiled=True)  111 us
    all_gather x1, waiting for transfers between devices, on_device(): lax.all_gather(w_cross, 'expert', axis=0, tiled=True)  60.4 us
    reduce_scatter x1, waiting for transfers between devices, on_device(): lax.psum_scatter(jnp.dot(block_rows, second, preferred_element_type=jnp.f...  51.8 us
    all_gather x1, waiting for transfers between devices, on_device(): column = lax.all_gather(encoded, 'group', axis=0, tiled=True)  39 us
    all_gather x1, waiting for transfers between devices, on_device(): lax.all_gather(normed, 'group', axis=0, tiled=True)  30.8 us
    all_to_all x1, waiting for transfers between devices, on_device(): lax.all_to_all(outgoing_pages, 'expert', split_axis=0, concat_axis=0, til...  27.9 us
    all_to_all x1, waiting for transfers between devices, on_device(): lax.all_to_all(expert_out, 'expert', split_axis=0, concat_axis=0, tiled=T...  15.7 us
    all_to_all x1, starting transfers between devices, on_device(): lax.all_to_all(outgoing_pages, 'expert', split_axis=0, concat_axis=0, til...  15.3 us
  transfers between devices with their start and end apart: 6, of which 6 were waited for; matrix products, arithmetic and copies ran while one was open for 2% of the time, Pallas kernels for 0%

commit v1 on v0

v1 whole, which is shorter than its diff:
```python
import math

import jax
import jax.numpy as jnp
from jax import lax
from jax.sharding import PartitionSpec as P

EPSILON = 1e-05
BF = jnp.bfloat16
F32 = jnp.float32


def layer_norm(values, gain_row):
    average = jnp.mean(values, axis=-1, keepdims=True)
    centred = values - average
    variance = jnp.mean(centred * centred, axis=-1, keepdims=True)
    return centred * lax.rsqrt(variance + EPSILON) * gain_row


def slot_numbers(id_rows):
    flat_ids = id_rows.reshape(-1)
    count = flat_ids.shape[0]
    same_expert = (flat_ids[:, None] == flat_ids[None, :]).astype(jnp.int32)
    position = jnp.arange(count, dtype=jnp.int32)
    earlier = (position[None, :] < position[:, None]).astype(jnp.int32)
    return jnp.sum(same_expert * earlier, axis=1)


def dot(a, b):
    return jnp.dot(a, b, preferred_element_type=F32)


def shift(value, by, groups):
    return lax.ppermute(value, "group", [(i, (i + by) % groups) for i in range(groups)])


def ring_gather(chunks, groups):
    half = groups // 2
    blocks = {0: list(chunks)}
    forward, backward = list(chunks), list(chunks)
    for step in range(1, half):
        for c in range(2):
            forward[c] = shift(forward[c], 1, groups)
            backward[c] = shift(backward[c], -1, groups)
        blocks[-step] = list(forward)
        blocks[step] = list(backward)
    blocks[half] = [shift(forward[0], 1, groups), shift(backward[1], -1, groups)]
    return blocks


def ring_scatter(partial, groups):
    half = groups // 2
    totals = []
    lengths = [(half - 1, half), (half, half - 1)]
    running = [[None, None], [None, None]]
    for step in range(half):
        for c in range(2):
            for way, sign in ((0, 1), (1, -1)):
                hops = lengths[c][way]
                if step >= hops:
                    continue
                offset = sign * (hops - step)
                if offset == -half:
                    offset = half
                value = partial(offset, c)
                if running[c][way] is not None:
                    value = value + running[c][way].astype(F32)
                running[c][way] = shift(value.astype(BF), sign, groups)
    for c in range(2):
        totals.append(
            partial(0, c) + running[c][0].astype(F32) + running[c][1].astype(F32)
        )
    return totals


def on_device(
    tokens,
    expert_ids,
    gates,
    ln_gain,
    w_in,
    b_in,
    w_out,
    b_out,
    final_gain,
    w_cross,
    lengths,
    page_table,
    queries,
):
    rows_dev, width = tokens.shape
    experts = lax.axis_size("expert")
    groups = lax.axis_size("group")
    capacity = 2 * rows_dev // experts
    places = experts * capacity
    sentences = lengths.shape[1]
    head_size = queries.shape[1]
    column = lax.axis_index("expert")
    row = lax.axis_index("group")
    first, second = w_in[0], w_out[0]
    half_width = width // 2

    cross_cols = w_cross.shape[1]
    own_cross = jnp.concatenate([w_cross, queries], axis=1)
    cross_rows = lax.all_gather(own_cross, "group", axis=0, tiled=False)
    cross_rows = jnp.concatenate(
        [
            cross_rows[:, :, :cross_cols].transpose(1, 0, 2).reshape(own_cross.shape[0], -1),
            cross_rows[:, :, cross_cols:].transpose(1, 0, 2).reshape(own_cross.shape[0], -1),
        ],
        axis=1,
    )
    cross = lax.all_gather(cross_rows, "expert", axis=0, tiled=True)
    cross_weights = cross[:, : groups * cross_cols]

    normed = layer_norm(tokens.astype(F32), ln_gain).astype(BF)
    target = (expert_ids.reshape(-1) * capacity + slot_numbers(expert_ids)).reshape(rows_dev, 2)
    place_ids = jnp.arange(places, dtype=jnp.int32)
    goes = (
        (place_ids[:, None] == target[None, :, 0]) | (place_ids[:, None] == target[None, :, 1])
    ).astype(BF)
    outgoing = dot(goes, normed).astype(BF).reshape(experts, capacity, width)
    arrived = lax.all_to_all(outgoing, "expert", 0, 0, tiled=True).reshape(places, width)

    blocks = ring_gather([arrived[:, :half_width], arrived[:, half_width:]], groups)
    hidden = {}
    for offset, halves in blocks.items():
        value = dot(halves[0], first[:half_width]) + dot(halves[1], first[half_width:])
        hidden[offset] = jax.nn.relu(value + b_in[0]).astype(BF)

    def partial(offset, c):
        return dot(hidden[offset], second[:, c * half_width : (c + 1) * half_width])

    sums = jnp.concatenate(ring_scatter(partial, groups), axis=1)
    expert_out = (sums + b_out[0]).astype(BF).reshape(experts, capacity, width)
    returned = lax.all_to_all(expert_out, "expert", 0, 0, tiled=True).reshape(places, width)

    moe = 0.0
    for k in range(2):
        picks = (target[:, k][:, None] == place_ids[None, :]).astype(BF)
        moe = moe + gates[:, k][:, None] * dot(picks, returned)
    encoded = layer_norm(tokens.astype(F32) + moe, final_gain).astype(BF)

    keyvals = dot(encoded, cross_weights).astype(BF).reshape(rows_dev, groups, 2, head_size)
    block = column * groups + row
    own_lengths = lax.dynamic_slice_in_dim(lengths, block, 1, 0)[0]
    owners = lax.dynamic_slice_in_dim(page_table, block, 1, 0)[0]
    slots_dev = groups * sentences
    own_queries = jnp.concatenate(
        [
            lax.dynamic_slice(
                cross,
                (owners[k] * slots_dev + row * sentences + k, groups * cross_cols),
                (1, groups * head_size),
            )
            for k in range(sentences)
        ],
        axis=0,
    ).reshape(sentences, groups, head_size)
    scores = jnp.einsum(
        "khs,rhs->hkr", own_queries, keyvals[:, :, 0], preferred_element_type=F32
    ) / math.sqrt(head_size)
    ends = jnp.cumsum(own_lengths)
    starts = ends - own_lengths
    row_ids = jnp.arange(rows_dev, dtype=jnp.int32)
    visible = (row_ids[None, :] >= starts[:, None]) & (row_ids[None, :] < ends[:, None])
    scores = jnp.where(visible[None], scores, -jnp.inf)
    highest = jnp.max(scores, axis=-1, keepdims=True)
    exponent = jnp.exp(scores - highest)
    attention = (exponent / jnp.sum(exponent, axis=-1, keepdims=True)).astype(BF)
    own_context = jnp.einsum(
        "hkr,rhs->hks", attention, keyvals[:, :, 1], preferred_element_type=F32
    ).astype(BF)

    slots = lax.all_to_all(own_context, "group", 0, 0, tiled=True).reshape(slots_dev, head_size)
    column_ids = jnp.arange(experts, dtype=jnp.int32)
    column_owners = lax.dynamic_slice_in_dim(page_table, column * groups, groups, 0).reshape(-1)
    to_owner = (column_ids[:, None] == column_owners[None, :]).astype(BF)
    sent = dot(to_owner, slots).astype(BF).reshape(experts, 1, head_size)
    received = lax.all_to_all(sent, "expert", 0, 0, tiled=True).reshape(experts, head_size)
    first_owners = page_table[:groups].reshape(-1)
    source = lax.rem(column - first_owners + experts, experts)
    from_source = (source[:, None] == column_ids[None, :]).astype(BF)
    context = dot(from_source, received).astype(BF)
    return (encoded, context)


def solution(mesh):
    return jax.shard_map(
        on_device,
        mesh=mesh,
        in_specs=(
            P(("expert", "group"), None),
            P(("expert", "group"), None),
            P(("expert", "group"), None),
            P(),
            P("expert", None, "group"),
            P("expert", "group"),
            P("expert", "group", None),
            P("expert", None),
            P(),
            P("expert", "group"),
            P(),
            P(),
            P("expert", "group"),
        ),
        out_specs=(P(("expert", "group"), None), P("expert", "group")),
        check_vma=False,
    )
```

time: 481 us -> 271 us (0.56)
  waiting for transfers between devices: 226 us -> 49.2 us
  starting transfers between devices: 26.6 us -> 111 us
  blocking collectives: 125 us -> 61.2 us
  local copies, waits for them, and re-layouts: 54.8 us -> 6.36 us
  other arithmetic: 11.3 us -> 4.79 us
    all_gather x3 -> x1, waiting for transfers between devices: 130 us -> 0.02 us  [on_device(): cross = lax.all_gather(cross_rows, 'expert', axis=0, tiled=True)]
    ppermute x0 -> x28, starting transfers between devices: none -> 81.1 us  [shift(): lax.ppermute(value, 'group', [(i, (i + by) % groups) for i in range(group...]
    all_to_all x1, blocking collectives: 111 us -> 40.5 us  [on_device(): lax.all_to_all(outgoing, 'expert', 0, 0, tiled=True).reshape(places, width)]
    reduce_scatter x1 -> x0, waiting for transfers between devices: 51.8 us -> none  [on_device(): lax.psum_scatter(jnp.dot(block_rows, second, preferred_element_type=jnp.f...]
    reshape x7 -> x5, local copies, waits for them, and re-layouts: 23.5 us -> 1.53 us  [the longest x1 0.63 us: on_device(): sent = dot(to_owner, slots).astype(BF).reshape(experts, 1, head_size)]
    ppermute x0 -> x28, waiting for transfers between devices: none -> 20.6 us  [shift(): lax.ppermute(value, 'group', [(i, (i + by) % groups) for i in range(group...]
    all_to_all x2 -> x3, waiting for transfers between devices: 43.6 us -> 28.5 us  [the longest x1 13.1 us: on_device(): lax.all_to_all(expert_out, 'expert', 0, 0, tiled=True)]
    all_to_all x1 -> x0, local copies, waits for them, and re-layouts: 7.59 us -> none  [on_device(): lax.all_to_all(outgoing, 'expert', split_axis=1, concat_axis=1, tiled=True)]
  transfers between devices with their start and end apart: 6 -> 32, of which waited for: 6 -> 13; matrix products, arithmetic and copies ran while one was open for 2% -> 7% of each run, Pallas kernels for 0% -> 0%
where the time goes in v1:
time: 271 us; the launch traced here: 269 us
  starting transfers between devices  111 us (41%)
  blocking collectives  61.2 us (23%)
  waiting for transfers between devices  49.2 us (18%)
  matrix products  19.2 us (7%)
  between operations  17.6 us (6%)
  local copies, waits for them, and re-layouts  6.36 us (2%)
  other arithmetic  4.79 us (2%)
    ppermute x28, starting transfers between devices, shift(): lax.ppermute(value, 'group', [(i, (i + by) % groups) for i in range(group...  81.1 us
    all_to_all x1, blocking collectives, on_device(): lax.all_to_all(outgoing, 'expert', 0, 0, tiled=True).reshape(places, width)  40.5 us
    all_gather x1, blocking collectives, on_device(): cross_rows = lax.all_gather(own_cross, 'group', axis=0, tiled=False)  20.7 us
    ppermute x28, waiting for transfers between devices, shift(): lax.ppermute(value, 'group', [(i, (i + by) % groups) for i in range(group...  20.6 us
    dot_general x38, matrix products, dot(): return jnp.dot(a, b, preferred_element_type=F32)  18.2 us
    all_to_all x1, starting transfers between devices, on_device(): lax.all_to_all(expert_out, 'expert', 0, 0, tiled=True)  16.7 us
    all_to_all x1, waiting for transfers between devices, on_device(): lax.all_to_all(expert_out, 'expert', 0, 0, tiled=True)  13.1 us
    all_to_all x1, waiting for transfers between devices, on_device(): lax.all_to_all(sent, 'expert', 0, 0, tiled=True).reshape(experts, head_size)  9.27 us
  transfers between devices with their start and end apart: 32, of which 13 were waited for; matrix products, arithmetic and copies ran while one was open for 7% of the time, Pallas kernels for 0%

profile of v1, /device:TPU:1, one launch (start us, length us, event | category | flops | bytes accessed | tf_op | source)
XLA Modules:
  0.0 269.2 jit_solution(11809884896635743280)
XLA Ops:
  7.2 0.8 pad_maximum_fusion.1
  8.0 20.7 %all-gather = bf16[256,384]{1,0:T(8,128)(2,1)S(1)} all-gather(bf16[32,384]{1,0:T(8,128)(2,1)S(1)} %pad_maximum_fusion.1), channel_id=2, replica_groups=mesh['expert'=64,'group'=8] {'group'}, dimensions={0}, use_global_device_ids=true | all-gather | bytes 221184 | tf_op jit(solution)/shard_map/all_gather | solution.py:105
  28.8 0.7 pad_maximum_fusion
  29.6 0.8 copy.61
  31.3 0.4 convolution_convert_fusion
  31.7 0.3 reshape.180
  32.0 40.5 %all_to_all.20 = bf16[64,2,2048]{2,1,0:T(2,128)(2,1)S(1)} all-to-all(bf16[64,2,2048]{2,1,0:T(2,128)(2,1)S(1)} %reshape.180), channel_id=1, replica_groups=mesh['expert'=64,'group'=8] {'expert'}, dimensions={0} | all-to-all | bytes 1048576 | tf_op jit(solution)/shard_map/all_to_all | solution.py:123
  72.8 3.5 %collective-permute-start.1 = (bf16[128,1024]{1,0:T(8,128)(2,1)S(1)}, bf16[128,1024]{1,0:T(8,128)(2,1)S(1)}, u32[]{:S(2)}, u32[]{:S(2)}) collective-permute-start(bf16[128,1024]{1,0:T(8,128)(2,1)S(1)} %get-tuple-element.7), channel_id=1, source_target_pairs={{0,7},{1,0},{2,1},{3,2},{4,3},{5,4},{6,5},{7,6},{8,15},{9,8},{10,9... | collective-permute-start | bytes 786440 | tf_op jit(solution)/shard_map/ppermute | solution.py:34
  76.4 2.0 collective-permute-start.10
  78.4 2.6 collective-permute-start.9
  81.0 3.9 %collective-permute-start = (bf16[128,1024]{1,0:T(8,128)(2,1)S(1)}, bf16[128,1024]{1,0:T(8,128)(2,1)S(1)}, u32[]{:S(2)}, u32[]{:S(2)}) collective-permute-start(bf16[128,1024]{1,0:T(8,128)(2,1)S(1)} %get-tuple-element.6), channel_id=1, source_target_pairs={{0,7},{1,0},{2,1},{3,2},{4,3},{5,4},{6,5},{7,6},{8,15},{9,8},{10,9... | collective-permute-start | bytes 786440 | tf_op jit(solution)/shard_map/ppermute | solution.py:34
  84.9 1.5 fusion.59
  87.5 3.2 %collective-permute-start.3 = (bf16[128,1024]{1,0:T(8,128)(2,1)S(1)}, bf16[128,1024]{1,0:T(8,128)(2,1)S(1)}, u32[]{:S(2)}, u32[]{:S(2)}) collective-permute-start(bf16[128,1024]{1,0:T(8,128)(2,1)S(1)} %collective-permute-done.1), channel_id=1, source_target_pairs={{0,7},{1,0},{2,1},{3,2},{4,3},{5,4},{6,5},{7,6},{8,15},{9,8},{10,9... | collective-permute-start | bytes 786440 | tf_op jit(solution)/shard_map/ppermute | solution.py:34
  90.7 1.8 collective-permute-done.9
  92.5 1.9 collective-permute-start.11
  94.4 2.0 collective-permute-start.12
  96.4 4.5 %collective-permute-start.2 = (bf16[128,1024]{1,0:T(8,128)(2,1)S(1)}, bf16[128,1024]{1,0:T(8,128)(2,1)S(1)}, u32[]{:S(2)}, u32[]{:S(2)}) collective-permute-start(bf16[128,1024]{1,0:T(8,128)(2,1)S(1)} %collective-permute-done), channel_id=1, source_target_pairs={{0,7},{1,0},{2,1},{3,2},{4,3},{5,4},{6,5},{7,6},{8,15},{9,8},{10,9... | collective-permute-start | bytes 786440 | tf_op jit(solution)/shard_map/ppermute | solution.py:34
  101.6 0.3 fusion.25
  103.5 3.4 %collective-permute-start.5 = (bf16[128,1024]{1,0:T(8,128)(2,1)S(1)}, bf16[128,1024]{1,0:T(8,128)(2,1)S(1)}, u32[]{:S(2)}, u32[]{:S(2)}) collective-permute-start(bf16[128,1024]{1,0:T(8,128)(2,1)S(1)} %collective-permute-done.3), channel_id=1, source_target_pairs={{0,7},{1,0},{2,1},{3,2},{4,3},{5,4},{6,5},{7,6},{8,15},{9,8},{10,9... | collective-permute-start | bytes 786440 | tf_op jit(solution)/shard_map/ppermute | solution.py:34
  106.9 1.9 collective-permute-start.13
  108.8 1.9 collective-permute-start.14
  110.8 4.6 %collective-permute-start.4 = (bf16[128,1024]{1,0:T(8,128)(2,1)S(1)}, bf16[128,1024]{1,0:T(8,128)(2,1)S(1)}, u32[]{:S(2)}, u32[]{:S(2)}) collective-permute-start(bf16[128,1024]{1,0:T(8,128)(2,1)S(1)} %collective-permute-done.2), channel_id=1, source_target_pairs={{0,7},{1,0},{2,1},{3,2},{4,3},{5,4},{6,5},{7,6},{8,15},{9,8},{10,9... | collective-permute-start | bytes 786440 | tf_op jit(solution)/shard_map/ppermute | solution.py:34
  116.0 0.3 fusion.29
  116.6 0.3 fusion.26
  117.6 1.0 collective-permute-done.4
  119.3 3.4 %collective-permute-start.6 = (bf16[128,1024]{1,0:T(8,128)(2,1)S(1)}, bf16[128,1024]{1,0:T(8,128)(2,1)S(1)}, u32[]{:S(2)}, u32[]{:S(2)}) collective-permute-start(bf16[128,1024]{1,0:T(8,128)(2,1)S(1)} %convolution_convert_fusion.4), channel_id=1, source_target_pairs={{0,1},{1,2},{2,3},{3,4},{4,5},{5,6},{6,7},{7,0},{8,9},{9,10},{10,1... | collective-permute-start | bytes 786440 | tf_op jit(solution)/shard_map/ppermute | solution.py:34
  122.7 4.0 %collective-permute-start.16 = (bf16[128,1024]{1,0:T(8,128)(2,1)S(1)}, bf16[128,1024]{1,0:T(8,128)(2,1)S(1)}, u32[]{:S(2)}, u32[]{:S(2)}) collective-permute-start(bf16[128,1024]{1,0:T(8,128)(2,1)S(1)} %collective-permute-done.5), channel_id=1, source_target_pairs={{0,7},{1,0},{2,1},{3,2},{4,3},{5,4},{6,5},{7,6},{8,15},{9,8},{10,9... | collective-permute-start | bytes 786440 | tf_op jit(solution)/shard_map/ppermute | solution.py:34
  127.0 0.3 fusion.30
  127.6 3.4 %collective-permute-start.25 = (bf16[128,1024]{1,0:T(8,128)(2,1)S(1)}, bf16[128,1024]{1,0:T(8,128)(2,1)S(1)}, u32[]{:S(2)}, u32[]{:S(2)}) collective-permute-start(bf16[128,1024]{1,0:T(8,128)(2,1)S(1)} %convolution_convert_fusion.1), channel_id=1, source_target_pairs={{0,7},{1,0},{2,1},{3,2},{4,3},{5,4},{6,5},{7,6},{8,15},{9,8},{10,9... | collective-permute-start | bytes 786440 | tf_op jit(solution)/shard_map/ppermute | solution.py:34
  131.0 1.9 collective-permute-start.15
  133.3 6.1 %collective-permute-done.15 = bf16[128,1024]{1,0:T(8,128)(2,1)S(1)} collective-permute-done((bf16[128,1024]{1,0:T(8,128)(2,1)S(1)}, bf16[128,1024]{1,0:T(8,128)(2,1)S(1)}, u32[]{:S(2)}, u32[]{:S(2)}) %collective-permute-start.15) | collective-permute-done | bytes 262176 | tf_op jit(solution)/shard_map/ppermute | solution.py:34
  139.3 0.3 fusion.31
  140.0 1.9 collective-permute-start.17
  142.3 3.4 %collective-permute-start.7 = (bf16[128,1024]{1,0:T(8,128)(2,1)S(1)}, bf16[128,1024]{1,0:T(8,128)(2,1)S(1)}, u32[]{:S(2)}, u32[]{:S(2)}) collective-permute-start(bf16[128,1024]{1,0:T(8,128)(2,1)S(1)} %add_convert_fusion.9), channel_id=1, source_target_pairs={{0,1},{1,2},{2,3},{3,4},{4,5},{5,6},{6,7},{7,0},{8,9},{9,10},{10,1... | collective-permute-start | bytes 786440 | tf_op jit(solution)/shard_map/ppermute | solution.py:34
  145.9 1.9 collective-permute-start.21
  148.2 4.6 %collective-permute-start.26 = (bf16[128,1024]{1,0:T(8,128)(2,1)S(1)}, bf16[128,1024]{1,0:T(8,128)(2,1)S(1)}, u32[]{:S(2)}, u32[]{:S(2)}) collective-permute-start(bf16[128,1024]{1,0:T(8,128)(2,1)S(1)} %add_convert_fusion.1), channel_id=1, source_target_pairs={{0,7},{1,0},{2,1},{3,2},{4,3},{5,4},{6,5},{7,6},{8,15},{9,8},{10,9... | collective-permute-start | bytes 786440 | tf_op jit(solution)/shard_map/ppermute | solution.py:34
  153.1 1.9 collective-permute-start.18
  155.4 3.3 %collective-permute-start.22 = (bf16[128,1024]{1,0:T(8,128)(2,1)S(1)}, bf16[128,1024]{1,0:T(8,128)(2,1)S(1)}, u32[]{:S(2)}, u32[]{:S(2)}) collective-permute-start(bf16[128,1024]{1,0:T(8,128)(2,1)S(1)} %add_convert_fusion.4), channel_id=1, source_target_pairs={{0,1},{1,2},{2,3},{3,4},{4,5},{5,6},{6,7},{7,0},{8,9},{9,10},{10,1... | collective-permute-start | bytes 786440 | tf_op jit(solution)/shard_map/ppermute | solution.py:34
  158.7 3.0 %collective-permute-done.18 = bf16[128,1024]{1,0:T(8,128)(2,1)S(1)} collective-permute-done((bf16[128,1024]{1,0:T(8,128)(2,1)S(1)}, bf16[128,1024]{1,0:T(8,128)(2,1)S(1)}, u32[]{:S(2)}, u32[]{:S(2)}) %collective-permute-start.18) | collective-permute-done | bytes 262176 | tf_op jit(solution)/shard_map/ppermute | solution.py:34
  161.8 2.2 collective-permute-start.19
  164.0 3.1 %collective-permute-start.8 = (bf16[128,1024]{1,0:T(8,128)(2,1)S(1)}, bf16[128,1024]{1,0:T(8,128)(2,1)S(1)}, u32[]{:S(2)}, u32[]{:S(2)}) collective-permute-start(bf16[128,1024]{1,0:T(8,128)(2,1)S(1)} %add_convert_fusion.8), channel_id=1, source_target_pairs={{0,1},{1,2},{2,3},{3,4},{4,5},{5,6},{6,7},{7,0},{8,9},{9,10},{10,1... | collective-permute-start | bytes 786440 | tf_op jit(solution)/shard_map/ppermute | solution.py:34
  167.2 1.9 collective-permute-start.23
  169.2 1.2 collective-permute-done.19
  170.4 3.6 %collective-permute-start.20 = (bf16[128,1024]{1,0:T(8,128)(2,1)S(1)}, bf16[128,1024]{1,0:T(8,128)(2,1)S(1)}, u32[]{:S(2)}, u32[]{:S(2)}) collective-permute-start(bf16[128,1024]{1,0:T(8,128)(2,1)S(1)} %add_convert_fusion.5), channel_id=1, source_target_pairs={{0,7},{1,0},{2,1},{3,2},{4,3},{5,4},{6,5},{7,6},{8,15},{9,8},{10,9... | collective-permute-start | bytes 786440 | tf_op jit(solution)/shard_map/ppermute | solution.py:34
  174.1 2.2 collective-permute-start.27
  176.4 3.0 %collective-permute-start.24 = (bf16[128,1024]{1,0:T(8,128)(2,1)S(1)}, bf16[128,1024]{1,0:T(8,128)(2,1)S(1)}, u32[]{:S(2)}, u32[]{:S(2)}) collective-permute-start(bf16[128,1024]{1,0:T(8,128)(2,1)S(1)} %add_convert_fusion.2), channel_id=1, source_target_pairs={{0,1},{1,2},{2,3},{3,4},{4,5},{5,6},{6,7},{7,0},{8,9},{9,10},{10,1... | collective-permute-start | bytes 786440 | tf_op jit(solution)/shard_map/ppermute | solution.py:34
  180.2 2.4 collective-permute-done.27
  182.6 4.7 %collective-permute-done.24 = bf16[128,1024]{1,0:T(8,128)(2,1)S(1)} collective-permute-done((bf16[128,1024]{1,0:T(8,128)(2,1)S(1)}, bf16[128,1024]{1,0:T(8,128)(2,1)S(1)}, u32[]{:S(2)}, u32[]{:S(2)}) %collective-permute-start.24) | collective-permute-done | bytes 262176 | tf_op jit(solution)/shard_map/ppermute | solution.py:34
  187.7 1.3 fusion.36
  189.0 16.7 %all-to-all-start.1 = ((bf16[64,2,2048]{2,1,0:T(2,128)(2,1)}), bf16[64,2,2048]{2,1,0:T(2,128)(2,1)S(1)}, u32[]{:S(2)}, u32[]{:S(2)}) async-start(bf16[64,2,2048]{2,1,0:T(2,128)(2,1)} %fusion.36), calls=%async_computation.1 | async-start | bytes 1048576 | tf_op jit(solution)/shard_map/all_to_all | solution.py:136
  205.8 0.9 dynamic-slice_reduce_fusion
  206.6 0.5 fusion.146
  210.0 13.1 %all-to-all-done.1 = bf16[64,2,2048]{2,1,0:T(2,128)(2,1)S(1)} async-done(((bf16[64,2,2048]{2,1,0:T(2,128)(2,1)}), bf16[64,2,2048]{2,1,0:T(2,128)(2,1)S(1)}, u32[]{:S(2)}, u32[]{:S(2)}) %all-to-all-start.1) | async-done | bytes 524320 | tf_op jit(solution)/shard_map/all_to_all | solution.py:136
  223.5 0.4 fusion.147
  224.4 5.0 %fusion.5 = bf16[64,2048]{1,0:T(8,128)(2,1)S(1)} fusion(bf16[64,2048]{1,0:T(8,128)(2,1)S(1)} %multiply_convert_fusion, bf16[2048,3072]{1,0:T(8,128)(2,1)} %all-gather.3.cloned.1.call-done), kind=kOutput, calls=%fused_computation.8 | convolution fusion | flops 537001984 | bytes 8912896 | tf_op jit(solution)/shard_map/dot_general | solution.py:30
  229.6 0.4 fusion.145
  229.9 0.8 constant_dynamic-slice_fusion.3
  231.1 0.9 convolution_convert_fusion.7
  232.0 5.3 %all-to-all-start.2 = ((bf16[8,4,128]{2,1,0:T(4,128)(2,1)}), bf16[8,4,128]{2,1,0:T(4,128)(2,1)S(1)}, u32[]{:S(2)}, u32[]{:S(2)}) async-start(bf16[8,4,128]{2,1,0:T(4,128)(2,1)} %convolution_convert_fusion.7), calls=%async_computation.2 | async-start | bytes 16384 | tf_op jit(solution)/shard_map/all_to_all | solution.py:175
  237.7 6.2 %all-to-all-done.2 = bf16[8,4,128]{2,1,0:T(4,128)(2,1)S(1)} async-done(((bf16[8,4,128]{2,1,0:T(4,128)(2,1)}), bf16[8,4,128]{2,1,0:T(4,128)(2,1)S(1)}, u32[]{:S(2)}, u32[]{:S(2)}) %all-to-all-start.2) | async-done | bytes 8224 | tf_op jit(solution)/shard_map/all_to_all | solution.py:175
  244.0 0.6 copy.69
  244.6 7.7 %all-to-all-start.3 = ((bf16[64,1,128]{2,1,0:T(2,128)(2,1)}), bf16[64,1,128]{2,1,0:T(2,128)(2,1)S(1)}, u32[]{:S(2)}, u32[]{:S(2)}) async-start(bf16[64,1,128]{2,1,0:T(2,128)(2,1)} %copy.69), calls=%async_computation.3 | async-start | bytes 65536 | tf_op jit(solution)/shard_map/all_to_all | solution.py:180
  252.3 9.3 %all-to-all-done.3 = bf16[64,1,128]{2,1,0:T(2,128)(2,1)S(1)} async-done(((bf16[64,1,128]{2,1,0:T(2,128)(2,1)}), bf16[64,1,128]{2,1,0:T(2,128)(2,1)S(1)}, u32[]{:S(2)}, u32[]{:S(2)}) %all-to-all-start.3) | async-done | bytes 16416 | tf_op jit(solution)/shard_map/all_to_all | solution.py:180
  261.6 0.8 convolution_convert_fusion.6
  (119 shorter events, 13.2 us)
Async XLA Ops:
  7.2 24.1 %copy-start.7 = (s32[64,2]{0,1:T(2,128)S(1)}, s32[64,2]{0,1:T(2,128)}, u32[]{:S(2)}) copy-start(s32[64,2]{0,1:T(2,128)} %param.14) | copy-start | bytes 1540
  7.2 23.7 %copy-start.1 = (bf16[64,2048]{1,0:T(8,128)(2,1)S(1)}, bf16[64,2048]{1,0:T(8,128)(2,1)}, u32[]{:S(2)}) copy-start(bf16[64,2048]{1,0:T(8,128)(2,1)} %param.13) | copy-start | bytes 786436
  7.2 24.1 %copy-start.3 = (f32[2048]{0:T(1024)S(1)}, f32[2048]{0:T(1024)}, u32[]{:S(2)}) copy-start(f32[2048]{0:T(1024)} %param.16) | copy-start | bytes 24580
  7.2 217.2 %all-gather.3.cloned.1.call-start = ((), (), s32[]{:S(2)}) async-start(), calls=%async_computation.4 | async-start | bytes 12779520 | tf_op jit(solution)/shard_map/all_gather | solution.py:113
  72.6 13.9 %copy-start.10 = (f32[1,512]{1,0:T(1,128)S(1)}, f32[1,512]{1,0:T(1,128)}, u32[]{:S(2)}) copy-start(f32[1,512]{1,0:T(1,128)} %param.18) | copy-start | bytes 6148
  72.8 13.7 %copy-start.9 = (bf16[1,2048,512]{2,1,0:T(8,128)(2,1)S(1)}, bf16[1,2048,512]{2,1,0:T(8,128)(2,1)}, u32[]{:S(2)}) copy-start(bf16[1,2048,512]{2,1,0:T(8,128)(2,1)} %param.17) | copy-start | bytes 6291460
  72.8 14.0 %copy-start = (bf16[1,512,2048]{2,1,0:T(8,128)(2,1)S(1)}, bf16[1,512,2048]{2,1,0:T(8,128)(2,1)}, u32[]{:S(2)}) copy-start(bf16[1,512,2048]{2,1,0:T(8,128)(2,1)} %param.19) | copy-start | bytes 6291460
  72.8 14.6 %collective-permute-start.1 = (bf16[128,1024]{1,0:T(8,128)(2,1)S(1)}, bf16[128,1024]{1,0:T(8,128)(2,1)S(1)}, u32[]{:S(2)}, u32[]{:S(2)}) collective-permute-start(bf16[128,1024]{1,0:T(8,128)(2,1)S(1)} %get-tuple-element.7), channel_id=1, source_target_pairs={{0,7},{1,0},{2,1},{3,2},{4,3},{5,4},{6,5},{7,6},{8,15},{9,8},{10,9... | collective-permute-start | bytes 786440 | tf_op jit(solution)/shard_map/ppermute | solution.py:34
  76.4 18.1 %collective-permute-start.10 = (bf16[128,1024]{1,0:T(8,128)(2,1)S(1)}, bf16[128,1024]{1,0:T(8,128)(2,1)S(1)}, u32[]{:S(2)}, u32[]{:S(2)}) collective-permute-start(bf16[128,1024]{1,0:T(8,128)(2,1)S(1)} %get-tuple-element.7), channel_id=1, source_target_pairs={{0,1},{1,2},{2,3},{3,4},{4,5},{5,6},{6,7},{7,0},{8,9},{9,10},{10,1... | collective-permute-start | bytes 786440 | tf_op jit(solution)/shard_map/ppermute | solution.py:34
  78.4 14.1 %collective-permute-start.9 = (bf16[128,1024]{1,0:T(8,128)(2,1)S(1)}, bf16[128,1024]{1,0:T(8,128)(2,1)S(1)}, u32[]{:S(2)}, u32[]{:S(2)}) collective-permute-start(bf16[128,1024]{1,0:T(8,128)(2,1)S(1)} %get-tuple-element.6), channel_id=1, source_target_pairs={{0,1},{1,2},{2,3},{3,4},{4,5},{5,6},{6,7},{7,0},{8,9},{9,10},{10,1... | collective-permute-start | bytes 786440 | tf_op jit(solution)/shard_map/ppermute | solution.py:34
  81.0 15.4 %collective-permute-start = (bf16[128,1024]{1,0:T(8,128)(2,1)S(1)}, bf16[128,1024]{1,0:T(8,128)(2,1)S(1)}, u32[]{:S(2)}, u32[]{:S(2)}) collective-permute-start(bf16[128,1024]{1,0:T(8,128)(2,1)S(1)} %get-tuple-element.6), channel_id=1, source_target_pairs={{0,7},{1,0},{2,1},{3,2},{4,3},{5,4},{6,5},{7,6},{8,15},{9,8},{10,9... | collective-permute-start | bytes 786440 | tf_op jit(solution)/shard_map/ppermute | solution.py:34
  87.5 16.1 %collective-permute-start.3 = (bf16[128,1024]{1,0:T(8,128)(2,1)S(1)}, bf16[128,1024]{1,0:T(8,128)(2,1)S(1)}, u32[]{:S(2)}, u32[]{:S(2)}) collective-permute-start(bf16[128,1024]{1,0:T(8,128)(2,1)S(1)} %collective-permute-done.1), channel_id=1, source_target_pairs={{0,7},{1,0},{2,1},{3,2},{4,3},{5,4},{6,5},{7,6},{8,15},{9,8},{10,9... | collective-permute-start | bytes 786440 | tf_op jit(solution)/shard_map/ppermute | solution.py:34
  92.5 14.4 %collective-permute-start.11 = (bf16[128,1024]{1,0:T(8,128)(2,1)S(1)}, bf16[128,1024]{1,0:T(8,128)(2,1)S(1)}, u32[]{:S(2)}, u32[]{:S(2)}) collective-permute-start(bf16[128,1024]{1,0:T(8,128)(2,1)S(1)} %collective-permute-done.9), channel_id=1, source_target_pairs={{0,1},{1,2},{2,3},{3,4},{4,5},{5,6},{6,7},{7,0},{8,9},{9,10},{10,1... | collective-permute-start | bytes 786440 | tf_op jit(solution)/shard_map/ppermute | solution.py:34
  94.4 14.4 %collective-permute-start.12 = (bf16[128,1024]{1,0:T(8,128)(2,1)S(1)}, bf16[128,1024]{1,0:T(8,128)(2,1)S(1)}, u32[]{:S(2)}, u32[]{:S(2)}) collective-permute-start(bf16[128,1024]{1,0:T(8,128)(2,1)S(1)} %collective-permute-done.10), channel_id=1, source_target_pairs={{0,1},{1,2},{2,3},{3,4},{4,5},{5,6},{6,7},{7,0},{8,9},{9,10},{10,1... | collective-permute-start | bytes 786440 | tf_op jit(solution)/shard_map/ppermute | solution.py:34
  96.4 14.3 %collective-permute-start.2 = (bf16[128,1024]{1,0:T(8,128)(2,1)S(1)}, bf16[128,1024]{1,0:T(8,128)(2,1)S(1)}, u32[]{:S(2)}, u32[]{:S(2)}) collective-permute-start(bf16[128,1024]{1,0:T(8,128)(2,1)S(1)} %collective-permute-done), channel_id=1, source_target_pairs={{0,7},{1,0},{2,1},{3,2},{4,3},{5,4},{6,5},{7,6},{8,15},{9,8},{10,9... | collective-permute-start | bytes 786440 | tf_op jit(solution)/shard_map/ppermute | solution.py:34
  103.5 13.8 %collective-permute-start.5 = (bf16[128,1024]{1,0:T(8,128)(2,1)S(1)}, bf16[128,1024]{1,0:T(8,128)(2,1)S(1)}, u32[]{:S(2)}, u32[]{:S(2)}) collective-permute-start(bf16[128,1024]{1,0:T(8,128)(2,1)S(1)} %collective-permute-done.3), channel_id=1, source_target_pairs={{0,7},{1,0},{2,1},{3,2},{4,3},{5,4},{6,5},{7,6},{8,15},{9,8},{10,9... | collective-permute-start | bytes 786440 | tf_op jit(solution)/shard_map/ppermute | solution.py:34
  106.9 20.1 %collective-permute-start.13 = (bf16[128,1024]{1,0:T(8,128)(2,1)S(1)}, bf16[128,1024]{1,0:T(8,128)(2,1)S(1)}, u32[]{:S(2)}, u32[]{:S(2)}) collective-permute-start(bf16[128,1024]{1,0:T(8,128)(2,1)S(1)} %collective-permute-done.11), channel_id=1, source_target_pairs={{0,1},{1,2},{2,3},{3,4},{4,5},{5,6},{6,7},{7,0},{8,9},{9,10},{10,1... | collective-permute-start | bytes 786440 | tf_op jit(solution)/shard_map/ppermute | solution.py:34
  108.8 17.8 %collective-permute-start.14 = (bf16[128,1024]{1,0:T(8,128)(2,1)S(1)}, bf16[128,1024]{1,0:T(8,128)(2,1)S(1)}, u32[]{:S(2)}, u32[]{:S(2)}) collective-permute-start(bf16[128,1024]{1,0:T(8,128)(2,1)S(1)} %collective-permute-done.12), channel_id=1, source_target_pairs={{0,1},{1,2},{2,3},{3,4},{4,5},{5,6},{6,7},{7,0},{8,9},{9,10},{10,1... | collective-permute-start | bytes 786440 | tf_op jit(solution)/shard_map/ppermute | solution.py:34
  110.8 7.9 %collective-permute-start.4 = (bf16[128,1024]{1,0:T(8,128)(2,1)S(1)}, bf16[128,1024]{1,0:T(8,128)(2,1)S(1)}, u32[]{:S(2)}, u32[]{:S(2)}) collective-permute-start(bf16[128,1024]{1,0:T(8,128)(2,1)S(1)} %collective-permute-done.2), channel_id=1, source_target_pairs={{0,7},{1,0},{2,1},{3,2},{4,3},{5,4},{6,5},{7,6},{8,15},{9,8},{10,9... | collective-permute-start | bytes 786440 | tf_op jit(solution)/shard_map/ppermute | solution.py:34
  119.3 22.6 %collective-permute-start.6 = (bf16[128,1024]{1,0:T(8,128)(2,1)S(1)}, bf16[128,1024]{1,0:T(8,128)(2,1)S(1)}, u32[]{:S(2)}, u32[]{:S(2)}) collective-permute-start(bf16[128,1024]{1,0:T(8,128)(2,1)S(1)} %convolution_convert_fusion.4), channel_id=1, source_target_pairs={{0,1},{1,2},{2,3},{3,4},{4,5},{5,6},{6,7},{7,0},{8,9},{9,10},{10,1... | collective-permute-start | bytes 786440 | tf_op jit(solution)/shard_map/ppermute | solution.py:34
  122.7 10.3 %collective-permute-start.16 = (bf16[128,1024]{1,0:T(8,128)(2,1)S(1)}, bf16[128,1024]{1,0:T(8,128)(2,1)S(1)}, u32[]{:S(2)}, u32[]{:S(2)}) collective-permute-start(bf16[128,1024]{1,0:T(8,128)(2,1)S(1)} %collective-permute-done.5), channel_id=1, source_target_pairs={{0,7},{1,0},{2,1},{3,2},{4,3},{5,4},{6,5},{7,6},{8,15},{9,8},{10,9... | collective-permute-start | bytes 786440 | tf_op jit(solution)/shard_map/ppermute | solution.py:34
  127.6 20.2 %collective-permute-start.25 = (bf16[128,1024]{1,0:T(8,128)(2,1)S(1)}, bf16[128,1024]{1,0:T(8,128)(2,1)S(1)}, u32[]{:S(2)}, u32[]{:S(2)}) collective-permute-start(bf16[128,1024]{1,0:T(8,128)(2,1)S(1)} %convolution_convert_fusion.1), channel_id=1, source_target_pairs={{0,7},{1,0},{2,1},{3,2},{4,3},{5,4},{6,5},{7,6},{8,15},{9,8},{10,9... | collective-permute-start | bytes 786440 | tf_op jit(solution)/shard_map/ppermute | solution.py:34
  131.0 8.3 %collective-permute-start.15 = (bf16[128,1024]{1,0:T(8,128)(2,1)S(1)}, bf16[128,1024]{1,0:T(8,128)(2,1)S(1)}, u32[]{:S(2)}, u32[]{:S(2)}) collective-permute-start(bf16[128,1024]{1,0:T(8,128)(2,1)S(1)} %collective-permute-done.13), channel_id=1, source_target_pairs={{0,1},{1,2},{2,3},{3,4},{4,5},{5,6},{6,7},{7,0},{8,9},{9,10},{10,1... | collective-permute-start | bytes 786440 | tf_op jit(solution)/shard_map/ppermute | solution.py:34
  140.0 12.8 %collective-permute-start.17 = (bf16[128,1024]{1,0:T(8,128)(2,1)S(1)}, bf16[128,1024]{1,0:T(8,128)(2,1)S(1)}, u32[]{:S(2)}, u32[]{:S(2)}) collective-permute-start(bf16[128,1024]{1,0:T(8,128)(2,1)S(1)} %convolution_convert_fusion.3), channel_id=1, source_target_pairs={{0,7},{1,0},{2,1},{3,2},{4,3},{5,4},{6,5},{7,6},{8,15},{9,8},{10,9... | collective-permute-start | bytes 786440 | tf_op jit(solution)/shard_map/ppermute | solution.py:34
  142.3 21.7 %collective-permute-start.7 = (bf16[128,1024]{1,0:T(8,128)(2,1)S(1)}, bf16[128,1024]{1,0:T(8,128)(2,1)S(1)}, u32[]{:S(2)}, u32[]{:S(2)}) collective-permute-start(bf16[128,1024]{1,0:T(8,128)(2,1)S(1)} %add_convert_fusion.9), channel_id=1, source_target_pairs={{0,1},{1,2},{2,3},{3,4},{4,5},{5,6},{6,7},{7,0},{8,9},{9,10},{10,1... | collective-permute-start | bytes 786440 | tf_op jit(solution)/shard_map/ppermute | solution.py:34
  145.9 9.2 %collective-permute-start.21 = (bf16[128,1024]{1,0:T(8,128)(2,1)S(1)}, bf16[128,1024]{1,0:T(8,128)(2,1)S(1)}, u32[]{:S(2)}, u32[]{:S(2)}) collective-permute-start(bf16[128,1024]{1,0:T(8,128)(2,1)S(1)} %convolution_convert_fusion.2), channel_id=1, source_target_pairs={{0,1},{1,2},{2,3},{3,4},{4,5},{5,6},{6,7},{7,0},{8,9},{9,10},{10,1... | collective-permute-start | bytes 786440 | tf_op jit(solution)/shard_map/ppermute | solution.py:34
  148.2 25.8 %collective-permute-start.26 = (bf16[128,1024]{1,0:T(8,128)(2,1)S(1)}, bf16[128,1024]{1,0:T(8,128)(2,1)S(1)}, u32[]{:S(2)}, u32[]{:S(2)}) collective-permute-start(bf16[128,1024]{1,0:T(8,128)(2,1)S(1)} %add_convert_fusion.1), channel_id=1, source_target_pairs={{0,7},{1,0},{2,1},{3,2},{4,3},{5,4},{6,5},{7,6},{8,15},{9,8},{10,9... | collective-permute-start | bytes 786440 | tf_op jit(solution)/shard_map/ppermute | solution.py:34
  153.1 8.6 %collective-permute-start.18 = (bf16[128,1024]{1,0:T(8,128)(2,1)S(1)}, bf16[128,1024]{1,0:T(8,128)(2,1)S(1)}, u32[]{:S(2)}, u32[]{:S(2)}) collective-permute-start(bf16[128,1024]{1,0:T(8,128)(2,1)S(1)} %add_convert_fusion.7), channel_id=1, source_target_pairs={{0,7},{1,0},{2,1},{3,2},{4,3},{5,4},{6,5},{7,6},{8,15},{9,8},{10,9... | collective-permute-start | bytes 786440 | tf_op jit(solution)/shard_map/ppermute | solution.py:34
  155.4 11.7 %collective-permute-start.22 = (bf16[128,1024]{1,0:T(8,128)(2,1)S(1)}, bf16[128,1024]{1,0:T(8,128)(2,1)S(1)}, u32[]{:S(2)}, u32[]{:S(2)}) collective-permute-start(bf16[128,1024]{1,0:T(8,128)(2,1)S(1)} %add_convert_fusion.4), channel_id=1, source_target_pairs={{0,1},{1,2},{2,3},{3,4},{4,5},{5,6},{6,7},{7,0},{8,9},{9,10},{10,1... | collective-permute-start | bytes 786440 | tf_op jit(solution)/shard_map/ppermute | solution.py:34
  161.8 8.6 %collective-permute-start.19 = (bf16[128,1024]{1,0:T(8,128)(2,1)S(1)}, bf16[128,1024]{1,0:T(8,128)(2,1)S(1)}, u32[]{:S(2)}, u32[]{:S(2)}) collective-permute-start(bf16[128,1024]{1,0:T(8,128)(2,1)S(1)} %add_convert_fusion.6), channel_id=1, source_target_pairs={{0,7},{1,0},{2,1},{3,2},{4,3},{5,4},{6,5},{7,6},{8,15},{9,8},{10,9... | collective-permute-start | bytes 786440 | tf_op jit(solution)/shard_map/ppermute | solution.py:34
  164.0 15.4 %collective-permute-start.8 = (bf16[128,1024]{1,0:T(8,128)(2,1)S(1)}, bf16[128,1024]{1,0:T(8,128)(2,1)S(1)}, u32[]{:S(2)}, u32[]{:S(2)}) collective-permute-start(bf16[128,1024]{1,0:T(8,128)(2,1)S(1)} %add_convert_fusion.8), channel_id=1, source_target_pairs={{0,1},{1,2},{2,3},{3,4},{4,5},{5,6},{6,7},{7,0},{8,9},{9,10},{10,1... | collective-permute-start | bytes 786440 | tf_op jit(solution)/shard_map/ppermute | solution.py:34
  167.2 9.1 %collective-permute-start.23 = (bf16[128,1024]{1,0:T(8,128)(2,1)S(1)}, bf16[128,1024]{1,0:T(8,128)(2,1)S(1)}, u32[]{:S(2)}, u32[]{:S(2)}) collective-permute-start(bf16[128,1024]{1,0:T(8,128)(2,1)S(1)} %add_convert_fusion.3), channel_id=1, source_target_pairs={{0,1},{1,2},{2,3},{3,4},{4,5},{5,6},{6,7},{7,0},{8,9},{9,10},{10,1... | collective-permute-start | bytes 786440 | tf_op jit(solution)/shard_map/ppermute | solution.py:34
  170.4 9.3 %collective-permute-start.20 = (bf16[128,1024]{1,0:T(8,128)(2,1)S(1)}, bf16[128,1024]{1,0:T(8,128)(2,1)S(1)}, u32[]{:S(2)}, u32[]{:S(2)}) collective-permute-start(bf16[128,1024]{1,0:T(8,128)(2,1)S(1)} %add_convert_fusion.5), channel_id=1, source_target_pairs={{0,7},{1,0},{2,1},{3,2},{4,3},{5,4},{6,5},{7,6},{8,15},{9,8},{10,9... | collective-permute-start | bytes 786440 | tf_op jit(solution)/shard_map/ppermute | solution.py:34
  174.1 8.5 %collective-permute-start.27 = (bf16[128,1024]{1,0:T(8,128)(2,1)S(1)}, bf16[128,1024]{1,0:T(8,128)(2,1)S(1)}, u32[]{:S(2)}, u32[]{:S(2)}) collective-permute-start(bf16[128,1024]{1,0:T(8,128)(2,1)S(1)} %add_convert_fusion), channel_id=1, source_target_pairs={{0,7},{1,0},{2,1},{3,2},{4,3},{5,4},{6,5},{7,6},{8,15},{9,8},{10,9... | collective-permute-start | bytes 786440 | tf_op jit(solution)/shard_map/ppermute | solution.py:34
  176.4 10.8 %collective-permute-start.24 = (bf16[128,1024]{1,0:T(8,128)(2,1)S(1)}, bf16[128,1024]{1,0:T(8,128)(2,1)S(1)}, u32[]{:S(2)}, u32[]{:S(2)}) collective-permute-start(bf16[128,1024]{1,0:T(8,128)(2,1)S(1)} %add_convert_fusion.2), channel_id=1, source_target_pairs={{0,1},{1,2},{2,3},{3,4},{4,5},{5,6},{6,7},{7,0},{8,9},{9,10},{10,1... | collective-permute-start | bytes 786440 | tf_op jit(solution)/shard_map/ppermute | solution.py:34
  179.8 7.8 %copy-start.4 = (f32[1,2048]{1,0:T(1,128)S(1)}, f32[1,2048]{1,0:T(1,128)}, u32[]{:S(2)}) copy-start(f32[1,2048]{1,0:T(1,128)} %param.20) | copy-start | bytes 24580
  187.3 18.4 %copy-start.6 = (s32[512,4]{0,1:T(4,128)S(1)}, s32[512,4]{0,1:T(4,128)}, u32[]{:S(2)}) copy-start(s32[512,4]{0,1:T(4,128)} %param.24) | copy-start | bytes 24580
  187.3 22.6 %copy-start.8 = (f32[64,2]{0,1:T(2,128)S(1)}, f32[64,2]{0,1:T(2,128)}, u32[]{:S(2)}) copy-start(f32[64,2]{0,1:T(2,128)} %param.15) | copy-start | bytes 1540
  189.0 34.0 %all-to-all-start.1 = ((bf16[64,2,2048]{2,1,0:T(2,128)(2,1)}), bf16[64,2,2048]{2,1,0:T(2,128)(2,1)S(1)}, u32[]{:S(2)}, u32[]{:S(2)}) async-start(bf16[64,2,2048]{2,1,0:T(2,128)(2,1)} %fusion.36), calls=%async_computation.1 | async-start | bytes 1048576 | tf_op jit(solution)/shard_map/all_to_all | solution.py:136
  210.0 14.2 %copy-start.5 = (f32[2048]{0:T(1024)S(1)}, f32[2048]{0:T(1024)}, u32[]{:S(2)}) copy-start(f32[2048]{0:T(1024)} %param.21) | copy-start | bytes 24580
  224.3 5.1 %copy-start.2 = (bf16[64,2048]{1,0:T(8,128)(2,1)}, bf16[64,2048]{1,0:T(8,128)(2,1)S(1)}, u32[]{:S(2)}) copy-start(bf16[64,2048]{1,0:T(8,128)(2,1)S(1)} %multiply_convert_fusion) | copy-start | bytes 786436
  232.0 11.9 %all-to-all-start.2 = ((bf16[8,4,128]{2,1,0:T(4,128)(2,1)}), bf16[8,4,128]{2,1,0:T(4,128)(2,1)S(1)}, u32[]{:S(2)}, u32[]{:S(2)}) async-start(bf16[8,4,128]{2,1,0:T(4,128)(2,1)} %convolution_convert_fusion.7), calls=%async_computation.2 | async-start | bytes 16384 | tf_op jit(solution)/shard_map/all_to_all | solution.py:175
  244.6 17.0 %all-to-all-start.3 = ((bf16[64,1,128]{2,1,0:T(2,128)(2,1)}), bf16[64,1,128]{2,1,0:T(2,128)(2,1)S(1)}, u32[]{:S(2)}, u32[]{:S(2)}) async-start(bf16[64,1,128]{2,1,0:T(2,128)(2,1)} %copy.69), calls=%async_computation.3 | async-start | bytes 65536 | tf_op jit(solution)/shard_map/all_to_all | solution.py:180
Sparse Core Ops, SparseCore 0:
  29.7 106.9 all-gather.2

commit v2 on v1

--- a/solution.py
+++ b/solution.py
@@ -3,9 +3,12 @@
 import jax
 import jax.numpy as jnp
 from jax import lax
+from jax.experimental import pallas as pl
+from jax.experimental.pallas import tpu as pltpu
 from jax.sharding import PartitionSpec as P
 
 EPSILON = 1e-05
+PAD_ROWS = 192
 BF = jnp.bfloat16
 F32 = jnp.float32
 
@@ -34,43 +37,69 @@
     return lax.ppermute(value, "group", [(i, (i + by) % groups) for i in range(groups)])
 
 
-def ring_gather(chunks, groups):
+def expert_kernel(count, *refs):
+    rows, (w1, b1, w2), outs = refs[:count], refs[count : count + 3], refs[count + 3 :]
+    size = rows[0].shape[0]
+    value = jnp.concatenate([r[...] for r in rows], axis=0) if count > 1 else rows[0][...]
+    hidden = jnp.maximum(dot(value, w1[...]) + b1[...], 0.0).astype(BF)
+    terms = dot(hidden, w2[...]).astype(BF)
+    for n in range(count):
+        outs[n][...] = terms[n * size : (n + 1) * size]
+
+
+def expert_terms(rows, w1, b1, w2):
+    count, total = len(rows), sum(r.shape[0] for r in rows)
+    depth, units = w1.shape
+    width = w2.shape[1]
+    spec = pl.BlockSpec(memory_space=pltpu.VMEM)
+    return pl.pallas_call(
+        lambda *refs: expert_kernel(count, *refs),
+        out_shape=[jax.ShapeDtypeStruct((r.shape[0], width), BF) for r in rows],
+        in_specs=[spec] * (count + 3),
+        out_specs=[spec] * count,
+        compiler_params=pltpu.CompilerParams(vmem_limit_bytes=24 * 2**20),
+        cost_estimate=pl.CostEstimate(
+            flops=2 * total * units * (depth + width),
+            bytes_accessed=2 * (units * (depth + width) + total * (depth + width)),
+            transcendentals=0,
+        ),
+    )(*rows, w1, b1, w2)
+
+
+def ring_experts(own, experts_of, groups):
+    half, middle = groups // 2, own.shape[0] // 2
+    terms = {}
+    held = {0: own}
+    forward = backward = own
+    for step in range(1, half):
+        forward, backward = shift(forward, 1, groups), shift(backward, -1, groups)
+        (forward, backward), done = lax.optimization_barrier(
+            ((forward, backward), experts_of(list(held.values())))
+        )
+        terms.update(zip(held, done))
+        held = {-step: forward, step: backward}
+    far = [shift(forward[:middle], 1, groups), shift(backward[middle:], -1, groups)]
+    far, done = lax.optimization_barrier((far, experts_of(list(held.values()))))
+    terms.update(zip(held, done))
+    terms[half] = experts_of(far)
+    return terms
+
+
+def ring_sum(terms, groups):
     half = groups // 2
-    blocks = {0: list(chunks)}
-    forward, backward = list(chunks), list(chunks)
-    for step in range(1, half):
-        for c in range(2):
-            forward[c] = shift(forward[c], 1, groups)
-            backward[c] = shift(backward[c], -1, groups)
-        blocks[-step] = list(forward)
-        blocks[step] = list(backward)
-    blocks[half] = [shift(forward[0], 1, groups), shift(backward[1], -1, groups)]
-    return blocks
-
-
-def ring_scatter(partial, groups):
-    half = groups // 2
-    totals = []
-    lengths = [(half - 1, half), (half, half - 1)]
-    running = [[None, None], [None, None]]
-    for step in range(half):
-        for c in range(2):
-            for way, sign in ((0, 1), (1, -1)):
-                hops = lengths[c][way]
-                if step >= hops:
-                    continue
-                offset = sign * (hops - step)
-                if offset == -half:
-                    offset = half
-                value = partial(offset, c)
-                if running[c][way] is not None:
-                    value = value + running[c][way].astype(F32)
-                running[c][way] = shift(value.astype(BF), sign, groups)
-    for c in range(2):
-        totals.append(
-            partial(0, c) + running[c][0].astype(F32) + running[c][1].astype(F32)
-        )
-    return totals
+    forward = shift(terms[half][0], 1, groups)
+    backward = shift(terms[half][1], -1, groups)
+    for offset in range(half - 1, 0, -1):
+        ahead, behind = terms[offset].astype(F32), terms[-offset].astype(F32)
+        if offset == half - 1:
+            middle = forward.shape[0]
+            ahead = jnp.concatenate([ahead[:middle] + forward.astype(F32), ahead[middle:]], axis=0)
+            behind = jnp.concatenate([behind[:middle], behind[middle:] + backward.astype(F32)], axis=0)
+        else:
+            ahead, behind = ahead + forward.astype(F32), behind + backward.astype(F32)
+        forward = shift(ahead.astype(BF), 1, groups)
+        backward = shift(behind.astype(BF), -1, groups)
+    return terms[0].astype(F32) + forward.astype(F32) + backward.astype(F32)
 
 
 def on_device(
@@ -98,20 +127,12 @@
     column = lax.axis_index("expert")
     row = lax.axis_index("group")
     first, second = w_in[0], w_out[0]
-    half_width = width // 2
 
     cross_cols = w_cross.shape[1]
+    shard_rows = w_cross.shape[0]
     own_cross = jnp.concatenate([w_cross, queries], axis=1)
+    own_cross = jnp.pad(own_cross, ((0, PAD_ROWS - shard_rows), (0, 0)))
     cross_rows = lax.all_gather(own_cross, "group", axis=0, tiled=False)
-    cross_rows = jnp.concatenate(
-        [
-            cross_rows[:, :, :cross_cols].transpose(1, 0, 2).reshape(own_cross.shape[0], -1),
-            cross_rows[:, :, cross_cols:].transpose(1, 0, 2).reshape(own_cross.shape[0], -1),
-        ],
-        axis=1,
-    )
-    cross = lax.all_gather(cross_rows, "expert", axis=0, tiled=True)
-    cross_weights = cross[:, : groups * cross_cols]
 
     normed = layer_norm(tokens.astype(F32), ln_gain).astype(BF)
     target = (expert_ids.reshape(-1) * capacity + slot_numbers(expert_ids)).reshape(rows_dev, 2)
@@ -122,16 +143,20 @@
     outgoing = dot(goes, normed).astype(BF).reshape(experts, capacity, width)
     arrived = lax.all_to_all(outgoing, "expert", 0, 0, tiled=True).reshape(places, width)
 
-    blocks = ring_gather([arrived[:, :half_width], arrived[:, half_width:]], groups)
-    hidden = {}
-    for offset, halves in blocks.items():
-        value = dot(halves[0], first[:half_width]) + dot(halves[1], first[half_width:])
-        hidden[offset] = jax.nn.relu(value + b_in[0]).astype(BF)
-
-    def partial(offset, c):
-        return dot(hidden[offset], second[:, c * half_width : (c + 1) * half_width])
-
-    sums = jnp.concatenate(ring_scatter(partial, groups), axis=1)
+    terms = ring_experts(arrived, lambda rows: expert_terms(rows, first, b_in, second), groups)
+    cross_rows, _ = lax.optimization_barrier((cross_rows, terms[0]))
+    cross_rows = cross_rows[:, :shard_rows]
+    cross_rows = jnp.concatenate(
+        [
+            cross_rows[:, :, :cross_cols].transpose(1, 0, 2).reshape(shard_rows, -1),
+            cross_rows[:, :, cross_cols:].transpose(1, 0, 2).reshape(shard_rows, -1),
+        ],
+        axis=1,
+    )
+    cross = lax.all_gather(cross_rows, "expert", axis=0, tiled=True)
+    cross_weights = cross[:, : groups * cross_cols]
+
+    sums = ring_sum(terms, groups)
     expert_out = (sums + b_out[0]).astype(BF).reshape(experts, capacity, width)
     returned = lax.all_to_all(expert_out, "expert", 0, 0, tiled=True).reshape(places, width)
 

time: 271 us -> 243 us (0.90)
  blocking collectives: 61.2 us -> 32 us
  starting transfers between devices: 111 us -> 83.5 us
  waiting for transfers between devices: 49.2 us -> 69.8 us
  matrix products: 19.2 us -> 8.97 us
  local copies, waits for them, and re-layouts: 6.36 us -> 16.2 us
  Pallas kernels: 0 us -> 6.89 us
    ppermute x28 -> x16, starting transfers between devices: 81.1 us -> 54.4 us  [shift(): lax.ppermute(value, 'group', [(i, (i + by) % groups) for i in range(group...]
    all_gather x1 -> x0, blocking collectives: 20.7 us -> none  [on_device(): cross_rows = lax.all_gather(own_cross, 'group', axis=0, tiled=False)]
    ppermute x28 -> x16, waiting for transfers between devices: 20.6 us -> 41.1 us  [shift(): lax.ppermute(value, 'group', [(i, (i + by) % groups) for i in range(group...]
    dot_general x38 -> x6, matrix products: 18.2 us -> 7.93 us  [dot(): return jnp.dot(a, b, preferred_element_type=F32)]
    all_to_all x1, blocking collectives: 40.5 us -> 32 us  [on_device(): lax.all_to_all(outgoing, 'expert', 0, 0, tiled=True).reshape(places, width)]
    unnamed x27 -> x33, local copies, waits for them, and re-layouts: 0.89 us -> 8.14 us
    pallas_call x0 -> x5, Pallas kernels: none -> 6.89 us  [expert_terms(): pl.pallas_call(lambda *refs: expert_kernel(count, *refs), out_shape=[jax....]
  transfers between devices with their start and end apart: 32 -> 21, of which waited for: 13 -> 16; matrix products, arithmetic and copies ran while one was open for 7% -> 5% of each run, Pallas kernels for 0% -> 3%
where the time goes in v2:
time: 243 us; the launch traced here: 242 us
  starting transfers between devices  83.5 us (34%)
  waiting for transfers between devices  69.8 us (29%)
  blocking collectives  32 us (13%)
  between operations  17.1 us (7%)
  local copies, waits for them, and re-layouts  16.2 us (7%)
  matrix products  8.97 us (4%)
  other arithmetic  7.28 us (3%)
  Pallas kernels  6.89 us (3%)
    ppermute x16, starting transfers between devices, shift(): lax.ppermute(value, 'group', [(i, (i + by) % groups) for i in range(group...  54.4 us
    ppermute x16, waiting for transfers between devices, shift(): lax.ppermute(value, 'group', [(i, (i + by) % groups) for i in range(group...  41.1 us
    all_to_all x1, blocking collectives, on_device(): lax.all_to_all(outgoing, 'expert', 0, 0, tiled=True).reshape(places, width)  32 us
    all_to_all x1, starting transfers between devices, on_device(): lax.all_to_all(expert_out, 'expert', 0, 0, tiled=True)  15.8 us
    all_to_all x1, waiting for transfers between devices, on_device(): lax.all_to_all(expert_out, 'expert', 0, 0, tiled=True)  13.1 us
    all_to_all x1, waiting for transfers between devices, on_device(): lax.all_to_all(sent, 'expert', 0, 0, tiled=True).reshape(experts, head_size)  9.27 us
    unnamed x33, local copies, waits for them, and re-layouts  8.14 us
    dot_general x6, matrix products, dot(): return jnp.dot(a, b, preferred_element_type=F32)  7.93 us
  transfers between devices with their start and end apart: 21, of which 16 were waited for; matrix products, arithmetic and copies ran while one was open for 5% of the time, Pallas kernels for 3%

profile of v2, /device:TPU:1, one launch (start us, length us, event | category | flops | bytes accessed | tf_op | source)
XLA Modules:
  0.0 241.7 jit_solution(11742919506515556747)
XLA Ops:
  7.2 1.5 fusion.23
  8.9 0.8 copy.61
  10.2 0.7 multiply_add_fusion
  10.9 1.1 convert_reduce_fusion
  12.0 1.2 fusion.14
  13.2 1.3 convolution_convert_fusion
  14.8 32.0 %all_to_all.20 = bf16[64,2,2048]{2,1,0:T(2,128)(2,1)S(1)} all-to-all(bf16[64,2,2048]{2,1,0:T(2,128)(2,1)S(1)} %reshape.173), channel_id=1, replica_groups=mesh['expert'=64,'group'=8] {'expert'}, dimensions={0} | all-to-all | bytes 1048576 | tf_op jit(solution)/shard_map/all_to_all | solution.py:144
  47.0 3.2 %collective-permute-start = (bf16[128,2048]{1,0:T(8,128)(2,1)S(1)}, bf16[128,2048]{1,0:T(8,128)(2,1)S(1)}, u32[]{:S(2)}, u32[]{:S(2)}) collective-permute-start(bf16[128,2048]{1,0:T(8,128)(2,1)S(1)} %reshape.174.refs_0_), channel_id=1, source_target_pairs={{0,1},{1,2},{2,3},{3,4},{4,5},{5,6},{6,7},{7,0},{8,9},{9,10},{10,1... | collective-permute-start | bytes 1572872 | tf_op jit(solution)/shard_map/ppermute | solution.py:37
  50.2 3.8 %collective-permute-start.1 = (bf16[128,2048]{1,0:T(8,128)(2,1)S(1)}, bf16[128,2048]{1,0:T(8,128)(2,1)}, u32[]{:S(2)}, u32[]{:S(2)}) collective-permute-start(bf16[128,2048]{1,0:T(8,128)(2,1)S(1)} %reshape.174.refs_0_), channel_id=1, source_target_pairs={{0,7},{1,0},{2,1},{3,2},{4,3},{5,4},{6,5},{7,6},{8,15},{9,8},{10,9... | collective-permute-start | bytes 1572872 | tf_op jit(solution)/shard_map/ppermute | solution.py:37
  54.1 1.6 copy-done
  55.6 1.6 copy-done.2
  57.2 0.7 copy-done.7
  57.9 0.9 shard_map.140
  58.8 6.6 %collective-permute-done.refs_0_ = bf16[128,2048]{1,0:T(8,128)(2,1)S(1)} collective-permute-done((bf16[128,2048]{1,0:T(8,128)(2,1)S(1)}, bf16[128,2048]{1,0:T(8,128)(2,1)S(1)}, u32[]{:S(2)}, u32[]{:S(2)}) %collective-permute-start) | collective-permute-done | bytes 524320 | tf_op jit(solution)/shard_map/ppermute | solution.py:37
  65.4 0.8 copy-done.5
  66.2 2.0 copy.65
  68.2 0.7 pad_maximum_fusion.2
  68.9 2.8 %collective-permute-start.2 = (bf16[128,2048]{1,0:T(8,128)(2,1)}, bf16[128,2048]{1,0:T(8,128)(2,1)S(1)}, u32[]{:S(2)}, u32[]{:S(2)}) collective-permute-start(bf16[128,2048]{1,0:T(8,128)(2,1)} %copy-done.5), channel_id=1, source_target_pairs={{0,1},{1,2},{2,3},{3,4},{4,5},{5,6},{6,7},{7,0},{8,9},{9,10},{10,1... | collective-permute-start | bytes 1572872 | tf_op jit(solution)/shard_map/ppermute | solution.py:37
  71.8 4.1 %collective-permute-start.3 = (bf16[128,2048]{1,0:T(8,128)(2,1)}, bf16[128,2048]{1,0:T(8,128)(2,1)S(1)}, u32[]{:S(2)}, u32[]{:S(2)}) collective-permute-start(bf16[128,2048]{1,0:T(8,128)(2,1)} %collective-permute-done.1.refs_1_), channel_id=1, source_target_pairs={{0,7},{1,0},{2,1},{3,2},{4,3},{5,4},{6,5},{7,6},{8,15},{9,8},{10,9... | collective-permute-start | bytes 1572872 | tf_op jit(solution)/shard_map/ppermute | solution.py:37
  76.0 1.6 copy-done.3
  77.5 1.0 copy-done.6
  78.6 2.5 %shard_map.141 = (bf16[128,2048]{1,0:T(8,128)(2,1)S(1)}, bf16[128,2048]{1,0:T(8,128)(2,1)S(1)}) custom-call(bf16[128,2048]{1,0:T(8,128)(2,1)S(1)} %copy-done.6, bf16[128,2048]{1,0:T(8,128)(2,1)} %collective-permute-done.1.refs_1_, bf16[2048,512]{1,0:T(8,128)(2,1)S(1)} %bitcast.49, f32[1,512]{1,0:T(1,128)S(1)} %copy-done.8, bf16[512,2048]{1,0:T(8,128)(2,1)S(1)} %bitcast.54), custom_call_target="tpu_custom_call" | custom-call | flops 1073741824 | bytes 6291456 | tf_op jit(solution)/shard_map/pallas_call | solution.py:55
  81.1 4.6 %collective-permute-done.2.refs_0_ = bf16[128,2048]{1,0:T(8,128)(2,1)S(1)} collective-permute-done((bf16[128,2048]{1,0:T(8,128)(2,1)}, bf16[128,2048]{1,0:T(8,128)(2,1)S(1)}, u32[]{:S(2)}, u32[]{:S(2)}) %collective-permute-start.2) | collective-permute-done | bytes 524320 | tf_op jit(solution)/shard_map/ppermute | solution.py:37
  85.7 1.1 collective-permute-done.3.refs_1_
  86.8 3.9 %collective-permute-start.4 = (bf16[128,2048]{1,0:T(8,128)(2,1)S(1)}, bf16[128,2048]{1,0:T(8,128)(2,1)S(1)}, u32[]{:S(2)}, u32[]{:S(2)}) collective-permute-start(bf16[128,2048]{1,0:T(8,128)(2,1)S(1)} %collective-permute-done.2.refs_0_), channel_id=1, source_target_pairs={{0,1},{1,2},{2,3},{3,4},{4,5},{5,6},{6,7},{7,0},{8,9},{9,10},{10,1... | collective-permute-start | bytes 1572872 | tf_op jit(solution)/shard_map/ppermute | solution.py:37
  90.7 3.1 %collective-permute-start.5 = (bf16[128,2048]{1,0:T(8,128)(2,1)S(1)}, bf16[128,2048]{1,0:T(8,128)(2,1)S(1)}, u32[]{:S(2)}, u32[]{:S(2)}) collective-permute-start(bf16[128,2048]{1,0:T(8,128)(2,1)S(1)} %collective-permute-done.3.refs_1_), channel_id=1, source_target_pairs={{0,7},{1,0},{2,1},{3,2},{4,3},{5,4},{6,5},{7,6},{8,15},{9,8},{10,9... | collective-permute-start | bytes 1572872 | tf_op jit(solution)/shard_map/ppermute | solution.py:37
  93.8 1.3 shard_map.142
  95.2 7.4 %collective-permute-done.4.refs_0_ = bf16[128,2048]{1,0:T(8,128)(2,1)S(1)} collective-permute-done((bf16[128,2048]{1,0:T(8,128)(2,1)S(1)}, bf16[128,2048]{1,0:T(8,128)(2,1)S(1)}, u32[]{:S(2)}, u32[]{:S(2)}) %collective-permute-start.4) | collective-permute-done | bytes 524320 | tf_op jit(solution)/shard_map/ppermute | solution.py:37
  102.5 1.0 collective-permute-done.5.refs_1_
  103.6 2.8 %collective-permute-start.6 = (bf16[64,2048]{1,0:T(8,128)(2,1)S(1)}, bf16[64,2048]{1,0:T(8,128)(2,1)S(1)}, u32[]{:S(2)}, u32[]{:S(2)}) collective-permute-start(bf16[64,2048]{1,0:T(8,128)(2,1)S(1)} %slice.80), channel_id=1, source_target_pairs={{0,1},{1,2},{2,3},{3,4},{4,5},{5,6},{6,7},{7,0},{8,9},{9,10},{10,1... | collective-permute-start | bytes 786440 | tf_op jit(solution)/shard_map/ppermute | solution.py:37
  106.4 4.2 %collective-permute-start.7 = (bf16[64,2048]{1,0:T(8,128)(2,1)S(1)}, bf16[64,2048]{1,0:T(8,128)(2,1)S(1)}, u32[]{:S(2)}, u32[]{:S(2)}) collective-permute-start(bf16[64,2048]{1,0:T(8,128)(2,1)S(1)} %slice.81), channel_id=1, source_target_pairs={{0,7},{1,0},{2,1},{3,2},{4,3},{5,4},{6,5},{7,6},{8,15},{9,8},{10,9... | collective-permute-start | bytes 786440 | tf_op jit(solution)/shard_map/ppermute | solution.py:37
  110.6 1.3 shard_map.143
  112.0 0.4 collective-permute-done.6.refs_0_
  112.4 1.5 collective-permute-done.7.refs_1_
  113.9 0.8 shard_map.144
  114.8 3.4 %collective-permute-start.8 = (bf16[64,2048]{1,0:T(8,128)(2,1)S(1)}, bf16[64,2048]{1,0:T(8,128)(2,1)S(1)}, u32[]{:S(2)}, u32[]{:S(2)}) collective-permute-start(bf16[64,2048]{1,0:T(8,128)(2,1)S(1)} %get-tuple-element.44), channel_id=1, source_target_pairs={{0,1},{1,2},{2,3},{3,4},{4,5},{5,6},{6,7},{7,0},{8,9},{9,10},{10,1... | collective-permute-start | bytes 786440 | tf_op jit(solution)/shard_map/ppermute | solution.py:37
  118.3 3.6 %collective-permute-start.12 = (bf16[64,2048]{1,0:T(8,128)(2,1)S(1)}, bf16[64,2048]{1,0:T(8,128)(2,1)S(1)}, u32[]{:S(2)}, u32[]{:S(2)}) collective-permute-start(bf16[64,2048]{1,0:T(8,128)(2,1)S(1)} %get-tuple-element.48), channel_id=1, source_target_pairs={{0,7},{1,0},{2,1},{3,2},{4,3},{5,4},{6,5},{7,6},{8,15},{9,8},{10,9... | collective-permute-start | bytes 786440 | tf_op jit(solution)/shard_map/ppermute | solution.py:37
  121.9 1.6 collective-permute-done.8
  123.7 1.9 collective-permute-start.9
  126.0 4.3 %collective-permute-start.13 = (bf16[128,2048]{1,0:T(8,128)(2,1)S(1)}, bf16[128,2048]{1,0:T(8,128)(2,1)S(1)}, u32[]{:S(2)}, u32[]{:S(2)}) collective-permute-start(bf16[128,2048]{1,0:T(8,128)(2,1)S(1)} %pad_maximum_fusion.1), channel_id=1, source_target_pairs={{0,7},{1,0},{2,1},{3,2},{4,3},{5,4},{6,5},{7,6},{8,15},{9,8},{10,9... | collective-permute-start | bytes 1572872 | tf_op jit(solution)/shard_map/ppermute | solution.py:37
  130.4 4.9 %collective-permute-done.9 = bf16[128,2048]{1,0:T(8,128)(2,1)S(1)} collective-permute-done((bf16[128,2048]{1,0:T(8,128)(2,1)S(1)}, bf16[128,2048]{1,0:T(8,128)(2,1)S(1)}, u32[]{:S(2)}, u32[]{:S(2)}) %collective-permute-start.9) | collective-permute-done | bytes 524320 | tf_op jit(solution)/shard_map/ppermute | solution.py:37
  135.4 1.9 collective-permute-start.10
  137.4 4.6 %collective-permute-start.14 = (bf16[128,2048]{1,0:T(8,128)(2,1)S(1)}, bf16[128,2048]{1,0:T(8,128)(2,1)S(1)}, u32[]{:S(2)}, u32[]{:S(2)}) collective-permute-start(bf16[128,2048]{1,0:T(8,128)(2,1)S(1)} %add_convert_fusion.2), channel_id=1, source_target_pairs={{0,7},{1,0},{2,1},{3,2},{4,3},{5,4},{6,5},{7,6},{8,15},{9,8},{10,9... | collective-permute-start | bytes 1572872 | tf_op jit(solution)/shard_map/ppermute | solution.py:37
  142.0 4.9 %collective-permute-done.10 = bf16[128,2048]{1,0:T(8,128)(2,1)S(1)} collective-permute-done((bf16[128,2048]{1,0:T(8,128)(2,1)S(1)}, bf16[128,2048]{1,0:T(8,128)(2,1)S(1)}, u32[]{:S(2)}, u32[]{:S(2)}) %collective-permute-start.10) | collective-permute-done | bytes 524320 | tf_op jit(solution)/shard_map/ppermute | solution.py:37
  147.0 1.9 collective-permute-start.11
  149.1 4.7 %collective-permute-start.15 = (bf16[128,2048]{1,0:T(8,128)(2,1)S(1)}, bf16[128,2048]{1,0:T(8,128)(2,1)S(1)}, u32[]{:S(2)}, u32[]{:S(2)}) collective-permute-start(bf16[128,2048]{1,0:T(8,128)(2,1)S(1)} %add_convert_fusion.1), channel_id=1, source_target_pairs={{0,7},{1,0},{2,1},{3,2},{4,3},{5,4},{6,5},{7,6},{8,15},{9,8},{10,9... | collective-permute-start | bytes 1572872 | tf_op jit(solution)/shard_map/ppermute | solution.py:37
  153.8 5.3 %collective-permute-done.11 = bf16[128,2048]{1,0:T(8,128)(2,1)S(1)} collective-permute-done((bf16[128,2048]{1,0:T(8,128)(2,1)S(1)}, bf16[128,2048]{1,0:T(8,128)(2,1)S(1)}, u32[]{:S(2)}, u32[]{:S(2)}) %collective-permute-start.11) | collective-permute-done | bytes 524320 | tf_op jit(solution)/shard_map/ppermute | solution.py:37
  159.1 1.5 collective-permute-done.15
  160.9 1.2 reshape.175
  162.1 15.8 %all-to-all-start.1 = ((bf16[64,2,2048]{2,1,0:T(2,128)(2,1)}), bf16[64,2,2048]{2,1,0:T(2,128)(2,1)S(1)}, u32[]{:S(2)}, u32[]{:S(2)}) async-start(bf16[64,2,2048]{2,1,0:T(2,128)(2,1)} %reshape.175), calls=%async_computation.1 | async-start | bytes 1048576 | tf_op jit(solution)/shard_map/all_to_all | solution.py:161
  178.0 0.9 dynamic-slice_reduce_fusion
  178.8 0.5 fusion.45
  182.1 13.1 %all-to-all-done.1 = bf16[64,2,2048]{2,1,0:T(2,128)(2,1)S(1)} async-done(((bf16[64,2,2048]{2,1,0:T(2,128)(2,1)}), bf16[64,2,2048]{2,1,0:T(2,128)(2,1)S(1)}, u32[]{:S(2)}, u32[]{:S(2)}) %all-to-all-start.1) | async-done | bytes 524320 | tf_op jit(solution)/shard_map/all_to_all | solution.py:161
  195.7 0.4 fusion.46
  196.6 5.0 %fusion.5 = bf16[64,2048]{1,0:T(8,128)(2,1)S(1)} fusion(bf16[64,2048]{1,0:T(8,128)(2,1)S(1)} %multiply_convert_fusion, bf16[2048,3072]{1,0:T(8,128)(2,1)} %all-gather.4.cloned.1.call-done), kind=kOutput, calls=%fused_computation.8 | convolution fusion | flops 537001984 | bytes 8912896 | tf_op jit(solution)/shard_map/dot_general | solution.py:33
  201.8 0.4 fusion.44
  202.2 0.8 constant_dynamic-slice_fusion.3
  203.3 0.9 convolution_convert_fusion.3
  204.2 5.5 %all-to-all-start.2 = ((bf16[8,4,128]{2,1,0:T(4,128)(2,1)}), bf16[8,4,128]{2,1,0:T(4,128)(2,1)S(1)}, u32[]{:S(2)}, u32[]{:S(2)}) async-start(bf16[8,4,128]{2,1,0:T(4,128)(2,1)} %convolution_convert_fusion.3), calls=%async_computation.2 | async-start | bytes 16384 | tf_op jit(solution)/shard_map/all_to_all | solution.py:200
  210.1 6.2 %all-to-all-done.2 = bf16[8,4,128]{2,1,0:T(4,128)(2,1)S(1)} async-done(((bf16[8,4,128]{2,1,0:T(4,128)(2,1)}), bf16[8,4,128]{2,1,0:T(4,128)(2,1)S(1)}, u32[]{:S(2)}, u32[]{:S(2)}) %all-to-all-start.2) | async-done | bytes 8224 | tf_op jit(solution)/shard_map/all_to_all | solution.py:200
  216.4 0.6 copy.69
  217.0 7.7 %all-to-all-start.3 = ((bf16[64,1,128]{2,1,0:T(2,128)(2,1)}), bf16[64,1,128]{2,1,0:T(2,128)(2,1)S(1)}, u32[]{:S(2)}, u32[]{:S(2)}) async-start(bf16[64,1,128]{2,1,0:T(2,128)(2,1)} %copy.69), calls=%async_computation.3 | async-start | bytes 65536 | tf_op jit(solution)/shard_map/all_to_all | solution.py:205
  224.8 9.3 %all-to-all-done.3 = bf16[64,1,128]{2,1,0:T(2,128)(2,1)S(1)} async-done(((bf16[64,1,128]{2,1,0:T(2,128)(2,1)}), bf16[64,1,128]{2,1,0:T(2,128)(2,1)S(1)}, u32[]{:S(2)}, u32[]{:S(2)}) %all-to-all-start.3) | async-done | bytes 16416 | tf_op jit(solution)/shard_map/all_to_all | solution.py:205
  234.0 0.8 convolution_convert_fusion.2
  (80 shorter events, 4.9 us)
Async XLA Ops:
  7.2 68.8 %copy-start.1 = (bf16[1,2048,512]{2,1,0:T(8,128)(2,1)S(1)}, bf16[1,2048,512]{2,1,0:T(8,128)(2,1)}, u32[]{:S(2)}) copy-start(bf16[1,2048,512]{2,1,0:T(8,128)(2,1)} %param.17) | copy-start | bytes 6291460
  7.2 68.8 %copy-start.8 = (f32[1,512]{1,0:T(1,128)S(1)}, f32[1,512]{1,0:T(1,128)}, u32[]{:S(2)}) copy-start(f32[1,512]{1,0:T(1,128)} %refs_3_.7) | copy-start | bytes 6148
  7.2 59.0 %all-gather.6.cloned.1.call-start = ((), (), s32[]{:S(2)}) async-start(), calls=%async_computation.5 | async-start | bytes 1327104 | tf_op jit(solution)/shard_map/all_gather | solution.py:135
  8.8 187.8 %all-gather.4.cloned.1.call-start = ((), (), s32[]{:S(2)}) async-start(), calls=%async_computation.4 | async-start | bytes 12779520 | tf_op jit(solution)/shard_map/all_gather | solution.py:156
  47.0 18.4 %collective-permute-start = (bf16[128,2048]{1,0:T(8,128)(2,1)S(1)}, bf16[128,2048]{1,0:T(8,128)(2,1)S(1)}, u32[]{:S(2)}, u32[]{:S(2)}) collective-permute-start(bf16[128,2048]{1,0:T(8,128)(2,1)S(1)} %reshape.174.refs_0_), channel_id=1, source_target_pairs={{0,1},{1,2},{2,3},{3,4},{4,5},{5,6},{6,7},{7,0},{8,9},{9,10},{10,1... | collective-permute-start | bytes 1572872 | tf_op jit(solution)/shard_map/ppermute | solution.py:37
  50.2 16.0 %collective-permute-start.1 = (bf16[128,2048]{1,0:T(8,128)(2,1)S(1)}, bf16[128,2048]{1,0:T(8,128)(2,1)}, u32[]{:S(2)}, u32[]{:S(2)}) collective-permute-start(bf16[128,2048]{1,0:T(8,128)(2,1)S(1)} %reshape.174.refs_0_), channel_id=1, source_target_pairs={{0,7},{1,0},{2,1},{3,2},{4,3},{5,4},{6,5},{7,6},{8,15},{9,8},{10,9... | collective-permute-start | bytes 1572872 | tf_op jit(solution)/shard_map/ppermute | solution.py:37
  54.0 1.6 copy-start
  55.6 1.6 copy-start.2
  57.2 0.7 copy-start.7
  65.4 0.8 copy-start.5
  68.9 16.8 %collective-permute-start.2 = (bf16[128,2048]{1,0:T(8,128)(2,1)}, bf16[128,2048]{1,0:T(8,128)(2,1)S(1)}, u32[]{:S(2)}, u32[]{:S(2)}) collective-permute-start(bf16[128,2048]{1,0:T(8,128)(2,1)} %copy-done.5), channel_id=1, source_target_pairs={{0,1},{1,2},{2,3},{3,4},{4,5},{5,6},{6,7},{7,0},{8,9},{9,10},{10,1... | collective-permute-start | bytes 1572872 | tf_op jit(solution)/shard_map/ppermute | solution.py:37
  71.8 15.0 %collective-permute-start.3 = (bf16[128,2048]{1,0:T(8,128)(2,1)}, bf16[128,2048]{1,0:T(8,128)(2,1)S(1)}, u32[]{:S(2)}, u32[]{:S(2)}) collective-permute-start(bf16[128,2048]{1,0:T(8,128)(2,1)} %collective-permute-done.1.refs_1_), channel_id=1, source_target_pairs={{0,7},{1,0},{2,1},{3,2},{4,3},{5,4},{6,5},{7,6},{8,15},{9,8},{10,9... | collective-permute-start | bytes 1572872 | tf_op jit(solution)/shard_map/ppermute | solution.py:37
  75.9 1.6 copy-start.3
  77.5 1.0 copy-start.6
  78.6 35.4 %copy-start.4 = (bf16[1,512,2048]{2,1,0:T(8,128)(2,1)S(1)}, bf16[1,512,2048]{2,1,0:T(8,128)(2,1)}, u32[]{:S(2)}) copy-start(bf16[1,512,2048]{2,1,0:T(8,128)(2,1)} %param.19) | copy-start | bytes 6291460
  86.8 15.8 %collective-permute-start.4 = (bf16[128,2048]{1,0:T(8,128)(2,1)S(1)}, bf16[128,2048]{1,0:T(8,128)(2,1)S(1)}, u32[]{:S(2)}, u32[]{:S(2)}) collective-permute-start(bf16[128,2048]{1,0:T(8,128)(2,1)S(1)} %collective-permute-done.2.refs_0_), channel_id=1, source_target_pairs={{0,1},{1,2},{2,3},{3,4},{4,5},{5,6},{6,7},{7,0},{8,9},{9,10},{10,1... | collective-permute-start | bytes 1572872 | tf_op jit(solution)/shard_map/ppermute | solution.py:37
  90.7 12.9 %collective-permute-start.5 = (bf16[128,2048]{1,0:T(8,128)(2,1)S(1)}, bf16[128,2048]{1,0:T(8,128)(2,1)S(1)}, u32[]{:S(2)}, u32[]{:S(2)}) collective-permute-start(bf16[128,2048]{1,0:T(8,128)(2,1)S(1)} %collective-permute-done.3.refs_1_), channel_id=1, source_target_pairs={{0,7},{1,0},{2,1},{3,2},{4,3},{5,4},{6,5},{7,6},{8,15},{9,8},{10,9... | collective-permute-start | bytes 1572872 | tf_op jit(solution)/shard_map/ppermute | solution.py:37
  103.6 8.8 %collective-permute-start.6 = (bf16[64,2048]{1,0:T(8,128)(2,1)S(1)}, bf16[64,2048]{1,0:T(8,128)(2,1)S(1)}, u32[]{:S(2)}, u32[]{:S(2)}) collective-permute-start(bf16[64,2048]{1,0:T(8,128)(2,1)S(1)} %slice.80), channel_id=1, source_target_pairs={{0,1},{1,2},{2,3},{3,4},{4,5},{5,6},{6,7},{7,0},{8,9},{9,10},{10,1... | collective-permute-start | bytes 786440 | tf_op jit(solution)/shard_map/ppermute | solution.py:37
  106.4 7.5 %collective-permute-start.7 = (bf16[64,2048]{1,0:T(8,128)(2,1)S(1)}, bf16[64,2048]{1,0:T(8,128)(2,1)S(1)}, u32[]{:S(2)}, u32[]{:S(2)}) collective-permute-start(bf16[64,2048]{1,0:T(8,128)(2,1)S(1)} %slice.81), channel_id=1, source_target_pairs={{0,7},{1,0},{2,1},{3,2},{4,3},{5,4},{6,5},{7,6},{8,15},{9,8},{10,9... | collective-permute-start | bytes 786440 | tf_op jit(solution)/shard_map/ppermute | solution.py:37
  112.0 48.7 %copy-start.11 = (f32[1,2048]{1,0:T(1,128)S(1)}, f32[1,2048]{1,0:T(1,128)}, u32[]{:S(2)}) copy-start(f32[1,2048]{1,0:T(1,128)} %param.20) | copy-start | bytes 24580
  114.8 63.2 %copy-start.13 = (s32[512,4]{0,1:T(4,128)S(1)}, s32[512,4]{0,1:T(4,128)}, u32[]{:S(2)}) copy-start(s32[512,4]{0,1:T(4,128)} %param.24) | copy-start | bytes 24580
  114.8 67.3 %copy-start.14 = (f32[64,2]{0,1:T(2,128)S(1)}, f32[64,2]{0,1:T(2,128)}, u32[]{:S(2)}) copy-start(f32[64,2]{0,1:T(2,128)} %param.15) | copy-start | bytes 1540
  114.8 8.8 %collective-permute-start.8 = (bf16[64,2048]{1,0:T(8,128)(2,1)S(1)}, bf16[64,2048]{1,0:T(8,128)(2,1)S(1)}, u32[]{:S(2)}, u32[]{:S(2)}) collective-permute-start(bf16[64,2048]{1,0:T(8,128)(2,1)S(1)} %get-tuple-element.44), channel_id=1, source_target_pairs={{0,1},{1,2},{2,3},{3,4},{4,5},{5,6},{6,7},{7,0},{8,9},{9,10},{10,1... | collective-permute-start | bytes 786440 | tf_op jit(solution)/shard_map/ppermute | solution.py:37
  118.3 77.5 %copy-start.9 = (bf16[64,2048]{1,0:T(8,128)(2,1)S(1)}, bf16[64,2048]{1,0:T(8,128)(2,1)}, u32[]{:S(2)}) copy-start(bf16[64,2048]{1,0:T(8,128)(2,1)} %param.13) | copy-start | bytes 786436
  118.3 7.6 %collective-permute-start.12 = (bf16[64,2048]{1,0:T(8,128)(2,1)S(1)}, bf16[64,2048]{1,0:T(8,128)(2,1)S(1)}, u32[]{:S(2)}, u32[]{:S(2)}) collective-permute-start(bf16[64,2048]{1,0:T(8,128)(2,1)S(1)} %get-tuple-element.48), channel_id=1, source_target_pairs={{0,7},{1,0},{2,1},{3,2},{4,3},{5,4},{6,5},{7,6},{8,15},{9,8},{10,9... | collective-permute-start | bytes 786440 | tf_op jit(solution)/shard_map/ppermute | solution.py:37
  123.7 72.7 %copy-start.12 = (f32[2048]{0:T(1024)S(1)}, f32[2048]{0:T(1024)}, u32[]{:S(2)}) copy-start(f32[2048]{0:T(1024)} %param.21) | copy-start | bytes 24580
  123.7 11.5 %collective-permute-start.9 = (bf16[128,2048]{1,0:T(8,128)(2,1)S(1)}, bf16[128,2048]{1,0:T(8,128)(2,1)S(1)}, u32[]{:S(2)}, u32[]{:S(2)}) collective-permute-start(bf16[128,2048]{1,0:T(8,128)(2,1)S(1)} %pad_maximum_fusion), channel_id=1, source_target_pairs={{0,1},{1,2},{2,3},{3,4},{4,5},{5,6},{6,7},{7,0},{8,9},{9,10},{10,1... | collective-permute-start | bytes 1572872 | tf_op jit(solution)/shard_map/ppermute | solution.py:37
  126.0 11.3 %collective-permute-start.13 = (bf16[128,2048]{1,0:T(8,128)(2,1)S(1)}, bf16[128,2048]{1,0:T(8,128)(2,1)S(1)}, u32[]{:S(2)}, u32[]{:S(2)}) collective-permute-start(bf16[128,2048]{1,0:T(8,128)(2,1)S(1)} %pad_maximum_fusion.1), channel_id=1, source_target_pairs={{0,7},{1,0},{2,1},{3,2},{4,3},{5,4},{6,5},{7,6},{8,15},{9,8},{10,9... | collective-permute-start | bytes 1572872 | tf_op jit(solution)/shard_map/ppermute | solution.py:37
  135.4 11.5 %collective-permute-start.10 = (bf16[128,2048]{1,0:T(8,128)(2,1)S(1)}, bf16[128,2048]{1,0:T(8,128)(2,1)S(1)}, u32[]{:S(2)}, u32[]{:S(2)}) collective-permute-start(bf16[128,2048]{1,0:T(8,128)(2,1)S(1)} %add_convert_fusion.4), channel_id=1, source_target_pairs={{0,1},{1,2},{2,3},{3,4},{4,5},{5,6},{6,7},{7,0},{8,9},{9,10},{10,1... | collective-permute-start | bytes 1572872 | tf_op jit(solution)/shard_map/ppermute | solution.py:37
  137.4 11.5 %collective-permute-start.14 = (bf16[128,2048]{1,0:T(8,128)(2,1)S(1)}, bf16[128,2048]{1,0:T(8,128)(2,1)S(1)}, u32[]{:S(2)}, u32[]{:S(2)}) collective-permute-start(bf16[128,2048]{1,0:T(8,128)(2,1)S(1)} %add_convert_fusion.2), channel_id=1, source_target_pairs={{0,7},{1,0},{2,1},{3,2},{4,3},{5,4},{6,5},{7,6},{8,15},{9,8},{10,9... | collective-permute-start | bytes 1572872 | tf_op jit(solution)/shard_map/ppermute | solution.py:37
  147.0 12.1 %collective-permute-start.11 = (bf16[128,2048]{1,0:T(8,128)(2,1)S(1)}, bf16[128,2048]{1,0:T(8,128)(2,1)S(1)}, u32[]{:S(2)}, u32[]{:S(2)}) collective-permute-start(bf16[128,2048]{1,0:T(8,128)(2,1)S(1)} %add_convert_fusion.3), channel_id=1, source_target_pairs={{0,1},{1,2},{2,3},{3,4},{4,5},{5,6},{6,7},{7,0},{8,9},{9,10},{10,1... | collective-permute-start | bytes 1572872 | tf_op jit(solution)/shard_map/ppermute | solution.py:37
  149.1 11.5 %collective-permute-start.15 = (bf16[128,2048]{1,0:T(8,128)(2,1)S(1)}, bf16[128,2048]{1,0:T(8,128)(2,1)S(1)}, u32[]{:S(2)}, u32[]{:S(2)}) collective-permute-start(bf16[128,2048]{1,0:T(8,128)(2,1)S(1)} %add_convert_fusion.1), channel_id=1, source_target_pairs={{0,7},{1,0},{2,1},{3,2},{4,3},{5,4},{6,5},{7,6},{8,15},{9,8},{10,9... | collective-permute-start | bytes 1572872 | tf_op jit(solution)/shard_map/ppermute | solution.py:37
  162.1 33.1 %all-to-all-start.1 = ((bf16[64,2,2048]{2,1,0:T(2,128)(2,1)}), bf16[64,2,2048]{2,1,0:T(2,128)(2,1)S(1)}, u32[]{:S(2)}, u32[]{:S(2)}) async-start(bf16[64,2,2048]{2,1,0:T(2,128)(2,1)} %reshape.175), calls=%async_computation.1 | async-start | bytes 1048576 | tf_op jit(solution)/shard_map/all_to_all | solution.py:161
  196.5 38.3 %copy-start.10 = (bf16[64,2048]{1,0:T(8,128)(2,1)}, bf16[64,2048]{1,0:T(8,128)(2,1)S(1)}, u32[]{:S(2)}) copy-start(bf16[64,2048]{1,0:T(8,128)(2,1)S(1)} %multiply_convert_fusion) | copy-start | bytes 786436
  204.2 12.1 %all-to-all-start.2 = ((bf16[8,4,128]{2,1,0:T(4,128)(2,1)}), bf16[8,4,128]{2,1,0:T(4,128)(2,1)S(1)}, u32[]{:S(2)}, u32[]{:S(2)}) async-start(bf16[8,4,128]{2,1,0:T(4,128)(2,1)} %convolution_convert_fusion.3), calls=%async_computation.2 | async-start | bytes 16384 | tf_op jit(solution)/shard_map/all_to_all | solution.py:200
  217.0 17.0 %all-to-all-start.3 = ((bf16[64,1,128]{2,1,0:T(2,128)(2,1)}), bf16[64,1,128]{2,1,0:T(2,128)(2,1)S(1)}, u32[]{:S(2)}, u32[]{:S(2)}) async-start(bf16[64,1,128]{2,1,0:T(2,128)(2,1)} %copy.69), calls=%async_computation.3 | async-start | bytes 65536 | tf_op jit(solution)/shard_map/all_to_all | solution.py:205
Sparse Core Ops, SparseCore 0:
  10.7 42.9 all-gather.5
  69.1 93.8 all-gather.3

commit v3 on v2

--- a/solution.py
+++ b/solution.py
@@ -20,21 +20,144 @@
     return centred * lax.rsqrt(variance + EPSILON) * gain_row
 
 
-def slot_numbers(id_rows):
-    flat_ids = id_rows.reshape(-1)
-    count = flat_ids.shape[0]
-    same_expert = (flat_ids[:, None] == flat_ids[None, :]).astype(jnp.int32)
-    position = jnp.arange(count, dtype=jnp.int32)
-    earlier = (position[None, :] < position[:, None]).astype(jnp.int32)
-    return jnp.sum(same_expert * earlier, axis=1)
-
-
 def dot(a, b):
     return jnp.dot(a, b, preferred_element_type=F32)
 
 
 def shift(value, by, groups):
     return lax.ppermute(value, "group", [(i, (i + by) % groups) for i in range(groups)])
+
+
+def whole(count):
+    return [pl.BlockSpec(memory_space=pltpu.VMEM)] * count
+
+
+def iota(shape, axis):
+    return lax.broadcasted_iota(jnp.int32, shape, axis)
+
+
+def dispatch_kernel(tokens, ids, gain, weights, asked, outgoing, picks, cross, rows_in, gain_in, sems):
+    rows = tokens.shape[0]
+    count, places = picks.shape
+    capacity = count // rows
+    cols = weights.shape[1]
+    cross[...] = jnp.zeros_like(cross)
+    copies = [
+        pltpu.make_async_copy(tokens, rows_in, sems.at[0]),
+        pltpu.make_async_copy(gain, gain_in, sems.at[1]),
+        pltpu.make_async_copy(weights, cross.at[: weights.shape[0], :cols], sems.at[2]),
+        pltpu.make_async_copy(asked, cross.at[: asked.shape[0], cols:], sems.at[3]),
+    ]
+    for copy in copies:
+        copy.start()
+    square = (count, count)
+    along, down = iota(square, 1), iota(square, 0)
+    spread = (iota((rows, count), 1) % rows == iota((rows, count), 0)).astype(BF)
+    ids_along = dot(ids[...].astype(F32).astype(BF), spread).astype(jnp.int32)
+    id_row = jnp.where(iota((1, count), 1) < rows, ids_along[0:1], ids_along[1:2])
+    id_along = jnp.broadcast_to(id_row, square)
+    id_down = jnp.sum(jnp.where(along == down, id_along, 0), axis=1, keepdims=True)
+    key_along = 2 * (along % rows) + along // rows
+    key_down = 2 * (down % rows) + down // rows
+    same = id_along == id_down
+    slot_along = jnp.sum((same & (key_down < key_along)).astype(jnp.int32), axis=0, keepdims=True)
+    slot_down = jnp.sum((same & (key_along < key_down)).astype(jnp.int32), axis=1, keepdims=True)
+    target_along = id_row * capacity + slot_along
+    target_down = id_down * capacity + slot_down
+    picks[...] = (target_down == iota((count, places), 1)).astype(BF)
+    by_assignment = (target_along == iota((places, count), 0)).astype(BF)
+    token_of = (iota((count, rows), 0) % rows == iota((count, rows), 1)).astype(BF)
+    goes = dot(by_assignment, token_of).astype(BF)
+    for copy in copies:
+        copy.wait()
+    normed = layer_norm(rows_in[...].astype(F32), gain_in[...]).astype(BF)
+    outgoing[...] = dot(goes, normed).astype(BF)
+
+
+def dispatch(tokens, expert_ids, gain, weights, asked, places):
+    rows, width = tokens.shape
+    count = expert_ids.size
+    anywhere = pl.BlockSpec(memory_space=pl.ANY)
+    return pl.pallas_call(
+        dispatch_kernel,
+        out_shape=[
+            jax.ShapeDtypeStruct((places, width), BF),
+            jax.ShapeDtypeStruct((count, places), BF),
+            jax.ShapeDtypeStruct((PAD_ROWS, weights.shape[1] + asked.shape[1]), BF),
+        ],
+        in_specs=[anywhere, *whole(1), anywhere, anywhere, anywhere],
+        out_specs=whole(3),
+        scratch_shapes=[
+            pltpu.VMEM((rows, width), BF),
+            pltpu.VMEM((1, width), F32),
+            pltpu.SemaphoreType.DMA((4,)),
+        ],
+        compiler_params=pltpu.CompilerParams(vmem_limit_bytes=40 * 2**20),
+    )(tokens, expert_ids.T, gain.reshape(1, width), weights, asked)
+
+
+def tail_kernel(
+    tokens, returned, picks, gates, gain, cross, asked, marks, encoded, context, weights, sems
+):
+    rows = tokens.shape[0]
+    count, head_size = context.shape
+    heads = weights.shape[0]
+    sentences = count // heads
+    step = 2 * head_size
+    copies = [
+        pltpu.make_async_copy(cross.at[:, h * step : (h + 1) * step], weights.at[h], sems.at[h])
+        for h in range(heads)
+    ]
+    for copy in copies:
+        copy.start()
+    picked = dot(picks[...], returned[...])
+    moe = gates[:, 0:1] * picked[:rows] + gates[:, 1:2] * picked[rows:]
+    value = layer_norm(tokens[...].astype(F32) + moe, gain[...]).astype(BF)
+    encoded[...] = value
+    head_of = iota((count, head_size), 0) // sentences
+    scores = jnp.zeros((count, rows), F32)
+    values = []
+    for h in range(heads):
+        copies[h].wait()
+        both = dot(value, weights[h]).astype(BF)
+        query = jnp.where(head_of == h, asked[...], 0).astype(BF)
+        scores += lax.dot_general(
+            query, both[:, :head_size], (((1,), (1,)), ((), ())), preferred_element_type=F32
+        )
+        values.append(both[:, head_size:])
+    scores = scores / math.sqrt(head_size)
+    row_ids = iota((count, rows), 1)
+    visible = (row_ids >= marks[:, 0:1]) & (row_ids < marks[:, 1:2])
+    scores = jnp.where(visible, scores, -jnp.inf)
+    exponent = jnp.exp(scores - jnp.max(scores, axis=-1, keepdims=True))
+    attention = (exponent / jnp.sum(exponent, axis=-1, keepdims=True)).astype(BF)
+    result = jnp.zeros((count, head_size), F32)
+    for h in range(heads):
+        result = jnp.where(head_of == h, dot(attention, values[h]), result)
+    context[...] = result.astype(BF)
+
+
+def tail(tokens, returned, picks, gates, gain, cross, asked, marks, heads):
+    rows, width = tokens.shape
+    step = 2 * asked.shape[1]
+    specs = whole(8)
+    specs[5] = pl.BlockSpec(memory_space=pl.ANY)
+    return pl.pallas_call(
+        tail_kernel,
+        out_shape=[jax.ShapeDtypeStruct((rows, width), BF), jax.ShapeDtypeStruct(asked.shape, BF)],
+        in_specs=specs,
+        out_specs=whole(2),
+        scratch_shapes=[
+            pltpu.VMEM((heads, width, step), BF),
+            pltpu.SemaphoreType.DMA((heads,)),
+        ],
+        compiler_params=pltpu.CompilerParams(vmem_limit_bytes=40 * 2**20),
+        cost_estimate=pl.CostEstimate(
+            flops=2 * rows * width * heads * step,
+            bytes_accessed=2 * width * heads * step,
+            transcendentals=0,
+        ),
+    )(tokens, returned, picks, gates, gain.reshape(1, width), cross, asked, marks)
 
 
 def expert_kernel(count, *refs):
@@ -130,17 +253,9 @@
 
     cross_cols = w_cross.shape[1]
     shard_rows = w_cross.shape[0]
-    own_cross = jnp.concatenate([w_cross, queries], axis=1)
-    own_cross = jnp.pad(own_cross, ((0, PAD_ROWS - shard_rows), (0, 0)))
+    outgoing, picks, own_cross = dispatch(tokens, expert_ids, ln_gain, w_cross, queries, places)
     cross_rows = lax.all_gather(own_cross, "group", axis=0, tiled=False)
-
-    normed = layer_norm(tokens.astype(F32), ln_gain).astype(BF)
-    target = (expert_ids.reshape(-1) * capacity + slot_numbers(expert_ids)).reshape(rows_dev, 2)
-    place_ids = jnp.arange(places, dtype=jnp.int32)
-    goes = (
-        (place_ids[:, None] == target[None, :, 0]) | (place_ids[:, None] == target[None, :, 1])
-    ).astype(BF)
-    outgoing = dot(goes, normed).astype(BF).reshape(experts, capacity, width)
+    outgoing = outgoing.reshape(experts, capacity, width)
     arrived = lax.all_to_all(outgoing, "expert", 0, 0, tiled=True).reshape(places, width)
 
     terms = ring_experts(arrived, lambda rows: expert_terms(rows, first, b_in, second), groups)
@@ -154,24 +269,16 @@
         axis=1,
     )
     cross = lax.all_gather(cross_rows, "expert", axis=0, tiled=True)
-    cross_weights = cross[:, : groups * cross_cols]
 
     sums = ring_sum(terms, groups)
     expert_out = (sums + b_out[0]).astype(BF).reshape(experts, capacity, width)
     returned = lax.all_to_all(expert_out, "expert", 0, 0, tiled=True).reshape(places, width)
 
-    moe = 0.0
-    for k in range(2):
-        picks = (target[:, k][:, None] == place_ids[None, :]).astype(BF)
-        moe = moe + gates[:, k][:, None] * dot(picks, returned)
-    encoded = layer_norm(tokens.astype(F32) + moe, final_gain).astype(BF)
-
-    keyvals = dot(encoded, cross_weights).astype(BF).reshape(rows_dev, groups, 2, head_size)
     block = column * groups + row
     own_lengths = lax.dynamic_slice_in_dim(lengths, block, 1, 0)[0]
     owners = lax.dynamic_slice_in_dim(page_table, block, 1, 0)[0]
     slots_dev = groups * sentences
-    own_queries = jnp.concatenate(
+    asked = jnp.concatenate(
         [
             lax.dynamic_slice(
                 cross,
@@ -181,21 +288,15 @@
             for k in range(sentences)
         ],
         axis=0,
-    ).reshape(sentences, groups, head_size)
-    scores = jnp.einsum(
-        "khs,rhs->hkr", own_queries, keyvals[:, :, 0], preferred_element_type=F32
-    ) / math.sqrt(head_size)
+    )
+    asked = asked.reshape(sentences, groups, head_size).transpose(1, 0, 2).reshape(-1, head_size)
     ends = jnp.cumsum(own_lengths)
-    starts = ends - own_lengths
-    row_ids = jnp.arange(rows_dev, dtype=jnp.int32)
-    visible = (row_ids[None, :] >= starts[:, None]) & (row_ids[None, :] < ends[:, None])
-    scores = jnp.where(visible[None], scores, -jnp.inf)
-    highest = jnp.max(scores, axis=-1, keepdims=True)
-    exponent = jnp.exp(scores - highest)
-    attention = (exponent / jnp.sum(exponent, axis=-1, keepdims=True)).astype(BF)
-    own_context = jnp.einsum(
-        "hkr,rhs->hks", attention, keyvals[:, :, 1], preferred_element_type=F32
-    ).astype(BF)
+    marks = jnp.tile(jnp.stack([ends - own_lengths, ends], axis=1), (groups, 1))
+
+    encoded, own_context = tail(
+        tokens, returned, picks, gates, final_gain, cross, asked, marks, groups
+    )
+    own_context = own_context.reshape(groups, sentences, head_size)
 
     slots = lax.all_to_all(own_context, "group", 0, 0, tiled=True).reshape(slots_dev, head_size)
     column_ids = jnp.arange(experts, dtype=jnp.int32)

time: 243 us -> 248 us (1.021)
  matrix products: 8.97 us -> 0.91 us
  waiting for transfers between devices: 69.8 us -> 77.3 us
  Pallas kernels: 6.89 us -> 14.1 us
  other arithmetic: 7.28 us -> 1.96 us
  local copies, waits for them, and re-layouts: 16.2 us -> 19.9 us
    ppermute x16, waiting for transfers between devices: 41.1 us -> 49 us  [shift(): lax.ppermute(value, 'group', [(i, (i + by) % groups) for i in range(group...]
    pallas_call x0 -> x2, Pallas kernels: none -> 7.35 us  [the longest x1 6.22 us: tail(): pl.pallas_call(tail_kernel, out_shape=[jax.ShapeDtypeStruct((rows, width)...]
    dot_general x6 -> x2, matrix products: 7.93 us -> 0.91 us  [dot(): return jnp.dot(a, b, preferred_element_type=F32)]
    unnamed x33 -> x40, local copies, waits for them, and re-layouts: 8.14 us -> 12.7 us
    reduce_sum x4 -> x0, other arithmetic: 2.68 us -> none  [the longest x2 1.42 us: layer_norm(): variance = jnp.mean(centred * centred, axis=-1, keepdims=True)]
  transfers between devices with their start and end apart: 21 -> 21, of which waited for: 16 -> 18; matrix products, arithmetic and copies ran while one was open for 5% -> 2% of each run, Pallas kernels for 3% -> 3%
where the time goes in v3:
time: 248 us; the launch traced here: 247 us
  starting transfers between devices  83.4 us (34%)
  waiting for transfers between devices  77.3 us (31%)
  blocking collectives  32 us (13%)
  local copies, waits for them, and re-layouts  19.9 us (8%)
  between operations  17.2 us (7%)
  Pallas kernels  14.1 us (6%)
    ppermute x16, starting transfers between devices, shift(): lax.ppermute(value, 'group', [(i, (i + by) % groups) for i in range(group...  55.1 us
    ppermute x16, waiting for transfers between devices, shift(): lax.ppermute(value, 'group', [(i, (i + by) % groups) for i in range(group...  49 us
    all_to_all x1, blocking collectives, on_device(): lax.all_to_all(outgoing, 'expert', 0, 0, tiled=True).reshape(places, width)  32 us
    all_to_all x1, starting transfers between devices, on_device(): lax.all_to_all(expert_out, 'expert', 0, 0, tiled=True)  16.6 us
    all_to_all x1, waiting for transfers between devices, on_device(): lax.all_to_all(expert_out, 'expert', 0, 0, tiled=True)  12.8 us
    unnamed x40, local copies, waits for them, and re-layouts  12.7 us
    all_to_all x1, waiting for transfers between devices, on_device(): lax.all_to_all(sent, 'expert', 0, 0, tiled=True).reshape(experts, head_size)  9.27 us
    all_to_all x1, starting transfers between devices, on_device(): lax.all_to_all(sent, 'expert', 0, 0, tiled=True).reshape(experts, head_size)  7.7 us
  transfers between devices with their start and end apart: 21, of which 18 were waited for; matrix products, arithmetic and copies ran while one was open for 2% of the time, Pallas kernels for 3%

profile of v3, /device:TPU:1, one launch (start us, length us, event | category | flops | bytes accessed | tf_op | source)
XLA Modules:
  0.0 246.8 jit_solution(8530036559125306388)
XLA Ops:
  7.2 1.1 copy-done.5
  8.3 0.7 copy-done.10
  9.0 0.7 copy-done.12
  9.7 0.7 copy-done.13
  10.4 0.7 copy-done.14
  11.1 1.1 shard_map.140
  12.3 0.3 reshape.104
  12.7 32.0 %all_to_all.20 = bf16[64,2,2048]{2,1,0:T(2,128)(2,1)S(1)} all-to-all(bf16[64,2,2048]{2,1,0:T(2,128)(2,1)S(1)} %reshape.104), channel_id=1, replica_groups=mesh['expert'=64,'group'=8] {'expert'}, dimensions={0} | all-to-all | bytes 1048576 | tf_op jit(solution)/shard_map/all_to_all | solution.py:259
  44.8 3.2 %collective-permute-start = (bf16[128,2048]{1,0:T(8,128)(2,1)S(1)}, bf16[128,2048]{1,0:T(8,128)(2,1)S(1)}, u32[]{:S(2)}, u32[]{:S(2)}) collective-permute-start(bf16[128,2048]{1,0:T(8,128)(2,1)S(1)} %reshape.105.refs_0_), channel_id=1, source_target_pairs={{0,1},{1,2},{2,3},{3,4},{4,5},{5,6},{6,7},{7,0},{8,9},{9,10},{10,1... | collective-permute-start | bytes 1572872 | tf_op jit(solution)/shard_map/ppermute | solution.py:28
  48.0 3.8 %collective-permute-start.1 = (bf16[128,2048]{1,0:T(8,128)(2,1)S(1)}, bf16[128,2048]{1,0:T(8,128)(2,1)}, u32[]{:S(2)}, u32[]{:S(2)}) collective-permute-start(bf16[128,2048]{1,0:T(8,128)(2,1)S(1)} %reshape.105.refs_0_), channel_id=1, source_target_pairs={{0,7},{1,0},{2,1},{3,2},{4,3},{5,4},{6,5},{7,6},{8,15},{9,8},{10,9... | collective-permute-start | bytes 1572872 | tf_op jit(solution)/shard_map/ppermute | solution.py:28
  51.9 1.6 copy-done.1
  53.5 0.9 shard_map.141
  54.4 11.0 %collective-permute-done.refs_0_ = bf16[128,2048]{1,0:T(8,128)(2,1)S(1)} collective-permute-done((bf16[128,2048]{1,0:T(8,128)(2,1)S(1)}, bf16[128,2048]{1,0:T(8,128)(2,1)S(1)}, u32[]{:S(2)}, u32[]{:S(2)}) %collective-permute-start) | collective-permute-done | bytes 524320 | tf_op jit(solution)/shard_map/ppermute | solution.py:28
  65.3 0.8 copy-done.7
  66.1 2.0 copy.37
  68.2 0.7 pad_maximum_fusion.2
  69.0 2.7 %collective-permute-start.2 = (bf16[128,2048]{1,0:T(8,128)(2,1)S(1)}, bf16[128,2048]{1,0:T(8,128)(2,1)S(1)}, u32[]{:S(2)}, u32[]{:S(2)}) collective-permute-start(bf16[128,2048]{1,0:T(8,128)(2,1)S(1)} %copy-done.8), channel_id=1, source_target_pairs={{0,1},{1,2},{2,3},{3,4},{4,5},{5,6},{6,7},{7,0},{8,9},{9,10},{10,1... | collective-permute-start | bytes 1572872 | tf_op jit(solution)/shard_map/ppermute | solution.py:28
  71.7 3.8 %collective-permute-start.3 = (bf16[128,2048]{1,0:T(8,128)(2,1)}, bf16[128,2048]{1,0:T(8,128)(2,1)S(1)}, u32[]{:S(2)}, u32[]{:S(2)}) collective-permute-start(bf16[128,2048]{1,0:T(8,128)(2,1)} %collective-permute-done.1.refs_1_), channel_id=1, source_target_pairs={{0,7},{1,0},{2,1},{3,2},{4,3},{5,4},{6,5},{7,6},{8,15},{9,8},{10,9... | collective-permute-start | bytes 1572872 | tf_op jit(solution)/shard_map/ppermute | solution.py:28
  75.5 1.6 copy-done.2
  77.1 2.4 shard_map.142
  79.5 5.7 %collective-permute-done.2.refs_0_ = bf16[128,2048]{1,0:T(8,128)(2,1)S(1)} collective-permute-done((bf16[128,2048]{1,0:T(8,128)(2,1)S(1)}, bf16[128,2048]{1,0:T(8,128)(2,1)S(1)}, u32[]{:S(2)}, u32[]{:S(2)}) %collective-permute-start.2) | collective-permute-done | bytes 524320 | tf_op jit(solution)/shard_map/ppermute | solution.py:28
  85.1 2.1 collective-permute-done.3.refs_1_
  87.3 3.0 %collective-permute-start.4 = (bf16[128,2048]{1,0:T(8,128)(2,1)S(1)}, bf16[128,2048]{1,0:T(8,128)(2,1)S(1)}, u32[]{:S(2)}, u32[]{:S(2)}) collective-permute-start(bf16[128,2048]{1,0:T(8,128)(2,1)S(1)} %collective-permute-done.2.refs_0_), channel_id=1, source_target_pairs={{0,1},{1,2},{2,3},{3,4},{4,5},{5,6},{6,7},{7,0},{8,9},{9,10},{10,1... | collective-permute-start | bytes 1572872 | tf_op jit(solution)/shard_map/ppermute | solution.py:28
  90.3 3.5 %collective-permute-start.5 = (bf16[128,2048]{1,0:T(8,128)(2,1)S(1)}, bf16[128,2048]{1,0:T(8,128)(2,1)S(1)}, u32[]{:S(2)}, u32[]{:S(2)}) collective-permute-start(bf16[128,2048]{1,0:T(8,128)(2,1)S(1)} %collective-permute-done.3.refs_1_), channel_id=1, source_target_pairs={{0,7},{1,0},{2,1},{3,2},{4,3},{5,4},{6,5},{7,6},{8,15},{9,8},{10,9... | collective-permute-start | bytes 1572872 | tf_op jit(solution)/shard_map/ppermute | solution.py:28
  93.8 1.3 shard_map.143
  95.1 7.3 %collective-permute-done.4.refs_0_ = bf16[128,2048]{1,0:T(8,128)(2,1)S(1)} collective-permute-done((bf16[128,2048]{1,0:T(8,128)(2,1)S(1)}, bf16[128,2048]{1,0:T(8,128)(2,1)S(1)}, u32[]{:S(2)}, u32[]{:S(2)}) %collective-permute-start.4) | collective-permute-done | bytes 524320 | tf_op jit(solution)/shard_map/ppermute | solution.py:28
  102.4 1.2 collective-permute-done.5.refs_1_
  103.7 3.4 %collective-permute-start.6 = (bf16[64,2048]{1,0:T(8,128)(2,1)S(1)}, bf16[64,2048]{1,0:T(8,128)(2,1)S(1)}, u32[]{:S(2)}, u32[]{:S(2)}) collective-permute-start(bf16[64,2048]{1,0:T(8,128)(2,1)S(1)} %slice.54), channel_id=1, source_target_pairs={{0,1},{1,2},{2,3},{3,4},{4,5},{5,6},{6,7},{7,0},{8,9},{9,10},{10,1... | collective-permute-start | bytes 786440 | tf_op jit(solution)/shard_map/ppermute | solution.py:28
  107.1 3.6 %collective-permute-start.7 = (bf16[64,2048]{1,0:T(8,128)(2,1)S(1)}, bf16[64,2048]{1,0:T(8,128)(2,1)S(1)}, u32[]{:S(2)}, u32[]{:S(2)}) collective-permute-start(bf16[64,2048]{1,0:T(8,128)(2,1)S(1)} %slice.55), channel_id=1, source_target_pairs={{0,7},{1,0},{2,1},{3,2},{4,3},{5,4},{6,5},{7,6},{8,15},{9,8},{10,9... | collective-permute-start | bytes 786440 | tf_op jit(solution)/shard_map/ppermute | solution.py:28
  110.8 1.3 shard_map.144
  112.1 0.3 collective-permute-done.6.refs_0_
  112.4 2.3 collective-permute-done.7.refs_1_
  114.7 0.8 shard_map.145
  115.5 4.4 %collective-permute-start.12 = (bf16[64,2048]{1,0:T(8,128)(2,1)S(1)}, bf16[64,2048]{1,0:T(8,128)(2,1)S(1)}, u32[]{:S(2)}, u32[]{:S(2)}) collective-permute-start(bf16[64,2048]{1,0:T(8,128)(2,1)S(1)} %get-tuple-element.54), channel_id=1, source_target_pairs={{0,7},{1,0},{2,1},{3,2},{4,3},{5,4},{6,5},{7,6},{8,15},{9,8},{10,9... | collective-permute-start | bytes 786440 | tf_op jit(solution)/shard_map/ppermute | solution.py:28
  120.0 1.9 collective-permute-start.8
  121.9 1.3 collective-permute-done.12
  123.4 5.0 %collective-permute-start.13 = (bf16[128,2048]{1,0:T(8,128)(2,1)S(1)}, bf16[128,2048]{1,0:T(8,128)(2,1)S(1)}, u32[]{:S(2)}, u32[]{:S(2)}) collective-permute-start(bf16[128,2048]{1,0:T(8,128)(2,1)S(1)} %pad_maximum_fusion.1), channel_id=1, source_target_pairs={{0,7},{1,0},{2,1},{3,2},{4,3},{5,4},{6,5},{7,6},{8,15},{9,8},{10,9... | collective-permute-start | bytes 1572872 | tf_op jit(solution)/shard_map/ppermute | solution.py:28
  128.4 0.3 collective-permute-done.8
  128.8 1.9 collective-permute-start.9
  130.8 3.7 %collective-permute-done.13 = bf16[128,2048]{1,0:T(8,128)(2,1)S(1)} collective-permute-done((bf16[128,2048]{1,0:T(8,128)(2,1)S(1)}, bf16[128,2048]{1,0:T(8,128)(2,1)S(1)}, u32[]{:S(2)}, u32[]{:S(2)}) %collective-permute-start.13) | collective-permute-done | bytes 524320 | tf_op jit(solution)/shard_map/ppermute | solution.py:28
  134.6 5.5 %collective-permute-start.14 = (bf16[128,2048]{1,0:T(8,128)(2,1)S(1)}, bf16[128,2048]{1,0:T(8,128)(2,1)S(1)}, u32[]{:S(2)}, u32[]{:S(2)}) collective-permute-start(bf16[128,2048]{1,0:T(8,128)(2,1)S(1)} %add_convert_fusion.2), channel_id=1, source_target_pairs={{0,7},{1,0},{2,1},{3,2},{4,3},{5,4},{6,5},{7,6},{8,15},{9,8},{10,9... | collective-permute-start | bytes 1572872 | tf_op jit(solution)/shard_map/ppermute | solution.py:28
  140.2 0.4 collective-permute-done.9
  140.7 1.9 collective-permute-start.10
  142.6 3.7 %collective-permute-done.14 = bf16[128,2048]{1,0:T(8,128)(2,1)S(1)} collective-permute-done((bf16[128,2048]{1,0:T(8,128)(2,1)S(1)}, bf16[128,2048]{1,0:T(8,128)(2,1)S(1)}, u32[]{:S(2)}, u32[]{:S(2)}) %collective-permute-start.14) | collective-permute-done | bytes 524320 | tf_op jit(solution)/shard_map/ppermute | solution.py:28
  146.4 5.4 %collective-permute-start.15 = (bf16[128,2048]{1,0:T(8,128)(2,1)S(1)}, bf16[128,2048]{1,0:T(8,128)(2,1)S(1)}, u32[]{:S(2)}, u32[]{:S(2)}) collective-permute-start(bf16[128,2048]{1,0:T(8,128)(2,1)S(1)} %add_convert_fusion.1), channel_id=1, source_target_pairs={{0,7},{1,0},{2,1},{3,2},{4,3},{5,4},{6,5},{7,6},{8,15},{9,8},{10,9... | collective-permute-start | bytes 1572872 | tf_op jit(solution)/shard_map/ppermute | solution.py:28
  151.8 0.4 collective-permute-done.10
  152.3 1.9 collective-permute-start.11
  154.2 3.9 %collective-permute-done.15 = bf16[128,2048]{1,0:T(8,128)(2,1)S(1)} collective-permute-done((bf16[128,2048]{1,0:T(8,128)(2,1)S(1)}, bf16[128,2048]{1,0:T(8,128)(2,1)S(1)}, u32[]{:S(2)}, u32[]{:S(2)}) %collective-permute-start.15) | collective-permute-done | bytes 524320 | tf_op jit(solution)/shard_map/ppermute | solution.py:28
  158.2 5.5 %collective-permute-done.11 = bf16[128,2048]{1,0:T(8,128)(2,1)S(1)} collective-permute-done((bf16[128,2048]{1,0:T(8,128)(2,1)S(1)}, bf16[128,2048]{1,0:T(8,128)(2,1)S(1)}, u32[]{:S(2)}, u32[]{:S(2)}) %collective-permute-start.11) | collective-permute-done | bytes 524320 | tf_op jit(solution)/shard_map/ppermute | solution.py:28
  163.6 0.3 add_convert_fusion
  163.9 1.2 reshape.106
  165.1 16.6 %all-to-all-start.1 = ((bf16[64,2,2048]{2,1,0:T(2,128)(2,1)}), bf16[64,2,2048]{2,1,0:T(2,128)(2,1)S(1)}, u32[]{:S(2)}, u32[]{:S(2)}) async-start(bf16[64,2,2048]{2,1,0:T(2,128)(2,1)} %reshape.106), calls=%async_computation.1 | async-start | bytes 1048576 | tf_op jit(solution)/shard_map/all_to_all | solution.py:275
  181.8 0.9 dynamic-slice_reduce_fusion
  182.7 0.6 fusion.6
  186.2 12.8 %all-to-all-done.1 = bf16[64,2,2048]{2,1,0:T(2,128)(2,1)S(1)} async-done(((bf16[64,2,2048]{2,1,0:T(2,128)(2,1)}), bf16[64,2,2048]{2,1,0:T(2,128)(2,1)S(1)}, u32[]{:S(2)}, u32[]{:S(2)}) %all-to-all-start.1) | async-done | bytes 524320 | tf_op jit(solution)/shard_map/all_to_all | solution.py:275
  199.2 0.8 constant_dynamic-slice_fusion.3
  200.1 4.6 %copy-done.4 = bf16[2048,3072]{1,0:T(8,128)(2,1)S(1)} copy-done((bf16[2048,3072]{1,0:T(8,128)(2,1)S(1)}, bf16[2048,3072]{1,0:T(8,128)(2,1)}, u32[]{:S(2)}) %copy-start.4) | copy-done | bytes 12582936
  204.7 6.2 %shard_map.146 = (bf16[64,2048]{1,0:T(8,128)(2,1)}, bf16[32,128]{1,0:T(8,128)(2,1)}) custom-call(bf16[64,2048]{1,0:T(8,128)(2,1)S(1)} %copy-done.6, bf16[128,2048]{1,0:T(8,128)(2,1)S(1)} %reshape.107.returned, bf16[128,128]{1,0:T(8,128)(2,1)S(1)} %get-tuple-element.55.picks, f32[64,2]{1,0:T(8,128)S(1)} %copy.40.gates, f32[1,2048]{1,0:T(1,128)S(1)} %bitcast.47, ...), custom_call_target="tpu_custom_call" | custom-call | flops 536870912 | bytes 8388608 | tf_op jit(solution)/shard_map/pallas_call | solution.py:145
  210.9 3.9 %all-to-all-start.2 = ((bf16[8,4,128]{2,1,0:T(4,128)(2,1)}), bf16[8,4,128]{2,1,0:T(4,128)(2,1)S(1)}, u32[]{:S(2)}, u32[]{:S(2)}) async-start(bf16[8,4,128]{2,1,0:T(4,128)(2,1)} %bitcast.17), calls=%async_computation.2 | async-start | bytes 16384 | tf_op jit(solution)/shard_map/all_to_all | solution.py:301
  215.2 6.2 %all-to-all-done.2 = bf16[8,4,128]{2,1,0:T(4,128)(2,1)S(1)} async-done(((bf16[8,4,128]{2,1,0:T(4,128)(2,1)}), bf16[8,4,128]{2,1,0:T(4,128)(2,1)S(1)}, u32[]{:S(2)}, u32[]{:S(2)}) %all-to-all-start.2) | async-done | bytes 8224 | tf_op jit(solution)/shard_map/all_to_all | solution.py:301
  221.5 0.6 copy.44
  222.2 7.7 %all-to-all-start.3 = ((bf16[64,1,128]{2,1,0:T(2,128)(2,1)}), bf16[64,1,128]{2,1,0:T(2,128)(2,1)S(1)}, u32[]{:S(2)}, u32[]{:S(2)}) async-start(bf16[64,1,128]{2,1,0:T(2,128)(2,1)} %copy.44), calls=%async_computation.3 | async-start | bytes 65536 | tf_op jit(solution)/shard_map/all_to_all | solution.py:306
  229.9 9.3 %all-to-all-done.3 = bf16[64,1,128]{2,1,0:T(2,128)(2,1)S(1)} async-done(((bf16[64,1,128]{2,1,0:T(2,128)(2,1)}), bf16[64,1,128]{2,1,0:T(2,128)(2,1)S(1)}, u32[]{:S(2)}, u32[]{:S(2)}) %all-to-all-start.3) | async-done | bytes 16416 | tf_op jit(solution)/shard_map/all_to_all | solution.py:306
  239.2 0.8 convolution_convert_fusion.1
  (66 shorter events, 2.4 us)
Async XLA Ops:
  7.2 44.7 %copy-start = (bf16[1,2048,512]{2,1,0:T(8,128)(2,1)S(1)}, bf16[1,2048,512]{2,1,0:T(8,128)(2,1)}, u32[]{:S(2)}) copy-start(bf16[1,2048,512]{2,1,0:T(8,128)(2,1)} %param.17) | copy-start | bytes 6291460
  7.2 59.0 %all-gather.6.cloned.1.call-start = ((), (), s32[]{:S(2)}) async-start(), calls=%async_computation.5 | async-start | bytes 1327104 | tf_op jit(solution)/shard_map/all_gather | solution.py:257
  7.2 1.1 copy-start.5
  8.3 0.7 copy-start.10
  9.0 0.7 copy-start.12
  9.7 0.7 copy-start.13
  10.4 0.7 copy-start.14
  11.1 40.8 %copy-start.9 = (f32[1,512]{1,0:T(1,128)S(1)}, f32[1,512]{1,0:T(1,128)}, u32[]{:S(2)}) copy-start(f32[1,512]{1,0:T(1,128)} %refs_3_.7) | copy-start | bytes 6148
  12.3 186.9 %all-gather.4.cloned.1.call-start = ((), (), s32[]{:S(2)}) async-start(), calls=%async_computation.4 | async-start | bytes 12779520 | tf_op jit(solution)/shard_map/all_gather | solution.py:271
  44.8 20.5 %collective-permute-start = (bf16[128,2048]{1,0:T(8,128)(2,1)S(1)}, bf16[128,2048]{1,0:T(8,128)(2,1)S(1)}, u32[]{:S(2)}, u32[]{:S(2)}) collective-permute-start(bf16[128,2048]{1,0:T(8,128)(2,1)S(1)} %reshape.105.refs_0_), channel_id=1, source_target_pairs={{0,1},{1,2},{2,3},{3,4},{4,5},{5,6},{6,7},{7,0},{8,9},{9,10},{10,1... | collective-permute-start | bytes 1572872 | tf_op jit(solution)/shard_map/ppermute | solution.py:28
  48.0 18.1 %collective-permute-start.1 = (bf16[128,2048]{1,0:T(8,128)(2,1)S(1)}, bf16[128,2048]{1,0:T(8,128)(2,1)}, u32[]{:S(2)}, u32[]{:S(2)}) collective-permute-start(bf16[128,2048]{1,0:T(8,128)(2,1)S(1)} %reshape.105.refs_0_), channel_id=1, source_target_pairs={{0,7},{1,0},{2,1},{3,2},{4,3},{5,4},{6,5},{7,6},{8,15},{9,8},{10,9... | collective-permute-start | bytes 1572872 | tf_op jit(solution)/shard_map/ppermute | solution.py:28
  51.9 1.6 copy-start.1
  65.3 0.8 copy-start.7
  66.1 2.8 %copy-start.8 = (bf16[128,2048]{1,0:T(8,128)(2,1)S(1)}, bf16[128,2048]{1,0:T(8,128)(2,1)}, u32[]{:S(2)}) copy-start(bf16[128,2048]{1,0:T(8,128)(2,1)} %copy-done.7) | copy-start | bytes 1572868
  69.0 16.2 %collective-permute-start.2 = (bf16[128,2048]{1,0:T(8,128)(2,1)S(1)}, bf16[128,2048]{1,0:T(8,128)(2,1)S(1)}, u32[]{:S(2)}, u32[]{:S(2)}) collective-permute-start(bf16[128,2048]{1,0:T(8,128)(2,1)S(1)} %copy-done.8), channel_id=1, source_target_pairs={{0,1},{1,2},{2,3},{3,4},{4,5},{5,6},{6,7},{7,0},{8,9},{9,10},{10,1... | collective-permute-start | bytes 1572872 | tf_op jit(solution)/shard_map/ppermute | solution.py:28
  71.7 15.6 %collective-permute-start.3 = (bf16[128,2048]{1,0:T(8,128)(2,1)}, bf16[128,2048]{1,0:T(8,128)(2,1)S(1)}, u32[]{:S(2)}, u32[]{:S(2)}) collective-permute-start(bf16[128,2048]{1,0:T(8,128)(2,1)} %collective-permute-done.1.refs_1_), channel_id=1, source_target_pairs={{0,7},{1,0},{2,1},{3,2},{4,3},{5,4},{6,5},{7,6},{8,15},{9,8},{10,9... | collective-permute-start | bytes 1572872 | tf_op jit(solution)/shard_map/ppermute | solution.py:28
  75.5 1.6 copy-start.2
  87.3 15.1 %collective-permute-start.4 = (bf16[128,2048]{1,0:T(8,128)(2,1)S(1)}, bf16[128,2048]{1,0:T(8,128)(2,1)S(1)}, u32[]{:S(2)}, u32[]{:S(2)}) collective-permute-start(bf16[128,2048]{1,0:T(8,128)(2,1)S(1)} %collective-permute-done.2.refs_0_), channel_id=1, source_target_pairs={{0,1},{1,2},{2,3},{3,4},{4,5},{5,6},{6,7},{7,0},{8,9},{9,10},{10,1... | collective-permute-start | bytes 1572872 | tf_op jit(solution)/shard_map/ppermute | solution.py:28
  90.3 13.4 %collective-permute-start.5 = (bf16[128,2048]{1,0:T(8,128)(2,1)S(1)}, bf16[128,2048]{1,0:T(8,128)(2,1)S(1)}, u32[]{:S(2)}, u32[]{:S(2)}) collective-permute-start(bf16[128,2048]{1,0:T(8,128)(2,1)S(1)} %collective-permute-done.3.refs_1_), channel_id=1, source_target_pairs={{0,7},{1,0},{2,1},{3,2},{4,3},{5,4},{6,5},{7,6},{8,15},{9,8},{10,9... | collective-permute-start | bytes 1572872 | tf_op jit(solution)/shard_map/ppermute | solution.py:28
  103.7 8.7 %collective-permute-start.6 = (bf16[64,2048]{1,0:T(8,128)(2,1)S(1)}, bf16[64,2048]{1,0:T(8,128)(2,1)S(1)}, u32[]{:S(2)}, u32[]{:S(2)}) collective-permute-start(bf16[64,2048]{1,0:T(8,128)(2,1)S(1)} %slice.54), channel_id=1, source_target_pairs={{0,1},{1,2},{2,3},{3,4},{4,5},{5,6},{6,7},{7,0},{8,9},{9,10},{10,1... | collective-permute-start | bytes 786440 | tf_op jit(solution)/shard_map/ppermute | solution.py:28
  107.1 7.6 %copy-start.3 = (bf16[1,512,2048]{2,1,0:T(8,128)(2,1)S(1)}, bf16[1,512,2048]{2,1,0:T(8,128)(2,1)}, u32[]{:S(2)}) copy-start(bf16[1,512,2048]{2,1,0:T(8,128)(2,1)} %param.19) | copy-start | bytes 6291460
  107.1 7.5 %collective-permute-start.7 = (bf16[64,2048]{1,0:T(8,128)(2,1)S(1)}, bf16[64,2048]{1,0:T(8,128)(2,1)S(1)}, u32[]{:S(2)}, u32[]{:S(2)}) collective-permute-start(bf16[64,2048]{1,0:T(8,128)(2,1)S(1)} %slice.55), channel_id=1, source_target_pairs={{0,7},{1,0},{2,1},{3,2},{4,3},{5,4},{6,5},{7,6},{8,15},{9,8},{10,9... | collective-permute-start | bytes 786440 | tf_op jit(solution)/shard_map/ppermute | solution.py:28
  115.5 7.7 %collective-permute-start.12 = (bf16[64,2048]{1,0:T(8,128)(2,1)S(1)}, bf16[64,2048]{1,0:T(8,128)(2,1)S(1)}, u32[]{:S(2)}, u32[]{:S(2)}) collective-permute-start(bf16[64,2048]{1,0:T(8,128)(2,1)S(1)} %get-tuple-element.54), channel_id=1, source_target_pairs={{0,7},{1,0},{2,1},{3,2},{4,3},{5,4},{6,5},{7,6},{8,15},{9,8},{10,9... | collective-permute-start | bytes 786440 | tf_op jit(solution)/shard_map/ppermute | solution.py:28
  120.0 8.7 %collective-permute-start.8 = (bf16[64,2048]{1,0:T(8,128)(2,1)S(1)}, bf16[64,2048]{1,0:T(8,128)(2,1)S(1)}, u32[]{:S(2)}, u32[]{:S(2)}) collective-permute-start(bf16[64,2048]{1,0:T(8,128)(2,1)S(1)} %get-tuple-element.50), channel_id=1, source_target_pairs={{0,1},{1,2},{2,3},{3,4},{4,5},{5,6},{6,7},{7,0},{8,9},{9,10},{10,1... | collective-permute-start | bytes 786440 | tf_op jit(solution)/shard_map/ppermute | solution.py:28
  123.4 11.1 %collective-permute-start.13 = (bf16[128,2048]{1,0:T(8,128)(2,1)S(1)}, bf16[128,2048]{1,0:T(8,128)(2,1)S(1)}, u32[]{:S(2)}, u32[]{:S(2)}) collective-permute-start(bf16[128,2048]{1,0:T(8,128)(2,1)S(1)} %pad_maximum_fusion.1), channel_id=1, source_target_pairs={{0,7},{1,0},{2,1},{3,2},{4,3},{5,4},{6,5},{7,6},{8,15},{9,8},{10,9... | collective-permute-start | bytes 1572872 | tf_op jit(solution)/shard_map/ppermute | solution.py:28
  128.8 11.7 %collective-permute-start.9 = (bf16[128,2048]{1,0:T(8,128)(2,1)S(1)}, bf16[128,2048]{1,0:T(8,128)(2,1)S(1)}, u32[]{:S(2)}, u32[]{:S(2)}) collective-permute-start(bf16[128,2048]{1,0:T(8,128)(2,1)S(1)} %pad_maximum_fusion), channel_id=1, source_target_pairs={{0,1},{1,2},{2,3},{3,4},{4,5},{5,6},{6,7},{7,0},{8,9},{9,10},{10,1... | collective-permute-start | bytes 1572872 | tf_op jit(solution)/shard_map/ppermute | solution.py:28
  134.6 29.0 %copy-start.15 = (f32[1,2048]{1,0:T(1,128)S(1)}, f32[1,2048]{1,0:T(1,128)}, u32[]{:S(2)}) copy-start(f32[1,2048]{1,0:T(1,128)} %param.20) | copy-start | bytes 24580
  134.6 11.6 %collective-permute-start.14 = (bf16[128,2048]{1,0:T(8,128)(2,1)S(1)}, bf16[128,2048]{1,0:T(8,128)(2,1)S(1)}, u32[]{:S(2)}, u32[]{:S(2)}) collective-permute-start(bf16[128,2048]{1,0:T(8,128)(2,1)S(1)} %add_convert_fusion.2), channel_id=1, source_target_pairs={{0,7},{1,0},{2,1},{3,2},{4,3},{5,4},{6,5},{7,6},{8,15},{9,8},{10,9... | collective-permute-start | bytes 1572872 | tf_op jit(solution)/shard_map/ppermute | solution.py:28
  140.7 11.5 %collective-permute-start.10 = (bf16[128,2048]{1,0:T(8,128)(2,1)S(1)}, bf16[128,2048]{1,0:T(8,128)(2,1)S(1)}, u32[]{:S(2)}, u32[]{:S(2)}) collective-permute-start(bf16[128,2048]{1,0:T(8,128)(2,1)S(1)} %add_convert_fusion.4), channel_id=1, source_target_pairs={{0,1},{1,2},{2,3},{3,4},{4,5},{5,6},{6,7},{7,0},{8,9},{9,10},{10,1... | collective-permute-start | bytes 1572872 | tf_op jit(solution)/shard_map/ppermute | solution.py:28
  146.4 11.8 %collective-permute-start.15 = (bf16[128,2048]{1,0:T(8,128)(2,1)S(1)}, bf16[128,2048]{1,0:T(8,128)(2,1)S(1)}, u32[]{:S(2)}, u32[]{:S(2)}) collective-permute-start(bf16[128,2048]{1,0:T(8,128)(2,1)S(1)} %add_convert_fusion.1), channel_id=1, source_target_pairs={{0,7},{1,0},{2,1},{3,2},{4,3},{5,4},{6,5},{7,6},{8,15},{9,8},{10,9... | collective-permute-start | bytes 1572872 | tf_op jit(solution)/shard_map/ppermute | solution.py:28
  152.3 11.3 %collective-permute-start.11 = (bf16[128,2048]{1,0:T(8,128)(2,1)S(1)}, bf16[128,2048]{1,0:T(8,128)(2,1)S(1)}, u32[]{:S(2)}, u32[]{:S(2)}) collective-permute-start(bf16[128,2048]{1,0:T(8,128)(2,1)S(1)} %add_convert_fusion.3), channel_id=1, source_target_pairs={{0,1},{1,2},{2,3},{3,4},{4,5},{5,6},{6,7},{7,0},{8,9},{9,10},{10,1... | collective-permute-start | bytes 1572872 | tf_op jit(solution)/shard_map/ppermute | solution.py:28
  163.6 18.0 %copy-start.17 = (f32[64,2]{0,1:T(2,128)S(1)}, f32[64,2]{0,1:T(2,128)}, u32[]{:S(2)}) copy-start(f32[64,2]{0,1:T(2,128)} %param.15) | copy-start | bytes 1540
  163.6 18.2 %copy-start.16 = (s32[512,4]{0,1:T(4,128)S(1)}, s32[512,4]{0,1:T(4,128)}, u32[]{:S(2)}) copy-start(s32[512,4]{0,1:T(4,128)} %param.24) | copy-start | bytes 24580
  163.9 36.2 %copy-start.6 = (bf16[64,2048]{1,0:T(8,128)(2,1)S(1)}, bf16[64,2048]{1,0:T(8,128)(2,1)}, u32[]{:S(2)}) copy-start(bf16[64,2048]{1,0:T(8,128)(2,1)} %tokens.3) | copy-start | bytes 786436
  163.9 36.2 %copy-start.11 = (f32[2048]{0:T(1024)S(1)}, f32[2048]{0:T(1024)}, u32[]{:S(2)}) copy-start(f32[2048]{0:T(1024)} %param.21) | copy-start | bytes 24580
  165.1 33.9 %all-to-all-start.1 = ((bf16[64,2,2048]{2,1,0:T(2,128)(2,1)}), bf16[64,2,2048]{2,1,0:T(2,128)(2,1)S(1)}, u32[]{:S(2)}, u32[]{:S(2)}) async-start(bf16[64,2,2048]{2,1,0:T(2,128)(2,1)} %reshape.106), calls=%async_computation.1 | async-start | bytes 1048576 | tf_op jit(solution)/shard_map/all_to_all | solution.py:275
  200.1 4.6 %copy-start.4 = (bf16[2048,3072]{1,0:T(8,128)(2,1)S(1)}, bf16[2048,3072]{1,0:T(8,128)(2,1)}, u32[]{:S(2)}) copy-start(bf16[2048,3072]{1,0:T(8,128)(2,1)} %all-gather.4.cloned.1.call-done.cross) | copy-start | bytes 37748740
  210.9 10.5 %all-to-all-start.2 = ((bf16[8,4,128]{2,1,0:T(4,128)(2,1)}), bf16[8,4,128]{2,1,0:T(4,128)(2,1)S(1)}, u32[]{:S(2)}, u32[]{:S(2)}) async-start(bf16[8,4,128]{2,1,0:T(4,128)(2,1)} %bitcast.17), calls=%async_computation.2 | async-start | bytes 16384 | tf_op jit(solution)/shard_map/all_to_all | solution.py:301
  222.2 17.0 %all-to-all-start.3 = ((bf16[64,1,128]{2,1,0:T(2,128)(2,1)}), bf16[64,1,128]{2,1,0:T(2,128)(2,1)S(1)}, u32[]{:S(2)}, u32[]{:S(2)}) async-start(bf16[64,1,128]{2,1,0:T(2,128)(2,1)} %copy.44), calls=%async_computation.3 | async-start | bytes 65536 | tf_op jit(solution)/shard_map/all_to_all | solution.py:306
Sparse Core Ops, SparseCore 0:
  12.4 43.9 all-gather.5
  69.1 93.8 all-gather.3

commit v4 on v3

--- a/solution.py
+++ b/solution.py
@@ -92,19 +92,26 @@
             pltpu.VMEM((1, width), F32),
             pltpu.SemaphoreType.DMA((4,)),
         ],
-        compiler_params=pltpu.CompilerParams(vmem_limit_bytes=40 * 2**20),
     )(tokens, expert_ids.T, gain.reshape(1, width), weights, asked)
 
 
 def tail_kernel(
-    tokens, returned, picks, gates, gain, cross, asked, marks, encoded, context, weights, sems
+    info, tokens, returned, picks, gates, gain, cross, encoded, context, weights, asked, sems
 ):
     rows = tokens.shape[0]
     count, head_size = context.shape
     heads = weights.shape[0]
     sentences = count // heads
     step = 2 * head_size
+    block = asked.shape[1]
     copies = [
+        pltpu.make_async_copy(
+            cross.at[pl.ds(pl.multiple_of(info[0, k] // block * block, block), block), heads * step :],
+            asked.at[k],
+            sems.at[heads + k],
+        )
+        for k in range(sentences)
+    ] + [
         pltpu.make_async_copy(cross.at[:, h * step : (h + 1) * step], weights.at[h], sems.at[h])
         for h in range(heads)
     ]
@@ -114,20 +121,31 @@
     moe = gates[:, 0:1] * picked[:rows] + gates[:, 1:2] * picked[rows:]
     value = layer_norm(tokens[...].astype(F32) + moe, gain[...]).astype(BF)
     encoded[...] = value
+    sentence_of = iota((count, 1), 0) % sentences
     head_of = iota((count, head_size), 0) // sentences
+    begin = jnp.zeros((count, 1), jnp.int32)
+    end = jnp.zeros((count, 1), jnp.int32)
+    queries = jnp.zeros((count, heads * head_size), F32)
+    for k in range(sentences):
+        begin = jnp.where(sentence_of == k, info[1, k], begin)
+        end = jnp.where(sentence_of == k, info[2, k], end)
+        copies[k].wait()
+        chosen = (iota((count, block), 1) == info[0, k] % block) & (iota((count, block), 0) % sentences == k)
+        queries += dot(chosen.astype(BF), asked[k])
+    queries = queries.astype(BF)
     scores = jnp.zeros((count, rows), F32)
     values = []
     for h in range(heads):
-        copies[h].wait()
+        copies[sentences + h].wait()
         both = dot(value, weights[h]).astype(BF)
-        query = jnp.where(head_of == h, asked[...], 0).astype(BF)
+        query = jnp.where(head_of == h, queries[:, h * head_size : (h + 1) * head_size], 0).astype(BF)
         scores += lax.dot_general(
             query, both[:, :head_size], (((1,), (1,)), ((), ())), preferred_element_type=F32
         )
         values.append(both[:, head_size:])
     scores = scores / math.sqrt(head_size)
     row_ids = iota((count, rows), 1)
-    visible = (row_ids >= marks[:, 0:1]) & (row_ids < marks[:, 1:2])
+    visible = (row_ids >= begin) & (row_ids < end)
     scores = jnp.where(visible, scores, -jnp.inf)
     exponent = jnp.exp(scores - jnp.max(scores, axis=-1, keepdims=True))
     attention = (exponent / jnp.sum(exponent, axis=-1, keepdims=True)).astype(BF)
@@ -137,27 +155,33 @@
     context[...] = result.astype(BF)
 
 
-def tail(tokens, returned, picks, gates, gain, cross, asked, marks, heads):
+def tail(info, tokens, returned, picks, gates, gain, cross, heads, head_size):
     rows, width = tokens.shape
-    step = 2 * asked.shape[1]
-    specs = whole(8)
-    specs[5] = pl.BlockSpec(memory_space=pl.ANY)
+    step = 2 * head_size
+    sentences = info.shape[1]
+    specs = whole(7)
+    specs[0] = pl.BlockSpec(memory_space=pltpu.SMEM)
+    specs[6] = pl.BlockSpec(memory_space=pl.ANY)
     return pl.pallas_call(
         tail_kernel,
-        out_shape=[jax.ShapeDtypeStruct((rows, width), BF), jax.ShapeDtypeStruct(asked.shape, BF)],
+        out_shape=[
+            jax.ShapeDtypeStruct((rows, width), BF),
+            jax.ShapeDtypeStruct((heads * sentences, head_size), BF),
+        ],
         in_specs=specs,
         out_specs=whole(2),
         scratch_shapes=[
             pltpu.VMEM((heads, width, step), BF),
-            pltpu.SemaphoreType.DMA((heads,)),
-        ],
-        compiler_params=pltpu.CompilerParams(vmem_limit_bytes=40 * 2**20),
+            pltpu.VMEM((sentences, 16, heads * head_size), BF),
+            pltpu.SemaphoreType.DMA((heads + sentences,)),
+        ],
+        compiler_params=pltpu.CompilerParams(vmem_limit_bytes=60 * 2**20),
         cost_estimate=pl.CostEstimate(
             flops=2 * rows * width * heads * step,
             bytes_accessed=2 * width * heads * step,
             transcendentals=0,
         ),
-    )(tokens, returned, picks, gates, gain.reshape(1, width), cross, asked, marks)
+    )(info, tokens, returned, picks, gates, gain.reshape(1, width), cross)
 
 
 def expert_kernel(count, *refs):
@@ -278,23 +302,12 @@
     own_lengths = lax.dynamic_slice_in_dim(lengths, block, 1, 0)[0]
     owners = lax.dynamic_slice_in_dim(page_table, block, 1, 0)[0]
     slots_dev = groups * sentences
-    asked = jnp.concatenate(
-        [
-            lax.dynamic_slice(
-                cross,
-                (owners[k] * slots_dev + row * sentences + k, groups * cross_cols),
-                (1, groups * head_size),
-            )
-            for k in range(sentences)
-        ],
-        axis=0,
-    )
-    asked = asked.reshape(sentences, groups, head_size).transpose(1, 0, 2).reshape(-1, head_size)
     ends = jnp.cumsum(own_lengths)
-    marks = jnp.tile(jnp.stack([ends - own_lengths, ends], axis=1), (groups, 1))
+    query_rows = owners * slots_dev + row * sentences + jnp.arange(sentences, dtype=jnp.int32)
+    info = jnp.stack([query_rows, ends - own_lengths, ends])
 
     encoded, own_context = tail(
-        tokens, returned, picks, gates, final_gain, cross, asked, marks, groups
+        info, tokens, returned, picks, gates, final_gain, cross, groups, head_size
     )
     own_context = own_context.reshape(groups, sentences, head_size)
 

time: 248 us -> 240 us (0.968)
  local copies, waits for them, and re-layouts: 19.9 us -> 12.5 us
  Pallas kernels: 14.1 us -> 17 us
  between operations: 17.2 us -> 14.5 us
    unnamed x40 -> x25, local copies, waits for them, and re-layouts: 12.7 us -> 4.93 us
  transfers between devices with their start and end apart: 21 -> 21, of which waited for: 18 -> 17; matrix products, arithmetic and copies ran while one was open for 2% -> 3% of each run, Pallas kernels for 3% -> 3%
where the time goes in v4:
time: 240 us; the launch traced here: 239 us
  starting transfers between devices  81.9 us (34%)
  waiting for transfers between devices  77.7 us (32%)
  blocking collectives  32 us (13%)
  Pallas kernels  17 us (7%)
  between operations  14.5 us (6%)
  local copies, waits for them, and re-layouts  12.5 us (5%)
  other arithmetic  2.54 us (1%)
    ppermute x16, starting transfers between devices, shift(): lax.ppermute(value, 'group', [(i, (i + by) % groups) for i in range(group...  53.2 us
    ppermute x16, waiting for transfers between devices, shift(): lax.ppermute(value, 'group', [(i, (i + by) % groups) for i in range(group...  47.4 us
    all_to_all x1, blocking collectives, on_device(): lax.all_to_all(outgoing, 'expert', 0, 0, tiled=True).reshape(places, width)  32 us
    all_to_all x1, starting transfers between devices, on_device(): lax.all_to_all(expert_out, 'expert', 0, 0, tiled=True)  15.9 us
    all_to_all x1, waiting for transfers between devices, on_device(): lax.all_to_all(expert_out, 'expert', 0, 0, tiled=True)  14.9 us
    all_to_all x1, waiting for transfers between devices, on_device(): lax.all_to_all(sent, 'expert', 0, 0, tiled=True).reshape(experts, head_size)  9.28 us
    all_to_all x1, starting transfers between devices, on_device(): lax.all_to_all(sent, 'expert', 0, 0, tiled=True).reshape(experts, head_size)  7.71 us
    pallas_call x1, Pallas kernels, tail(): pl.pallas_call(tail_kernel, out_shape=[jax.ShapeDtypeStruct((rows, width)...  7.05 us
  transfers between devices with their start and end apart: 21, of which 17 were waited for; matrix products, arithmetic and copies ran while one was open for 3% of the time, Pallas kernels for 3%

profile of v4, /device:TPU:1, one launch (start us, length us, event | category | flops | bytes accessed | tf_op | source)
XLA Modules:
  0.0 239.1 jit_solution(9259360212016704164)
XLA Ops:
  7.2 3.2 %shard_map.140 = (bf16[128,2048]{1,0:T(8,128)(2,1)}, bf16[128,128]{1,0:T(8,128)(2,1)}, bf16[192,384]{1,0:T(8,128)(2,1)}) custom-call(bf16[64,2048]{1,0:T(8,128)(2,1)} %tokens.3, s32[2,64]{1,0:T(2,128)} %bitcast.43, f32[1,2048]{1,0:T(1,128)} %bitcast.41, bf16[32,256]{1,0:T(8,128)(2,1)} %weights.1, bf16[32,128]{1,0:T(8,128)(2,1)} %asked.1), custom_call_target="tpu_custom_call" | custom-call | tf_op jit(solution)/shard_map/pallas_call | solution.py:81
  10.5 1.4 reshape.67
  11.9 32.0 %all_to_all.20 = bf16[64,2,2048]{2,1,0:T(2,128)(2,1)S(1)} all-to-all(bf16[64,2,2048]{2,1,0:T(2,128)(2,1)S(1)} %reshape.67), channel_id=1, replica_groups=mesh['expert'=64,'group'=8] {'expert'}, dimensions={0} | all-to-all | bytes 1048576 | tf_op jit(solution)/shard_map/all_to_all | solution.py:283
  43.8 0.2 reshape.68.refs_0_
  44.0 3.2 %collective-permute-start = (bf16[128,2048]{1,0:T(8,128)(2,1)S(1)}, bf16[128,2048]{1,0:T(8,128)(2,1)S(1)}, u32[]{:S(2)}, u32[]{:S(2)}) collective-permute-start(bf16[128,2048]{1,0:T(8,128)(2,1)S(1)} %reshape.68.refs_0_), channel_id=1, source_target_pairs={{0,1},{1,2},{2,3},{3,4},{4,5},{5,6},{6,7},{7,0},{8,9},{9,10},{10,1... | collective-permute-start | bytes 1572872 | tf_op jit(solution)/shard_map/ppermute | solution.py:28
  47.2 3.8 %collective-permute-start.1 = (bf16[128,2048]{1,0:T(8,128)(2,1)S(1)}, bf16[128,2048]{1,0:T(8,128)(2,1)}, u32[]{:S(2)}, u32[]{:S(2)}) collective-permute-start(bf16[128,2048]{1,0:T(8,128)(2,1)S(1)} %reshape.68.refs_0_), channel_id=1, source_target_pairs={{0,7},{1,0},{2,1},{3,2},{4,3},{5,4},{6,5},{7,6},{8,15},{9,8},{10,9... | collective-permute-start | bytes 1572872 | tf_op jit(solution)/shard_map/ppermute | solution.py:28
  51.1 1.6 copy-done.1
  52.7 0.8 shard_map.141
  53.5 9.8 %collective-permute-done.refs_0_ = bf16[128,2048]{1,0:T(8,128)(2,1)S(1)} collective-permute-done((bf16[128,2048]{1,0:T(8,128)(2,1)S(1)}, bf16[128,2048]{1,0:T(8,128)(2,1)S(1)}, u32[]{:S(2)}, u32[]{:S(2)}) %collective-permute-start) | collective-permute-done | bytes 524320 | tf_op jit(solution)/shard_map/ppermute | solution.py:28
  63.4 0.8 copy-done.4
  64.2 0.5 collective-permute-done.1.refs_1_
  64.7 2.0 copy.39
  66.8 0.7 pad_maximum_fusion.2
  67.5 2.3 collective-permute-start.2
  69.8 4.2 %collective-permute-start.3 = (bf16[128,2048]{1,0:T(8,128)(2,1)}, bf16[128,2048]{1,0:T(8,128)(2,1)S(1)}, u32[]{:S(2)}, u32[]{:S(2)}) collective-permute-start(bf16[128,2048]{1,0:T(8,128)(2,1)} %collective-permute-done.1.refs_1_), channel_id=1, source_target_pairs={{0,7},{1,0},{2,1},{3,2},{4,3},{5,4},{6,5},{7,6},{8,15},{9,8},{10,9... | collective-permute-start | bytes 1572872 | tf_op jit(solution)/shard_map/ppermute | solution.py:28
  74.1 1.6 copy-done.2
  75.7 2.4 shard_map.142
  78.0 5.4 %collective-permute-done.2.refs_0_ = bf16[128,2048]{1,0:T(8,128)(2,1)S(1)} collective-permute-done((bf16[128,2048]{1,0:T(8,128)(2,1)S(1)}, bf16[128,2048]{1,0:T(8,128)(2,1)S(1)}, u32[]{:S(2)}, u32[]{:S(2)}) %collective-permute-start.2) | collective-permute-done | bytes 524320 | tf_op jit(solution)/shard_map/ppermute | solution.py:28
  83.4 2.0 collective-permute-done.3.refs_1_
  85.4 2.8 %collective-permute-start.4 = (bf16[128,2048]{1,0:T(8,128)(2,1)S(1)}, bf16[128,2048]{1,0:T(8,128)(2,1)S(1)}, u32[]{:S(2)}, u32[]{:S(2)}) collective-permute-start(bf16[128,2048]{1,0:T(8,128)(2,1)S(1)} %collective-permute-done.2.refs_0_), channel_id=1, source_target_pairs={{0,1},{1,2},{2,3},{3,4},{4,5},{5,6},{6,7},{7,0},{8,9},{9,10},{10,1... | collective-permute-start | bytes 1572872 | tf_op jit(solution)/shard_map/ppermute | solution.py:28
  88.2 3.7 %collective-permute-start.5 = (bf16[128,2048]{1,0:T(8,128)(2,1)S(1)}, bf16[128,2048]{1,0:T(8,128)(2,1)S(1)}, u32[]{:S(2)}, u32[]{:S(2)}) collective-permute-start(bf16[128,2048]{1,0:T(8,128)(2,1)S(1)} %collective-permute-done.3.refs_1_), channel_id=1, source_target_pairs={{0,7},{1,0},{2,1},{3,2},{4,3},{5,4},{6,5},{7,6},{8,15},{9,8},{10,9... | collective-permute-start | bytes 1572872 | tf_op jit(solution)/shard_map/ppermute | solution.py:28
  91.9 1.4 shard_map.143
  93.3 7.0 %collective-permute-done.4.refs_0_ = bf16[128,2048]{1,0:T(8,128)(2,1)S(1)} collective-permute-done((bf16[128,2048]{1,0:T(8,128)(2,1)S(1)}, bf16[128,2048]{1,0:T(8,128)(2,1)S(1)}, u32[]{:S(2)}, u32[]{:S(2)}) %collective-permute-start.4) | collective-permute-done | bytes 524320 | tf_op jit(solution)/shard_map/ppermute | solution.py:28
  100.3 0.9 collective-permute-done.5.refs_1_
  101.2 4.5 %collective-permute-start.6 = (bf16[64,2048]{1,0:T(8,128)(2,1)S(1)}, bf16[64,2048]{1,0:T(8,128)(2,1)S(1)}, u32[]{:S(2)}, u32[]{:S(2)}) collective-permute-start(bf16[64,2048]{1,0:T(8,128)(2,1)S(1)} %slice.38), channel_id=1, source_target_pairs={{0,1},{1,2},{2,3},{3,4},{4,5},{5,6},{6,7},{7,0},{8,9},{9,10},{10,1... | collective-permute-start | bytes 786440 | tf_op jit(solution)/shard_map/ppermute | solution.py:28
  105.7 3.0 %collective-permute-start.7 = (bf16[64,2048]{1,0:T(8,128)(2,1)S(1)}, bf16[64,2048]{1,0:T(8,128)(2,1)S(1)}, u32[]{:S(2)}, u32[]{:S(2)}) collective-permute-start(bf16[64,2048]{1,0:T(8,128)(2,1)S(1)} %slice.39), channel_id=1, source_target_pairs={{0,7},{1,0},{2,1},{3,2},{4,3},{5,4},{6,5},{7,6},{8,15},{9,8},{10,9... | collective-permute-start | bytes 786440 | tf_op jit(solution)/shard_map/ppermute | solution.py:28
  108.7 1.3 shard_map.144
  110.1 0.3 collective-permute-done.6.refs_0_
  110.4 2.9 %collective-permute-done.7.refs_1_ = bf16[64,2048]{1,0:T(8,128)(2,1)S(1)} collective-permute-done((bf16[64,2048]{1,0:T(8,128)(2,1)S(1)}, bf16[64,2048]{1,0:T(8,128)(2,1)S(1)}, u32[]{:S(2)}, u32[]{:S(2)}) %collective-permute-start.7) | collective-permute-done | bytes 262176 | tf_op jit(solution)/shard_map/ppermute | solution.py:28
  113.3 0.9 shard_map.145
  114.2 3.0 %collective-permute-start.8 = (bf16[64,2048]{1,0:T(8,128)(2,1)S(1)}, bf16[64,2048]{1,0:T(8,128)(2,1)S(1)}, u32[]{:S(2)}, u32[]{:S(2)}) collective-permute-start(bf16[64,2048]{1,0:T(8,128)(2,1)S(1)} %get-tuple-element.50), channel_id=1, source_target_pairs={{0,1},{1,2},{2,3},{3,4},{4,5},{5,6},{6,7},{7,0},{8,9},{9,10},{10,1... | collective-permute-start | bytes 786440 | tf_op jit(solution)/shard_map/ppermute | solution.py:28
  117.2 3.4 %collective-permute-start.12 = (bf16[64,2048]{1,0:T(8,128)(2,1)S(1)}, bf16[64,2048]{1,0:T(8,128)(2,1)S(1)}, u32[]{:S(2)}, u32[]{:S(2)}) collective-permute-start(bf16[64,2048]{1,0:T(8,128)(2,1)S(1)} %get-tuple-element.54), channel_id=1, source_target_pairs={{0,7},{1,0},{2,1},{3,2},{4,3},{5,4},{6,5},{7,6},{8,15},{9,8},{10,9... | collective-permute-start | bytes 786440 | tf_op jit(solution)/shard_map/ppermute | solution.py:28
  120.7 1.8 collective-permute-done.8
  122.6 1.9 collective-permute-start.9
  124.5 0.2 collective-permute-done.12
  124.9 4.4 %collective-permute-start.13 = (bf16[128,2048]{1,0:T(8,128)(2,1)S(1)}, bf16[128,2048]{1,0:T(8,128)(2,1)S(1)}, u32[]{:S(2)}, u32[]{:S(2)}) collective-permute-start(bf16[128,2048]{1,0:T(8,128)(2,1)S(1)} %pad_maximum_fusion.1), channel_id=1, source_target_pairs={{0,7},{1,0},{2,1},{3,2},{4,3},{5,4},{6,5},{7,6},{8,15},{9,8},{10,9... | collective-permute-start | bytes 1572872 | tf_op jit(solution)/shard_map/ppermute | solution.py:28
  129.3 4.9 %collective-permute-done.9 = bf16[128,2048]{1,0:T(8,128)(2,1)S(1)} collective-permute-done((bf16[128,2048]{1,0:T(8,128)(2,1)S(1)}, bf16[128,2048]{1,0:T(8,128)(2,1)S(1)}, u32[]{:S(2)}, u32[]{:S(2)}) %collective-permute-start.9) | collective-permute-done | bytes 524320 | tf_op jit(solution)/shard_map/ppermute | solution.py:28
  134.3 1.9 collective-permute-start.10
  136.3 0.1 add_convert_fusion.2
  136.4 4.6 %collective-permute-start.14 = (bf16[128,2048]{1,0:T(8,128)(2,1)S(1)}, bf16[128,2048]{1,0:T(8,128)(2,1)S(1)}, u32[]{:S(2)}, u32[]{:S(2)}) collective-permute-start(bf16[128,2048]{1,0:T(8,128)(2,1)S(1)} %add_convert_fusion.2), channel_id=1, source_target_pairs={{0,7},{1,0},{2,1},{3,2},{4,3},{5,4},{6,5},{7,6},{8,15},{9,8},{10,9... | collective-permute-start | bytes 1572872 | tf_op jit(solution)/shard_map/ppermute | solution.py:28
  141.0 4.9 %collective-permute-done.10 = bf16[128,2048]{1,0:T(8,128)(2,1)S(1)} collective-permute-done((bf16[128,2048]{1,0:T(8,128)(2,1)S(1)}, bf16[128,2048]{1,0:T(8,128)(2,1)S(1)}, u32[]{:S(2)}, u32[]{:S(2)}) %collective-permute-start.10) | collective-permute-done | bytes 524320 | tf_op jit(solution)/shard_map/ppermute | solution.py:28
  145.9 0.1 add_convert_fusion.3
  146.0 1.9 collective-permute-start.11
  147.9 0.1 add_convert_fusion.1
  148.1 4.6 %collective-permute-start.15 = (bf16[128,2048]{1,0:T(8,128)(2,1)S(1)}, bf16[128,2048]{1,0:T(8,128)(2,1)S(1)}, u32[]{:S(2)}, u32[]{:S(2)}) collective-permute-start(bf16[128,2048]{1,0:T(8,128)(2,1)S(1)} %add_convert_fusion.1), channel_id=1, source_target_pairs={{0,7},{1,0},{2,1},{3,2},{4,3},{5,4},{6,5},{7,6},{8,15},{9,8},{10,9... | collective-permute-start | bytes 1572872 | tf_op jit(solution)/shard_map/ppermute | solution.py:28
  152.7 5.2 %collective-permute-done.11 = bf16[128,2048]{1,0:T(8,128)(2,1)S(1)} collective-permute-done((bf16[128,2048]{1,0:T(8,128)(2,1)S(1)}, bf16[128,2048]{1,0:T(8,128)(2,1)S(1)}, u32[]{:S(2)}, u32[]{:S(2)}) %collective-permute-start.11) | collective-permute-done | bytes 524320 | tf_op jit(solution)/shard_map/ppermute | solution.py:28
  157.8 1.5 collective-permute-done.15
  159.3 0.3 add_convert_fusion
  159.6 1.2 reshape.69
  160.7 15.9 %all-to-all-start.1 = ((bf16[64,2,2048]{2,1,0:T(2,128)(2,1)}), bf16[64,2,2048]{2,1,0:T(2,128)(2,1)S(1)}, u32[]{:S(2)}, u32[]{:S(2)}) async-start(bf16[64,2,2048]{2,1,0:T(2,128)(2,1)} %reshape.69), calls=%async_computation.1 | async-start | bytes 1048576 | tf_op jit(solution)/shard_map/all_to_all | solution.py:299
  176.7 0.8 constant_dynamic-slice_fusion.1
  177.5 0.2 reduce-window_clone.1
  177.8 0.7 copy.41.gates
  178.5 0.6 pad_add_fusion.info
  179.1 14.9 %all-to-all-done.1 = bf16[64,2,2048]{2,1,0:T(2,128)(2,1)S(1)} async-done(((bf16[64,2,2048]{2,1,0:T(2,128)(2,1)}), bf16[64,2,2048]{2,1,0:T(2,128)(2,1)S(1)}, u32[]{:S(2)}, u32[]{:S(2)}) %all-to-all-start.1) | async-done | bytes 524320 | tf_op jit(solution)/shard_map/all_to_all | solution.py:299
  194.0 1.0 reshape.70.returned
  195.0 7.1 %shard_map.146 = (bf16[64,2048]{1,0:T(8,128)(2,1)}, bf16[32,128]{1,0:T(8,128)(2,1)}) custom-call(s32[3,4]{1,0:T(4,128)} %pad_add_fusion.info, bf16[64,2048]{1,0:T(8,128)(2,1)} %tokens.3, bf16[128,2048]{1,0:T(8,128)(2,1)} %reshape.70.returned, bf16[128,128]{1,0:T(8,128)(2,1)} %get-tuple-element.55.picks, f32[64,2]{1,0:T(8,128)} %copy.41.gates, ...), custom_call_target="tpu_custom_call" | custom-call | flops 536870912 | bytes 8388608 | tf_op jit(solution)/shard_map/pallas_call | solution.py:165
  202.0 5.1 %all-to-all-start.2 = ((bf16[8,4,128]{2,1,0:T(4,128)(2,1)}), bf16[8,4,128]{2,1,0:T(4,128)(2,1)S(1)}, u32[]{:S(2)}, u32[]{:S(2)}) async-start(bf16[8,4,128]{2,1,0:T(4,128)(2,1)} %bitcast.42), calls=%async_computation.2 | async-start | bytes 16384 | tf_op jit(solution)/shard_map/all_to_all | solution.py:314
  207.5 6.2 %all-to-all-done.2 = bf16[8,4,128]{2,1,0:T(4,128)(2,1)S(1)} async-done(((bf16[8,4,128]{2,1,0:T(4,128)(2,1)}), bf16[8,4,128]{2,1,0:T(4,128)(2,1)S(1)}, u32[]{:S(2)}, u32[]{:S(2)}) %all-to-all-start.2) | async-done | bytes 8224 | tf_op jit(solution)/shard_map/all_to_all | solution.py:314
  213.7 0.1 fusion
  213.8 0.6 copy.44
  214.4 7.7 %all-to-all-start.3 = ((bf16[64,1,128]{2,1,0:T(2,128)(2,1)}), bf16[64,1,128]{2,1,0:T(2,128)(2,1)S(1)}, u32[]{:S(2)}, u32[]{:S(2)}) async-start(bf16[64,1,128]{2,1,0:T(2,128)(2,1)} %copy.44), calls=%async_computation.3 | async-start | bytes 65536 | tf_op jit(solution)/shard_map/all_to_all | solution.py:319
  222.2 9.3 %all-to-all-done.3 = bf16[64,1,128]{2,1,0:T(2,128)(2,1)S(1)} async-done(((bf16[64,1,128]{2,1,0:T(2,128)(2,1)}), bf16[64,1,128]{2,1,0:T(2,128)(2,1)S(1)}, u32[]{:S(2)}, u32[]{:S(2)}) %all-to-all-start.3) | async-done | bytes 16416 | tf_op jit(solution)/shard_map/all_to_all | solution.py:319
  231.4 0.8 convolution_convert_fusion.1
  (48 shorter events, 1.2 us)
Async XLA Ops:
  7.2 43.9 %copy-start = (bf16[1,2048,512]{2,1,0:T(8,128)(2,1)S(1)}, bf16[1,2048,512]{2,1,0:T(8,128)(2,1)}, u32[]{:S(2)}) copy-start(bf16[1,2048,512]{2,1,0:T(8,128)(2,1)} %param.17) | copy-start | bytes 6291460
  7.2 43.9 %copy-start.6 = (f32[1,512]{1,0:T(1,128)S(1)}, f32[1,512]{1,0:T(1,128)}, u32[]{:S(2)}) copy-start(f32[1,512]{1,0:T(1,128)} %refs_3_.7) | copy-start | bytes 6148
  7.2 57.5 %all-gather.6.cloned.1.call-start = ((), (), s32[]{:S(2)}) async-start(), calls=%async_computation.5 | async-start | bytes 1327104 | tf_op jit(solution)/shard_map/all_gather | solution.py:281
  10.4 184.5 %all-gather.4.cloned.1.call-start = ((), (), s32[]{:S(2)}) async-start(), calls=%async_computation.4 | async-start | bytes 12779520 | tf_op jit(solution)/shard_map/all_gather | solution.py:295
  44.0 19.3 %collective-permute-start = (bf16[128,2048]{1,0:T(8,128)(2,1)S(1)}, bf16[128,2048]{1,0:T(8,128)(2,1)S(1)}, u32[]{:S(2)}, u32[]{:S(2)}) collective-permute-start(bf16[128,2048]{1,0:T(8,128)(2,1)S(1)} %reshape.68.refs_0_), channel_id=1, source_target_pairs={{0,1},{1,2},{2,3},{3,4},{4,5},{5,6},{6,7},{7,0},{8,9},{9,10},{10,1... | collective-permute-start | bytes 1572872 | tf_op jit(solution)/shard_map/ppermute | solution.py:28
  47.2 17.5 %collective-permute-start.1 = (bf16[128,2048]{1,0:T(8,128)(2,1)S(1)}, bf16[128,2048]{1,0:T(8,128)(2,1)}, u32[]{:S(2)}, u32[]{:S(2)}) collective-permute-start(bf16[128,2048]{1,0:T(8,128)(2,1)S(1)} %reshape.68.refs_0_), channel_id=1, source_target_pairs={{0,7},{1,0},{2,1},{3,2},{4,3},{5,4},{6,5},{7,6},{8,15},{9,8},{10,9... | collective-permute-start | bytes 1572872 | tf_op jit(solution)/shard_map/ppermute | solution.py:28
  51.1 1.6 copy-start.1
  63.4 0.8 copy-start.4
  64.7 2.8 %copy-start.5 = (bf16[128,2048]{1,0:T(8,128)(2,1)S(1)}, bf16[128,2048]{1,0:T(8,128)(2,1)}, u32[]{:S(2)}) copy-start(bf16[128,2048]{1,0:T(8,128)(2,1)} %copy-done.4) | copy-start | bytes 1572868
  67.5 15.9 %collective-permute-start.2 = (bf16[128,2048]{1,0:T(8,128)(2,1)S(1)}, bf16[128,2048]{1,0:T(8,128)(2,1)S(1)}, u32[]{:S(2)}, u32[]{:S(2)}) collective-permute-start(bf16[128,2048]{1,0:T(8,128)(2,1)S(1)} %copy-done.5), channel_id=1, source_target_pairs={{0,1},{1,2},{2,3},{3,4},{4,5},{5,6},{6,7},{7,0},{8,9},{9,10},{10,1... | collective-permute-start | bytes 1572872 | tf_op jit(solution)/shard_map/ppermute | solution.py:28
  69.8 15.6 %collective-permute-start.3 = (bf16[128,2048]{1,0:T(8,128)(2,1)}, bf16[128,2048]{1,0:T(8,128)(2,1)S(1)}, u32[]{:S(2)}, u32[]{:S(2)}) collective-permute-start(bf16[128,2048]{1,0:T(8,128)(2,1)} %collective-permute-done.1.refs_1_), channel_id=1, source_target_pairs={{0,7},{1,0},{2,1},{3,2},{4,3},{5,4},{6,5},{7,6},{8,15},{9,8},{10,9... | collective-permute-start | bytes 1572872 | tf_op jit(solution)/shard_map/ppermute | solution.py:28
  74.1 1.6 copy-start.2
  85.4 14.9 %collective-permute-start.4 = (bf16[128,2048]{1,0:T(8,128)(2,1)S(1)}, bf16[128,2048]{1,0:T(8,128)(2,1)S(1)}, u32[]{:S(2)}, u32[]{:S(2)}) collective-permute-start(bf16[128,2048]{1,0:T(8,128)(2,1)S(1)} %collective-permute-done.2.refs_0_), channel_id=1, source_target_pairs={{0,1},{1,2},{2,3},{3,4},{4,5},{5,6},{6,7},{7,0},{8,9},{9,10},{10,1... | collective-permute-start | bytes 1572872 | tf_op jit(solution)/shard_map/ppermute | solution.py:28
  88.2 13.0 %collective-permute-start.5 = (bf16[128,2048]{1,0:T(8,128)(2,1)S(1)}, bf16[128,2048]{1,0:T(8,128)(2,1)S(1)}, u32[]{:S(2)}, u32[]{:S(2)}) collective-permute-start(bf16[128,2048]{1,0:T(8,128)(2,1)S(1)} %collective-permute-done.3.refs_1_), channel_id=1, source_target_pairs={{0,7},{1,0},{2,1},{3,2},{4,3},{5,4},{6,5},{7,6},{8,15},{9,8},{10,9... | collective-permute-start | bytes 1572872 | tf_op jit(solution)/shard_map/ppermute | solution.py:28
  101.2 9.1 %collective-permute-start.6 = (bf16[64,2048]{1,0:T(8,128)(2,1)S(1)}, bf16[64,2048]{1,0:T(8,128)(2,1)S(1)}, u32[]{:S(2)}, u32[]{:S(2)}) collective-permute-start(bf16[64,2048]{1,0:T(8,128)(2,1)S(1)} %slice.38), channel_id=1, source_target_pairs={{0,1},{1,2},{2,3},{3,4},{4,5},{5,6},{6,7},{7,0},{8,9},{9,10},{10,1... | collective-permute-start | bytes 786440 | tf_op jit(solution)/shard_map/ppermute | solution.py:28
  105.7 7.6 %copy-start.3 = (bf16[1,512,2048]{2,1,0:T(8,128)(2,1)S(1)}, bf16[1,512,2048]{2,1,0:T(8,128)(2,1)}, u32[]{:S(2)}) copy-start(bf16[1,512,2048]{2,1,0:T(8,128)(2,1)} %param.19) | copy-start | bytes 6291460
  105.7 7.5 %collective-permute-start.7 = (bf16[64,2048]{1,0:T(8,128)(2,1)S(1)}, bf16[64,2048]{1,0:T(8,128)(2,1)S(1)}, u32[]{:S(2)}, u32[]{:S(2)}) collective-permute-start(bf16[64,2048]{1,0:T(8,128)(2,1)S(1)} %slice.39), channel_id=1, source_target_pairs={{0,7},{1,0},{2,1},{3,2},{4,3},{5,4},{6,5},{7,6},{8,15},{9,8},{10,9... | collective-permute-start | bytes 786440 | tf_op jit(solution)/shard_map/ppermute | solution.py:28
  114.2 8.3 %collective-permute-start.8 = (bf16[64,2048]{1,0:T(8,128)(2,1)S(1)}, bf16[64,2048]{1,0:T(8,128)(2,1)S(1)}, u32[]{:S(2)}, u32[]{:S(2)}) collective-permute-start(bf16[64,2048]{1,0:T(8,128)(2,1)S(1)} %get-tuple-element.50), channel_id=1, source_target_pairs={{0,1},{1,2},{2,3},{3,4},{4,5},{5,6},{6,7},{7,0},{8,9},{9,10},{10,1... | collective-permute-start | bytes 786440 | tf_op jit(solution)/shard_map/ppermute | solution.py:28
  117.2 7.5 %collective-permute-start.12 = (bf16[64,2048]{1,0:T(8,128)(2,1)S(1)}, bf16[64,2048]{1,0:T(8,128)(2,1)S(1)}, u32[]{:S(2)}, u32[]{:S(2)}) collective-permute-start(bf16[64,2048]{1,0:T(8,128)(2,1)S(1)} %get-tuple-element.54), channel_id=1, source_target_pairs={{0,7},{1,0},{2,1},{3,2},{4,3},{5,4},{6,5},{7,6},{8,15},{9,8},{10,9... | collective-permute-start | bytes 786440 | tf_op jit(solution)/shard_map/ppermute | solution.py:28
  122.6 11.6 %collective-permute-start.9 = (bf16[128,2048]{1,0:T(8,128)(2,1)S(1)}, bf16[128,2048]{1,0:T(8,128)(2,1)S(1)}, u32[]{:S(2)}, u32[]{:S(2)}) collective-permute-start(bf16[128,2048]{1,0:T(8,128)(2,1)S(1)} %pad_maximum_fusion), channel_id=1, source_target_pairs={{0,1},{1,2},{2,3},{3,4},{4,5},{5,6},{6,7},{7,0},{8,9},{9,10},{10,1... | collective-permute-start | bytes 1572872 | tf_op jit(solution)/shard_map/ppermute | solution.py:28
  124.9 11.4 %collective-permute-start.13 = (bf16[128,2048]{1,0:T(8,128)(2,1)S(1)}, bf16[128,2048]{1,0:T(8,128)(2,1)S(1)}, u32[]{:S(2)}, u32[]{:S(2)}) collective-permute-start(bf16[128,2048]{1,0:T(8,128)(2,1)S(1)} %pad_maximum_fusion.1), channel_id=1, source_target_pairs={{0,7},{1,0},{2,1},{3,2},{4,3},{5,4},{6,5},{7,6},{8,15},{9,8},{10,9... | collective-permute-start | bytes 1572872 | tf_op jit(solution)/shard_map/ppermute | solution.py:28
  134.3 25.0 %copy-start.7 = (f32[1,2048]{1,0:T(1,128)S(1)}, f32[1,2048]{1,0:T(1,128)}, u32[]{:S(2)}) copy-start(f32[1,2048]{1,0:T(1,128)} %param.20) | copy-start | bytes 24580
  134.3 11.5 %collective-permute-start.10 = (bf16[128,2048]{1,0:T(8,128)(2,1)S(1)}, bf16[128,2048]{1,0:T(8,128)(2,1)S(1)}, u32[]{:S(2)}, u32[]{:S(2)}) collective-permute-start(bf16[128,2048]{1,0:T(8,128)(2,1)S(1)} %add_convert_fusion.4), channel_id=1, source_target_pairs={{0,1},{1,2},{2,3},{3,4},{4,5},{5,6},{6,7},{7,0},{8,9},{9,10},{10,1... | collective-permute-start | bytes 1572872 | tf_op jit(solution)/shard_map/ppermute | solution.py:28
  136.4 11.5 %collective-permute-start.14 = (bf16[128,2048]{1,0:T(8,128)(2,1)S(1)}, bf16[128,2048]{1,0:T(8,128)(2,1)S(1)}, u32[]{:S(2)}, u32[]{:S(2)}) collective-permute-start(bf16[128,2048]{1,0:T(8,128)(2,1)S(1)} %add_convert_fusion.2), channel_id=1, source_target_pairs={{0,7},{1,0},{2,1},{3,2},{4,3},{5,4},{6,5},{7,6},{8,15},{9,8},{10,9... | collective-permute-start | bytes 1572872 | tf_op jit(solution)/shard_map/ppermute | solution.py:28
  146.0 11.8 %collective-permute-start.11 = (bf16[128,2048]{1,0:T(8,128)(2,1)S(1)}, bf16[128,2048]{1,0:T(8,128)(2,1)S(1)}, u32[]{:S(2)}, u32[]{:S(2)}) collective-permute-start(bf16[128,2048]{1,0:T(8,128)(2,1)S(1)} %add_convert_fusion.3), channel_id=1, source_target_pairs={{0,1},{1,2},{2,3},{3,4},{4,5},{5,6},{6,7},{7,0},{8,9},{9,10},{10,1... | collective-permute-start | bytes 1572872 | tf_op jit(solution)/shard_map/ppermute | solution.py:28
  148.1 11.2 %collective-permute-start.15 = (bf16[128,2048]{1,0:T(8,128)(2,1)S(1)}, bf16[128,2048]{1,0:T(8,128)(2,1)S(1)}, u32[]{:S(2)}, u32[]{:S(2)}) collective-permute-start(bf16[128,2048]{1,0:T(8,128)(2,1)S(1)} %add_convert_fusion.1), channel_id=1, source_target_pairs={{0,7},{1,0},{2,1},{3,2},{4,3},{5,4},{6,5},{7,6},{8,15},{9,8},{10,9... | collective-permute-start | bytes 1572872 | tf_op jit(solution)/shard_map/ppermute | solution.py:28
  159.3 17.3 %copy-start.8 = (s32[512,4]{0,1:T(4,128)S(1)}, s32[512,4]{0,1:T(4,128)}, u32[]{:S(2)}) copy-start(s32[512,4]{0,1:T(4,128)} %param.24) | copy-start | bytes 24580
  159.3 18.5 %copy-start.9 = (f32[64,2]{0,1:T(2,128)S(1)}, f32[64,2]{0,1:T(2,128)}, u32[]{:S(2)}) copy-start(f32[64,2]{0,1:T(2,128)} %param.15) | copy-start | bytes 1540
  160.7 33.2 %all-to-all-start.1 = ((bf16[64,2,2048]{2,1,0:T(2,128)(2,1)}), bf16[64,2,2048]{2,1,0:T(2,128)(2,1)S(1)}, u32[]{:S(2)}, u32[]{:S(2)}) async-start(bf16[64,2,2048]{2,1,0:T(2,128)(2,1)} %reshape.69), calls=%async_computation.1 | async-start | bytes 1048576 | tf_op jit(solution)/shard_map/all_to_all | solution.py:299
  202.0 11.7 %all-to-all-start.2 = ((bf16[8,4,128]{2,1,0:T(4,128)(2,1)}), bf16[8,4,128]{2,1,0:T(4,128)(2,1)S(1)}, u32[]{:S(2)}, u32[]{:S(2)}) async-start(bf16[8,4,128]{2,1,0:T(4,128)(2,1)} %bitcast.42), calls=%async_computation.2 | async-start | bytes 16384 | tf_op jit(solution)/shard_map/all_to_all | solution.py:314
  214.4 17.0 %all-to-all-start.3 = ((bf16[64,1,128]{2,1,0:T(2,128)(2,1)}), bf16[64,1,128]{2,1,0:T(2,128)(2,1)S(1)}, u32[]{:S(2)}, u32[]{:S(2)}) async-start(bf16[64,1,128]{2,1,0:T(2,128)(2,1)} %copy.44), calls=%async_computation.3 | async-start | bytes 65536 | tf_op jit(solution)/shard_map/all_to_all | solution.py:319
Sparse Core Ops, SparseCore 0:
  10.7 43.9 all-gather.5
  67.7 93.8 all-gather.3

commit v5 on v4

--- a/solution.py
+++ b/solution.py
@@ -71,17 +71,18 @@
     for copy in copies:
         copy.wait()
     normed = layer_norm(rows_in[...].astype(F32), gain_in[...]).astype(BF)
-    outgoing[...] = dot(goes, normed).astype(BF)
+    outgoing[...] = dot(goes, normed).astype(BF).reshape(outgoing.shape)
 
 
 def dispatch(tokens, expert_ids, gain, weights, asked, places):
     rows, width = tokens.shape
     count = expert_ids.size
+    capacity = count // rows
     anywhere = pl.BlockSpec(memory_space=pl.ANY)
     return pl.pallas_call(
         dispatch_kernel,
         out_shape=[
-            jax.ShapeDtypeStruct((places, width), BF),
+            jax.ShapeDtypeStruct((places // capacity, capacity, width), BF),
             jax.ShapeDtypeStruct((count, places), BF),
             jax.ShapeDtypeStruct((PAD_ROWS, weights.shape[1] + asked.shape[1]), BF),
         ],
@@ -93,6 +94,25 @@
             pltpu.SemaphoreType.DMA((4,)),
         ],
     )(tokens, expert_ids.T, gain.reshape(1, width), weights, asked)
+
+
+def side_by_side_kernel(cols, parts, out):
+    rows = out.shape[0]
+    count, _, total = parts.shape
+    rest = total - cols
+    for n in range(count):
+        out[:, n * cols : (n + 1) * cols] = parts[n, :rows, :cols]
+        out[:, count * cols + n * rest : count * cols + (n + 1) * rest] = parts[n, :rows, cols:]
+
+
+def side_by_side(parts, rows, cols):
+    return pl.pallas_call(
+        lambda *refs: side_by_side_kernel(cols, *refs),
+        out_shape=jax.ShapeDtypeStruct((rows, parts.shape[0] * parts.shape[2]), BF),
+        in_specs=whole(1),
+        out_specs=pl.BlockSpec(memory_space=pltpu.VMEM),
+        compiler_params=pltpu.CompilerParams(vmem_limit_bytes=4 * 2**20),
+    )(parts)
 
 
 def tail_kernel(
@@ -117,7 +137,7 @@
     ]
     for copy in copies:
         copy.start()
-    picked = dot(picks[...], returned[...])
+    picked = dot(picks[...], returned[...].reshape(picks.shape[1], returned.shape[2]))
     moe = gates[:, 0:1] * picked[:rows] + gates[:, 1:2] * picked[rows:]
     value = layer_norm(tokens[...].astype(F32) + moe, gain[...]).astype(BF)
     encoded[...] = value
@@ -279,24 +299,16 @@
     shard_rows = w_cross.shape[0]
     outgoing, picks, own_cross = dispatch(tokens, expert_ids, ln_gain, w_cross, queries, places)
     cross_rows = lax.all_gather(own_cross, "group", axis=0, tiled=False)
-    outgoing = outgoing.reshape(experts, capacity, width)
     arrived = lax.all_to_all(outgoing, "expert", 0, 0, tiled=True).reshape(places, width)
 
     terms = ring_experts(arrived, lambda rows: expert_terms(rows, first, b_in, second), groups)
     cross_rows, _ = lax.optimization_barrier((cross_rows, terms[0]))
-    cross_rows = cross_rows[:, :shard_rows]
-    cross_rows = jnp.concatenate(
-        [
-            cross_rows[:, :, :cross_cols].transpose(1, 0, 2).reshape(shard_rows, -1),
-            cross_rows[:, :, cross_cols:].transpose(1, 0, 2).reshape(shard_rows, -1),
-        ],
-        axis=1,
-    )
+    cross_rows = side_by_side(cross_rows, shard_rows, cross_cols)
     cross = lax.all_gather(cross_rows, "expert", axis=0, tiled=True)
 
     sums = ring_sum(terms, groups)
     expert_out = (sums + b_out[0]).astype(BF).reshape(experts, capacity, width)
-    returned = lax.all_to_all(expert_out, "expert", 0, 0, tiled=True).reshape(places, width)
+    returned = lax.all_to_all(expert_out, "expert", 0, 0, tiled=True)
 
     block = column * groups + row
     own_lengths = lax.dynamic_slice_in_dim(lengths, block, 1, 0)[0]

time: 240 us -> 239 us (level)
    unnamed x25 -> x27, local copies, waits for them, and re-layouts: 4.93 us -> 8.05 us
  transfers between devices with their start and end apart: 21 -> 21, of which waited for: 17 -> 16; matrix products, arithmetic and copies ran while one was open for 3% -> 2% of each run, Pallas kernels for 3% -> 3%
where the time goes in v5:
time: 239 us; the launch traced here: 238 us
  starting transfers between devices  82.1 us (34%)
  waiting for transfers between devices  77.6 us (32%)
  blocking collectives  32.2 us (13%)
  Pallas kernels  17.6 us (7%)
  between operations  14.5 us (6%)
  local copies, waits for them, and re-layouts  11.2 us (5%)
    ppermute x16, starting transfers between devices, shift(): lax.ppermute(value, 'group', [(i, (i + by) % groups) for i in range(group...  52.8 us
    ppermute x16, waiting for transfers between devices, shift(): lax.ppermute(value, 'group', [(i, (i + by) % groups) for i in range(group...  47.3 us
    all_to_all x1, blocking collectives, on_device(): lax.all_to_all(outgoing, 'expert', 0, 0, tiled=True).reshape(places, width)  32.2 us
    all_to_all x1, starting transfers between devices, on_device(): returned = lax.all_to_all(expert_out, 'expert', 0, 0, tiled=True)  16.8 us
    all_to_all x1, waiting for transfers between devices, on_device(): returned = lax.all_to_all(expert_out, 'expert', 0, 0, tiled=True)  14.9 us
    all_to_all x1, waiting for transfers between devices, on_device(): lax.all_to_all(sent, 'expert', 0, 0, tiled=True).reshape(experts, head_size)  9.28 us
    unnamed x27, local copies, waits for them, and re-layouts  8.05 us
    all_to_all x1, starting transfers between devices, on_device(): lax.all_to_all(sent, 'expert', 0, 0, tiled=True).reshape(experts, head_size)  7.71 us
  transfers between devices with their start and end apart: 21, of which 16 were waited for; matrix products, arithmetic and copies ran while one was open for 2% of the time, Pallas kernels for 3%

profile of v5, /device:TPU:1, one launch (start us, length us, event | category | flops | bytes accessed | tf_op | source)
XLA Modules:
  0.0 237.9 jit_solution(5359836242539334588)
XLA Ops:
  7.2 3.2 %shard_map.140 = (bf16[64,2,2048]{2,1,0:T(2,128)(2,1)}, bf16[128,128]{1,0:T(8,128)(2,1)}, bf16[192,384]{1,0:T(8,128)(2,1)}) custom-call(bf16[64,2048]{1,0:T(8,128)(2,1)} %tokens.3, s32[2,64]{1,0:T(2,128)} %bitcast.31, f32[1,2048]{1,0:T(1,128)} %bitcast.29, bf16[32,256]{1,0:T(8,128)(2,1)} %weights.1, bf16[32,128]{1,0:T(8,128)(2,1)} %asked.1), custom_call_target="tpu_custom_call" | custom-call | tf_op jit(solution)/shard_map/pallas_call | solution.py:82
  10.5 32.2 %all_to_all.20 = bf16[64,2,2048]{2,1,0:T(2,128)(2,1)S(1)} all-to-all(bf16[64,2,2048]{2,1,0:T(2,128)(2,1)} %get-tuple-element.31), channel_id=1, replica_groups=mesh['expert'=64,'group'=8] {'expert'}, dimensions={0} | all-to-all | bytes 1048576 | tf_op jit(solution)/shard_map/all_to_all | solution.py:302
  42.6 0.2 reshape.55.refs_0_
  42.8 3.2 %collective-permute-start = (bf16[128,2048]{1,0:T(8,128)(2,1)S(1)}, bf16[128,2048]{1,0:T(8,128)(2,1)S(1)}, u32[]{:S(2)}, u32[]{:S(2)}) collective-permute-start(bf16[128,2048]{1,0:T(8,128)(2,1)S(1)} %reshape.55.refs_0_), channel_id=1, source_target_pairs={{0,1},{1,2},{2,3},{3,4},{4,5},{5,6},{6,7},{7,0},{8,9},{9,10},{10,1... | collective-permute-start | bytes 1572872 | tf_op jit(solution)/shard_map/ppermute | solution.py:28
  46.1 3.8 %collective-permute-start.1 = (bf16[128,2048]{1,0:T(8,128)(2,1)S(1)}, bf16[128,2048]{1,0:T(8,128)(2,1)}, u32[]{:S(2)}, u32[]{:S(2)}) collective-permute-start(bf16[128,2048]{1,0:T(8,128)(2,1)S(1)} %reshape.55.refs_0_), channel_id=1, source_target_pairs={{0,7},{1,0},{2,1},{3,2},{4,3},{5,4},{6,5},{7,6},{8,15},{9,8},{10,9... | collective-permute-start | bytes 1572872 | tf_op jit(solution)/shard_map/ppermute | solution.py:28
  49.9 1.6 copy-done.1
  51.5 0.9 shard_map.141
  52.4 11.2 %collective-permute-done.refs_0_ = bf16[128,2048]{1,0:T(8,128)(2,1)S(1)} collective-permute-done((bf16[128,2048]{1,0:T(8,128)(2,1)S(1)}, bf16[128,2048]{1,0:T(8,128)(2,1)S(1)}, u32[]{:S(2)}, u32[]{:S(2)}) %collective-permute-start) | collective-permute-done | bytes 524320 | tf_op jit(solution)/shard_map/ppermute | solution.py:28
  63.6 0.8 copy-done.5
  64.4 1.3 copy-done.4
  65.7 0.7 shard_map.146
  66.4 2.4 %collective-permute-start.2 = (bf16[128,2048]{1,0:T(8,128)(2,1)}, bf16[128,2048]{1,0:T(8,128)(2,1)S(1)}, u32[]{:S(2)}, u32[]{:S(2)}) collective-permute-start(bf16[128,2048]{1,0:T(8,128)(2,1)} %copy-done.5), channel_id=1, source_target_pairs={{0,1},{1,2},{2,3},{3,4},{4,5},{5,6},{6,7},{7,0},{8,9},{9,10},{10,1... | collective-permute-start | bytes 1572872 | tf_op jit(solution)/shard_map/ppermute | solution.py:28
  68.8 4.1 %collective-permute-start.3 = (bf16[128,2048]{1,0:T(8,128)(2,1)}, bf16[128,2048]{1,0:T(8,128)(2,1)S(1)}, u32[]{:S(2)}, u32[]{:S(2)}) collective-permute-start(bf16[128,2048]{1,0:T(8,128)(2,1)} %collective-permute-done.1.refs_1_), channel_id=1, source_target_pairs={{0,7},{1,0},{2,1},{3,2},{4,3},{5,4},{6,5},{7,6},{8,15},{9,8},{10,9... | collective-permute-start | bytes 1572872 | tf_op jit(solution)/shard_map/ppermute | solution.py:28
  72.9 1.6 copy-done.2
  74.5 1.0 copy-done.6
  75.5 2.4 shard_map.142
  77.9 4.8 %collective-permute-done.2.refs_0_ = bf16[128,2048]{1,0:T(8,128)(2,1)S(1)} collective-permute-done((bf16[128,2048]{1,0:T(8,128)(2,1)}, bf16[128,2048]{1,0:T(8,128)(2,1)S(1)}, u32[]{:S(2)}, u32[]{:S(2)}) %collective-permute-start.2) | collective-permute-done | bytes 524320 | tf_op jit(solution)/shard_map/ppermute | solution.py:28
  82.7 1.6 collective-permute-done.3.refs_1_
  84.4 3.0 %collective-permute-start.4 = (bf16[128,2048]{1,0:T(8,128)(2,1)S(1)}, bf16[128,2048]{1,0:T(8,128)(2,1)S(1)}, u32[]{:S(2)}, u32[]{:S(2)}) collective-permute-start(bf16[128,2048]{1,0:T(8,128)(2,1)S(1)} %collective-permute-done.2.refs_0_), channel_id=1, source_target_pairs={{0,1},{1,2},{2,3},{3,4},{4,5},{5,6},{6,7},{7,0},{8,9},{9,10},{10,1... | collective-permute-start | bytes 1572872 | tf_op jit(solution)/shard_map/ppermute | solution.py:28
  87.4 3.5 %collective-permute-start.5 = (bf16[128,2048]{1,0:T(8,128)(2,1)S(1)}, bf16[128,2048]{1,0:T(8,128)(2,1)S(1)}, u32[]{:S(2)}, u32[]{:S(2)}) collective-permute-start(bf16[128,2048]{1,0:T(8,128)(2,1)S(1)} %collective-permute-done.3.refs_1_), channel_id=1, source_target_pairs={{0,7},{1,0},{2,1},{3,2},{4,3},{5,4},{6,5},{7,6},{8,15},{9,8},{10,9... | collective-permute-start | bytes 1572872 | tf_op jit(solution)/shard_map/ppermute | solution.py:28
  90.9 1.3 shard_map.143
  92.3 7.3 %collective-permute-done.4.refs_0_ = bf16[128,2048]{1,0:T(8,128)(2,1)S(1)} collective-permute-done((bf16[128,2048]{1,0:T(8,128)(2,1)S(1)}, bf16[128,2048]{1,0:T(8,128)(2,1)S(1)}, u32[]{:S(2)}, u32[]{:S(2)}) %collective-permute-start.4) | collective-permute-done | bytes 524320 | tf_op jit(solution)/shard_map/ppermute | solution.py:28
  99.5 1.3 collective-permute-done.5.refs_1_
  100.8 3.4 %collective-permute-start.6 = (bf16[64,2048]{1,0:T(8,128)(2,1)S(1)}, bf16[64,2048]{1,0:T(8,128)(2,1)S(1)}, u32[]{:S(2)}, u32[]{:S(2)}) collective-permute-start(bf16[64,2048]{1,0:T(8,128)(2,1)S(1)} %slice.29), channel_id=1, source_target_pairs={{0,1},{1,2},{2,3},{3,4},{4,5},{5,6},{6,7},{7,0},{8,9},{9,10},{10,1... | collective-permute-start | bytes 786440 | tf_op jit(solution)/shard_map/ppermute | solution.py:28
  104.2 3.6 %collective-permute-start.7 = (bf16[64,2048]{1,0:T(8,128)(2,1)S(1)}, bf16[64,2048]{1,0:T(8,128)(2,1)S(1)}, u32[]{:S(2)}, u32[]{:S(2)}) collective-permute-start(bf16[64,2048]{1,0:T(8,128)(2,1)S(1)} %slice.30), channel_id=1, source_target_pairs={{0,7},{1,0},{2,1},{3,2},{4,3},{5,4},{6,5},{7,6},{8,15},{9,8},{10,9... | collective-permute-start | bytes 786440 | tf_op jit(solution)/shard_map/ppermute | solution.py:28
  107.9 1.3 shard_map.144
  109.2 0.3 collective-permute-done.6.refs_0_
  109.5 2.3 collective-permute-done.7.refs_1_
  111.8 0.8 shard_map.145
  112.6 3.1 %collective-permute-start.8 = (bf16[64,2048]{1,0:T(8,128)(2,1)S(1)}, bf16[64,2048]{1,0:T(8,128)(2,1)S(1)}, u32[]{:S(2)}, u32[]{:S(2)}) collective-permute-start(bf16[64,2048]{1,0:T(8,128)(2,1)S(1)} %get-tuple-element.50), channel_id=1, source_target_pairs={{0,1},{1,2},{2,3},{3,4},{4,5},{5,6},{6,7},{7,0},{8,9},{9,10},{10,1... | collective-permute-start | bytes 786440 | tf_op jit(solution)/shard_map/ppermute | solution.py:28
  115.7 3.4 %collective-permute-start.12 = (bf16[64,2048]{1,0:T(8,128)(2,1)S(1)}, bf16[64,2048]{1,0:T(8,128)(2,1)S(1)}, u32[]{:S(2)}, u32[]{:S(2)}) collective-permute-start(bf16[64,2048]{1,0:T(8,128)(2,1)S(1)} %get-tuple-element.54), channel_id=1, source_target_pairs={{0,7},{1,0},{2,1},{3,2},{4,3},{5,4},{6,5},{7,6},{8,15},{9,8},{10,9... | collective-permute-start | bytes 786440 | tf_op jit(solution)/shard_map/ppermute | solution.py:28
  119.2 1.8 collective-permute-done.8
  121.1 1.9 collective-permute-start.9
  123.0 0.2 collective-permute-done.12
  123.4 4.4 %collective-permute-start.13 = (bf16[128,2048]{1,0:T(8,128)(2,1)S(1)}, bf16[128,2048]{1,0:T(8,128)(2,1)S(1)}, u32[]{:S(2)}, u32[]{:S(2)}) collective-permute-start(bf16[128,2048]{1,0:T(8,128)(2,1)S(1)} %pad_maximum_fusion.1), channel_id=1, source_target_pairs={{0,7},{1,0},{2,1},{3,2},{4,3},{5,4},{6,5},{7,6},{8,15},{9,8},{10,9... | collective-permute-start | bytes 1572872 | tf_op jit(solution)/shard_map/ppermute | solution.py:28
  127.7 4.9 %collective-permute-done.9 = bf16[128,2048]{1,0:T(8,128)(2,1)S(1)} collective-permute-done((bf16[128,2048]{1,0:T(8,128)(2,1)S(1)}, bf16[128,2048]{1,0:T(8,128)(2,1)S(1)}, u32[]{:S(2)}, u32[]{:S(2)}) %collective-permute-start.9) | collective-permute-done | bytes 524320 | tf_op jit(solution)/shard_map/ppermute | solution.py:28
  132.6 0.1 add_convert_fusion.4
  132.8 1.9 collective-permute-start.10
  134.7 0.1 add_convert_fusion.2
  134.9 4.6 %collective-permute-start.14 = (bf16[128,2048]{1,0:T(8,128)(2,1)S(1)}, bf16[128,2048]{1,0:T(8,128)(2,1)S(1)}, u32[]{:S(2)}, u32[]{:S(2)}) collective-permute-start(bf16[128,2048]{1,0:T(8,128)(2,1)S(1)} %add_convert_fusion.2), channel_id=1, source_target_pairs={{0,7},{1,0},{2,1},{3,2},{4,3},{5,4},{6,5},{7,6},{8,15},{9,8},{10,9... | collective-permute-start | bytes 1572872 | tf_op jit(solution)/shard_map/ppermute | solution.py:28
  139.4 4.9 %collective-permute-done.10 = bf16[128,2048]{1,0:T(8,128)(2,1)S(1)} collective-permute-done((bf16[128,2048]{1,0:T(8,128)(2,1)S(1)}, bf16[128,2048]{1,0:T(8,128)(2,1)S(1)}, u32[]{:S(2)}, u32[]{:S(2)}) %collective-permute-start.10) | collective-permute-done | bytes 524320 | tf_op jit(solution)/shard_map/ppermute | solution.py:28
  144.3 0.1 add_convert_fusion.3
  144.5 1.9 collective-permute-start.11
  146.4 0.1 add_convert_fusion.1
  146.5 4.6 %collective-permute-start.15 = (bf16[128,2048]{1,0:T(8,128)(2,1)S(1)}, bf16[128,2048]{1,0:T(8,128)(2,1)S(1)}, u32[]{:S(2)}, u32[]{:S(2)}) collective-permute-start(bf16[128,2048]{1,0:T(8,128)(2,1)S(1)} %add_convert_fusion.1), channel_id=1, source_target_pairs={{0,7},{1,0},{2,1},{3,2},{4,3},{5,4},{6,5},{7,6},{8,15},{9,8},{10,9... | collective-permute-start | bytes 1572872 | tf_op jit(solution)/shard_map/ppermute | solution.py:28
  151.1 5.2 %collective-permute-done.11 = bf16[128,2048]{1,0:T(8,128)(2,1)S(1)} collective-permute-done((bf16[128,2048]{1,0:T(8,128)(2,1)S(1)}, bf16[128,2048]{1,0:T(8,128)(2,1)S(1)}, u32[]{:S(2)}, u32[]{:S(2)}) %collective-permute-start.11) | collective-permute-done | bytes 524320 | tf_op jit(solution)/shard_map/ppermute | solution.py:28
  156.3 1.5 collective-permute-done.15
  157.8 0.3 add_convert_fusion
  158.0 1.2 reshape.56
  159.2 16.8 %all-to-all-start.1 = ((bf16[64,2,2048]{2,1,0:T(2,128)(2,1)}), bf16[64,2,2048]{2,1,0:T(2,128)(2,1)S(1)}, u32[]{:S(2)}, u32[]{:S(2)}) async-start(bf16[64,2,2048]{2,1,0:T(2,128)(2,1)} %reshape.56), calls=%async_computation.1 | async-start | bytes 1048576 | tf_op jit(solution)/shard_map/all_to_all | solution.py:311
  176.0 0.8 constant_dynamic-slice_fusion.1
  176.9 0.2 reduce-window_clone.1
  177.2 0.7 copy.33.gates
  177.9 0.6 pad_add_fusion.info
  178.5 14.9 %all-to-all-done.1.returned = bf16[64,2,2048]{2,1,0:T(2,128)(2,1)S(1)} async-done(((bf16[64,2,2048]{2,1,0:T(2,128)(2,1)}), bf16[64,2,2048]{2,1,0:T(2,128)(2,1)S(1)}, u32[]{:S(2)}, u32[]{:S(2)}) %all-to-all-start.1) | async-done | bytes 524320 | tf_op jit(solution)/shard_map/all_to_all | solution.py:311
  193.3 0.8 copy-done.8
  194.1 7.1 %shard_map.147 = (bf16[64,2048]{1,0:T(8,128)(2,1)}, bf16[32,128]{1,0:T(8,128)(2,1)}) custom-call(s32[3,4]{1,0:T(4,128)} %pad_add_fusion.info, bf16[64,2048]{1,0:T(8,128)(2,1)} %tokens.3, bf16[64,2,2048]{2,1,0:T(2,128)(2,1)} %copy-done.8, bf16[128,128]{1,0:T(8,128)(2,1)} %get-tuple-element.55.picks, f32[64,2]{1,0:T(8,128)} %copy.33.gates, ...), custom_call_target="tpu_custom_call" | custom-call | flops 536870912 | bytes 8388608 | tf_op jit(solution)/shard_map/pallas_call | solution.py:185
  201.2 4.7 %all-to-all-start.2 = ((bf16[8,4,128]{2,1,0:T(4,128)(2,1)}), bf16[8,4,128]{2,1,0:T(4,128)(2,1)S(1)}, u32[]{:S(2)}, u32[]{:S(2)}) async-start(bf16[8,4,128]{2,1,0:T(4,128)(2,1)} %bitcast.30), calls=%async_computation.2 | async-start | bytes 16384 | tf_op jit(solution)/shard_map/all_to_all | solution.py:326
  206.3 6.2 %all-to-all-done.2 = bf16[8,4,128]{2,1,0:T(4,128)(2,1)S(1)} async-done(((bf16[8,4,128]{2,1,0:T(4,128)(2,1)}), bf16[8,4,128]{2,1,0:T(4,128)(2,1)S(1)}, u32[]{:S(2)}, u32[]{:S(2)}) %all-to-all-start.2) | async-done | bytes 8224 | tf_op jit(solution)/shard_map/all_to_all | solution.py:326
  212.5 0.1 fusion
  212.6 0.6 copy.36
  213.2 7.7 %all-to-all-start.3 = ((bf16[64,1,128]{2,1,0:T(2,128)(2,1)}), bf16[64,1,128]{2,1,0:T(2,128)(2,1)S(1)}, u32[]{:S(2)}, u32[]{:S(2)}) async-start(bf16[64,1,128]{2,1,0:T(2,128)(2,1)} %copy.36), calls=%async_computation.3 | async-start | bytes 65536 | tf_op jit(solution)/shard_map/all_to_all | solution.py:331
  221.0 9.3 %all-to-all-done.3 = bf16[64,1,128]{2,1,0:T(2,128)(2,1)S(1)} async-done(((bf16[64,1,128]{2,1,0:T(2,128)(2,1)}), bf16[64,1,128]{2,1,0:T(2,128)(2,1)S(1)}, u32[]{:S(2)}, u32[]{:S(2)}) %all-to-all-start.3) | async-done | bytes 16416 | tf_op jit(solution)/shard_map/all_to_all | solution.py:331
  230.3 0.8 convolution_convert_fusion.1
  (45 shorter events, 1.1 us)
Async XLA Ops:
  7.2 42.7 %copy-start = (bf16[1,2048,512]{2,1,0:T(8,128)(2,1)S(1)}, bf16[1,2048,512]{2,1,0:T(8,128)(2,1)}, u32[]{:S(2)}) copy-start(bf16[1,2048,512]{2,1,0:T(8,128)(2,1)} %param.17) | copy-start | bytes 6291460
  7.2 42.7 %copy-start.7 = (f32[1,512]{1,0:T(1,128)S(1)}, f32[1,512]{1,0:T(1,128)}, u32[]{:S(2)}) copy-start(f32[1,512]{1,0:T(1,128)} %refs_3_.7) | copy-start | bytes 6148
  7.2 57.2 %all-gather.6.cloned.1.call-start = ((), (), s32[]{:S(2)}) async-start(), calls=%async_computation.5 | async-start | bytes 1327104 | tf_op jit(solution)/shard_map/all_gather | solution.py:301
  10.4 182.9 %all-gather.4.cloned.1.call-start = ((), (), s32[]{:S(2)}) async-start(), calls=%async_computation.4 | async-start | bytes 12779520 | tf_op jit(solution)/shard_map/all_gather | solution.py:307
  42.8 20.7 %collective-permute-start = (bf16[128,2048]{1,0:T(8,128)(2,1)S(1)}, bf16[128,2048]{1,0:T(8,128)(2,1)S(1)}, u32[]{:S(2)}, u32[]{:S(2)}) collective-permute-start(bf16[128,2048]{1,0:T(8,128)(2,1)S(1)} %reshape.55.refs_0_), channel_id=1, source_target_pairs={{0,1},{1,2},{2,3},{3,4},{4,5},{5,6},{6,7},{7,0},{8,9},{9,10},{10,1... | collective-permute-start | bytes 1572872 | tf_op jit(solution)/shard_map/ppermute | solution.py:28
  46.1 18.3 %collective-permute-start.1 = (bf16[128,2048]{1,0:T(8,128)(2,1)S(1)}, bf16[128,2048]{1,0:T(8,128)(2,1)}, u32[]{:S(2)}, u32[]{:S(2)}) collective-permute-start(bf16[128,2048]{1,0:T(8,128)(2,1)S(1)} %reshape.55.refs_0_), channel_id=1, source_target_pairs={{0,7},{1,0},{2,1},{3,2},{4,3},{5,4},{6,5},{7,6},{8,15},{9,8},{10,9... | collective-permute-start | bytes 1572872 | tf_op jit(solution)/shard_map/ppermute | solution.py:28
  49.9 1.6 copy-start.1
  63.6 0.8 copy-start.5
  64.4 1.3 copy-start.4
  66.4 16.4 %collective-permute-start.2 = (bf16[128,2048]{1,0:T(8,128)(2,1)}, bf16[128,2048]{1,0:T(8,128)(2,1)S(1)}, u32[]{:S(2)}, u32[]{:S(2)}) collective-permute-start(bf16[128,2048]{1,0:T(8,128)(2,1)} %copy-done.5), channel_id=1, source_target_pairs={{0,1},{1,2},{2,3},{3,4},{4,5},{5,6},{6,7},{7,0},{8,9},{9,10},{10,1... | collective-permute-start | bytes 1572872 | tf_op jit(solution)/shard_map/ppermute | solution.py:28
  68.8 15.6 %collective-permute-start.3 = (bf16[128,2048]{1,0:T(8,128)(2,1)}, bf16[128,2048]{1,0:T(8,128)(2,1)S(1)}, u32[]{:S(2)}, u32[]{:S(2)}) collective-permute-start(bf16[128,2048]{1,0:T(8,128)(2,1)} %collective-permute-done.1.refs_1_), channel_id=1, source_target_pairs={{0,7},{1,0},{2,1},{3,2},{4,3},{5,4},{6,5},{7,6},{8,15},{9,8},{10,9... | collective-permute-start | bytes 1572872 | tf_op jit(solution)/shard_map/ppermute | solution.py:28
  72.9 1.6 copy-start.2
  74.5 1.0 copy-start.6
  84.4 15.1 %collective-permute-start.4 = (bf16[128,2048]{1,0:T(8,128)(2,1)S(1)}, bf16[128,2048]{1,0:T(8,128)(2,1)S(1)}, u32[]{:S(2)}, u32[]{:S(2)}) collective-permute-start(bf16[128,2048]{1,0:T(8,128)(2,1)S(1)} %collective-permute-done.2.refs_0_), channel_id=1, source_target_pairs={{0,1},{1,2},{2,3},{3,4},{4,5},{5,6},{6,7},{7,0},{8,9},{9,10},{10,1... | collective-permute-start | bytes 1572872 | tf_op jit(solution)/shard_map/ppermute | solution.py:28
  87.4 13.4 %collective-permute-start.5 = (bf16[128,2048]{1,0:T(8,128)(2,1)S(1)}, bf16[128,2048]{1,0:T(8,128)(2,1)S(1)}, u32[]{:S(2)}, u32[]{:S(2)}) collective-permute-start(bf16[128,2048]{1,0:T(8,128)(2,1)S(1)} %collective-permute-done.3.refs_1_), channel_id=1, source_target_pairs={{0,7},{1,0},{2,1},{3,2},{4,3},{5,4},{6,5},{7,6},{8,15},{9,8},{10,9... | collective-permute-start | bytes 1572872 | tf_op jit(solution)/shard_map/ppermute | solution.py:28
  100.8 8.7 %collective-permute-start.6 = (bf16[64,2048]{1,0:T(8,128)(2,1)S(1)}, bf16[64,2048]{1,0:T(8,128)(2,1)S(1)}, u32[]{:S(2)}, u32[]{:S(2)}) collective-permute-start(bf16[64,2048]{1,0:T(8,128)(2,1)S(1)} %slice.29), channel_id=1, source_target_pairs={{0,1},{1,2},{2,3},{3,4},{4,5},{5,6},{6,7},{7,0},{8,9},{9,10},{10,1... | collective-permute-start | bytes 786440 | tf_op jit(solution)/shard_map/ppermute | solution.py:28
  104.2 7.6 %copy-start.3 = (bf16[1,512,2048]{2,1,0:T(8,128)(2,1)S(1)}, bf16[1,512,2048]{2,1,0:T(8,128)(2,1)}, u32[]{:S(2)}) copy-start(bf16[1,512,2048]{2,1,0:T(8,128)(2,1)} %param.19) | copy-start | bytes 6291460
  104.2 7.5 %collective-permute-start.7 = (bf16[64,2048]{1,0:T(8,128)(2,1)S(1)}, bf16[64,2048]{1,0:T(8,128)(2,1)S(1)}, u32[]{:S(2)}, u32[]{:S(2)}) collective-permute-start(bf16[64,2048]{1,0:T(8,128)(2,1)S(1)} %slice.30), channel_id=1, source_target_pairs={{0,7},{1,0},{2,1},{3,2},{4,3},{5,4},{6,5},{7,6},{8,15},{9,8},{10,9... | collective-permute-start | bytes 786440 | tf_op jit(solution)/shard_map/ppermute | solution.py:28
  112.6 8.3 %collective-permute-start.8 = (bf16[64,2048]{1,0:T(8,128)(2,1)S(1)}, bf16[64,2048]{1,0:T(8,128)(2,1)S(1)}, u32[]{:S(2)}, u32[]{:S(2)}) collective-permute-start(bf16[64,2048]{1,0:T(8,128)(2,1)S(1)} %get-tuple-element.50), channel_id=1, source_target_pairs={{0,1},{1,2},{2,3},{3,4},{4,5},{5,6},{6,7},{7,0},{8,9},{9,10},{10,1... | collective-permute-start | bytes 786440 | tf_op jit(solution)/shard_map/ppermute | solution.py:28
  115.7 7.5 %collective-permute-start.12 = (bf16[64,2048]{1,0:T(8,128)(2,1)S(1)}, bf16[64,2048]{1,0:T(8,128)(2,1)S(1)}, u32[]{:S(2)}, u32[]{:S(2)}) collective-permute-start(bf16[64,2048]{1,0:T(8,128)(2,1)S(1)} %get-tuple-element.54), channel_id=1, source_target_pairs={{0,7},{1,0},{2,1},{3,2},{4,3},{5,4},{6,5},{7,6},{8,15},{9,8},{10,9... | collective-permute-start | bytes 786440 | tf_op jit(solution)/shard_map/ppermute | solution.py:28
  121.1 11.6 %collective-permute-start.9 = (bf16[128,2048]{1,0:T(8,128)(2,1)S(1)}, bf16[128,2048]{1,0:T(8,128)(2,1)S(1)}, u32[]{:S(2)}, u32[]{:S(2)}) collective-permute-start(bf16[128,2048]{1,0:T(8,128)(2,1)S(1)} %pad_maximum_fusion), channel_id=1, source_target_pairs={{0,1},{1,2},{2,3},{3,4},{4,5},{5,6},{6,7},{7,0},{8,9},{9,10},{10,1... | collective-permute-start | bytes 1572872 | tf_op jit(solution)/shard_map/ppermute | solution.py:28
  123.4 11.4 %collective-permute-start.13 = (bf16[128,2048]{1,0:T(8,128)(2,1)S(1)}, bf16[128,2048]{1,0:T(8,128)(2,1)S(1)}, u32[]{:S(2)}, u32[]{:S(2)}) collective-permute-start(bf16[128,2048]{1,0:T(8,128)(2,1)S(1)} %pad_maximum_fusion.1), channel_id=1, source_target_pairs={{0,7},{1,0},{2,1},{3,2},{4,3},{5,4},{6,5},{7,6},{8,15},{9,8},{10,9... | collective-permute-start | bytes 1572872 | tf_op jit(solution)/shard_map/ppermute | solution.py:28
  132.8 25.0 %copy-start.9 = (f32[1,2048]{1,0:T(1,128)S(1)}, f32[1,2048]{1,0:T(1,128)}, u32[]{:S(2)}) copy-start(f32[1,2048]{1,0:T(1,128)} %param.20) | copy-start | bytes 24580
  132.8 11.5 %collective-permute-start.10 = (bf16[128,2048]{1,0:T(8,128)(2,1)S(1)}, bf16[128,2048]{1,0:T(8,128)(2,1)S(1)}, u32[]{:S(2)}, u32[]{:S(2)}) collective-permute-start(bf16[128,2048]{1,0:T(8,128)(2,1)S(1)} %add_convert_fusion.4), channel_id=1, source_target_pairs={{0,1},{1,2},{2,3},{3,4},{4,5},{5,6},{6,7},{7,0},{8,9},{9,10},{10,1... | collective-permute-start | bytes 1572872 | tf_op jit(solution)/shard_map/ppermute | solution.py:28
  134.9 11.5 %collective-permute-start.14 = (bf16[128,2048]{1,0:T(8,128)(2,1)S(1)}, bf16[128,2048]{1,0:T(8,128)(2,1)S(1)}, u32[]{:S(2)}, u32[]{:S(2)}) collective-permute-start(bf16[128,2048]{1,0:T(8,128)(2,1)S(1)} %add_convert_fusion.2), channel_id=1, source_target_pairs={{0,7},{1,0},{2,1},{3,2},{4,3},{5,4},{6,5},{7,6},{8,15},{9,8},{10,9... | collective-permute-start | bytes 1572872 | tf_op jit(solution)/shard_map/ppermute | solution.py:28
  144.5 11.8 %collective-permute-start.11 = (bf16[128,2048]{1,0:T(8,128)(2,1)S(1)}, bf16[128,2048]{1,0:T(8,128)(2,1)S(1)}, u32[]{:S(2)}, u32[]{:S(2)}) collective-permute-start(bf16[128,2048]{1,0:T(8,128)(2,1)S(1)} %add_convert_fusion.3), channel_id=1, source_target_pairs={{0,1},{1,2},{2,3},{3,4},{4,5},{5,6},{6,7},{7,0},{8,9},{9,10},{10,1... | collective-permute-start | bytes 1572872 | tf_op jit(solution)/shard_map/ppermute | solution.py:28
  146.5 11.2 %collective-permute-start.15 = (bf16[128,2048]{1,0:T(8,128)(2,1)S(1)}, bf16[128,2048]{1,0:T(8,128)(2,1)S(1)}, u32[]{:S(2)}, u32[]{:S(2)}) collective-permute-start(bf16[128,2048]{1,0:T(8,128)(2,1)S(1)} %add_convert_fusion.1), channel_id=1, source_target_pairs={{0,7},{1,0},{2,1},{3,2},{4,3},{5,4},{6,5},{7,6},{8,15},{9,8},{10,9... | collective-permute-start | bytes 1572872 | tf_op jit(solution)/shard_map/ppermute | solution.py:28
  157.8 18.3 %copy-start.10 = (s32[512,4]{0,1:T(4,128)S(1)}, s32[512,4]{0,1:T(4,128)}, u32[]{:S(2)}) copy-start(s32[512,4]{0,1:T(4,128)} %param.24) | copy-start | bytes 24580
  157.8 19.4 %copy-start.11 = (f32[64,2]{0,1:T(2,128)S(1)}, f32[64,2]{0,1:T(2,128)}, u32[]{:S(2)}) copy-start(f32[64,2]{0,1:T(2,128)} %param.15) | copy-start | bytes 1540
  159.2 34.1 %all-to-all-start.1 = ((bf16[64,2,2048]{2,1,0:T(2,128)(2,1)}), bf16[64,2,2048]{2,1,0:T(2,128)(2,1)S(1)}, u32[]{:S(2)}, u32[]{:S(2)}) async-start(bf16[64,2,2048]{2,1,0:T(2,128)(2,1)} %reshape.56), calls=%async_computation.1 | async-start | bytes 1048576 | tf_op jit(solution)/shard_map/all_to_all | solution.py:311
  193.3 0.8 copy-start.8
  201.2 11.3 %all-to-all-start.2 = ((bf16[8,4,128]{2,1,0:T(4,128)(2,1)}), bf16[8,4,128]{2,1,0:T(4,128)(2,1)S(1)}, u32[]{:S(2)}, u32[]{:S(2)}) async-start(bf16[8,4,128]{2,1,0:T(4,128)(2,1)} %bitcast.30), calls=%async_computation.2 | async-start | bytes 16384 | tf_op jit(solution)/shard_map/all_to_all | solution.py:326
  213.2 17.0 %all-to-all-start.3 = ((bf16[64,1,128]{2,1,0:T(2,128)(2,1)}), bf16[64,1,128]{2,1,0:T(2,128)(2,1)S(1)}, u32[]{:S(2)}, u32[]{:S(2)}) async-start(bf16[64,1,128]{2,1,0:T(2,128)(2,1)} %copy.36), calls=%async_computation.3 | async-start | bytes 65536 | tf_op jit(solution)/shard_map/all_to_all | solution.py:331
Sparse Core Ops, SparseCore 0:
  10.7 44.0 all-gather.5
  66.5 93.6 all-gather.3
